TPU v7x, 128 devices: a whole 4x4x4 slice. The times are simulated.
128 devices in a mesh: expert: 16 (over x, z), tensor: 8 (over y, core).
Axes of the slice: x: 4, y: 4, z: 4, core: 2. Of those that a mesh axis runs over, the one named last changes fastest.
Arguments:
- layer_input: bfloat16 [8192, 2048], P('expert'), may hold values from -6 to 6
- attn_gain: float32 [2048], replicated, may hold values from 0.5 to 1.5
- w_query: bfloat16 [2048, 3072], P(None, 'tensor'), may hold values from -0.125 to 0.125
- w_kv_down: bfloat16 [2048, 576], replicated, may hold values from -0.125 to 0.125
- kv_gain: float32 [512], replicated, may hold values from 0.5 to 1.5
- w_kv_up: bfloat16 [512, 4096], P(None, 'tensor'), may hold values from -0.25 to 0.25
- w_out: bfloat16 [2048, 2048], P('tensor'), may hold values from -0.5 to 0.5
- ffn_gain: float32 [2048], replicated, may hold values from 0.5 to 1.5
- w_router: bfloat16 [2048, 32], replicated, may hold values from -0.0625 to 0.0625
- routes: int32 [8192, 6], P('expert'), may hold values from 0 to 31, all different within a row; in each aligned block of 512 rows (0 to 511, 512 to 1023, ...) at most 128 rows name the same one
- expert_gate: bfloat16 [32, 2048, 1408], P('expert', None, 'tensor'), may hold values from -0.125 to 0.125
- expert_up_projection: bfloat16 [32, 2048, 1408], P('expert', None, 'tensor'), may hold values from -0.125 to 0.125
- expert_down: bfloat16 [32, 1408, 2048], P('expert', 'tensor'), may hold values from -0.15625 to 0.15625
- shared_gate: bfloat16 [2048, 2816], P(None, 'tensor'), may hold values from -0.125 to 0.125
- shared_up: bfloat16 [2048, 2816], P(None, 'tensor'), may hold values from -0.125 to 0.125
- shared_down: bfloat16 [2816, 2048], P('tensor'), may hold values from -0.109375 to 0.109375
- cotangent: bfloat16 [8192, 2048], P(('expert', 'tensor')), may hold values from -6 to 6
Outputs:
- output: bfloat16 [8192, 2048], P(('expert', 'tensor'))
- grad_input: float32 [8192, 2048], P(('expert', 'tensor'))
- grad_attn_gain: float32 [2048], replicated
- grad_w_query: float32 [2048, 3072], P(None, 'tensor')
- grad_w_kv_down: float32 [2048, 576], replicated
- grad_kv_gain: float32 [512], replicated
- grad_w_kv_up: float32 [512, 4096], P(None, 'tensor')
- grad_w_out: float32 [2048, 2048], P('tensor')
- grad_ffn_gain: float32 [2048], replicated
- grad_w_router: float32 [2048, 32], replicated
- grad_expert_gate: float32 [32, 2048, 1408], P('expert', None, 'tensor')
- grad_expert_up: float32 [32, 2048, 1408], P('expert', None, 'tensor')
- grad_expert_down: float32 [32, 1408, 2048], P('expert', 'tensor')
- grad_shared_gate: float32 [2048, 2816], P(None, 'tensor')
- grad_shared_up: float32 [2048, 2816], P(None, 'tensor')
- grad_shared_down: float32 [2816, 2048], P('tensor')
Inputs may be any that keep to these rules, and one draw needn't show every extreme that they name: `routes`: each row names 6 different experts. Among the 512 rows of one sequence no expert is named by more than 128 rows, a bound that some block reaches; every expert is named somewhere.
All inputs are finite; a program needn't handle non-finite values.
Results may differ from a plain program's by a relative error of at most 0.025.
Values may be sent and summed in bfloat16 or wider, within the bound.
No kernel may reach another device: no remote copies, remote signals or barrier semaphores. Data moves between devices by JAX's collectives and lax.ppermute only.
A program may use at most 384 MiB of HBM per device.

v0:
```python
import jax
import jax.numpy as jnp
from jax import lax
from jax.sharding import PartitionSpec as P

D = 2048
NOPE = 128
ROPE = 64
VDIM = 128
KV_RANK = 512
TOP = 6


epsilon = 1e-06
route_scale = 2.446
theta_base = 50000.0


def in_blocks(x, dim, size):
    shape = x.shape
    tiles = x.reshape(*shape[:dim], size, shape[dim] // size, *shape[dim + 1 :])
    return jnp.moveaxis(tiles, dim, 0)


def sent_and_summed(x, axis, dim):
    size = lax.axis_size(axis)
    tiles = lax.all_to_all(in_blocks(x, dim, size), axis, 0, 0, tiled=True)
    return jnp.sum(tiles.astype(jnp.float32), axis=0)


def sent_together(arrays, axis, dim, along):
    widths = [a.shape[along] for a in arrays]
    both = jnp.concatenate(arrays, axis=along)
    filled = lax.all_gather(both, axis, axis=dim, tiled=True)
    return tuple(jnp.split(filled, [sum(widths[:k]) for k in range(1, len(widths))], axis=along))


def from_everyone(x, axis):
    size = lax.axis_size(axis)
    return lax.all_to_all(jnp.broadcast_to(x[None], (size, *x.shape)), axis, 0, 0, tiled=True)


def in_order(tiles, dim):
    shape = list(tiles.shape[1:])
    shape[dim] *= tiles.shape[0]
    return jnp.moveaxis(tiles, 0, dim).reshape(shape)


def collect(x, axis, dim):
    tiles = from_everyone(x, axis)
    return in_order(tiles, dim)


def sent_together_2(arrays, axis, dim, along):
    both = jnp.concatenate(arrays, axis=along)
    filled, at, finished = (lax.psum_scatter(both, axis, scatter_dimension=dim, tiled=True), 0, [])
    for a in arrays:
        finished.append(lax.slice_in_dim(filled, at, at + a.shape[along], axis=along))
        at += a.shape[along]
    return tuple(finished)


def in_one(arrays, axis):
    ends = [0]
    for a in arrays:
        ends.append(ends[-1] + a.size)
    total = lax.psum(jnp.concatenate([a.ravel() for a in arrays]), axis)
    return tuple((total[b:e].reshape(a.shape) for a, b, e in zip(arrays, ends, ends[1:])))


def tables(length):
    half_width = ROPE // 2
    steps_float = jnp.arange(half_width, dtype=jnp.float32) * (2.0 / ROPE)
    frequency = jnp.exp(-jnp.log(theta_base) * steps_float)
    angles = jnp.arange(length, dtype=jnp.float32)[:, None] * frequency[None, :]
    return (jnp.cos(angles), jnp.sin(angles))


def rotate(values, cos_table, sin_table):
    half_width = ROPE // 2
    first_half = values[..., :half_width]
    second_half = values[..., half_width:]
    return jnp.concatenate(
        [
            first_half * cos_table - second_half * sin_table,
            second_half * cos_table + first_half * sin_table,
        ],
        axis=-1,
    )


def rotate_back(upstream, cos_table, sin_table):
    half_width = ROPE // 2
    first_half = upstream[..., :half_width]
    second_half = upstream[..., half_width:]
    return jnp.concatenate(
        [
            first_half * cos_table + second_half * sin_table,
            second_half * cos_table - first_half * sin_table,
        ],
        axis=-1,
    )


def matmul(left, right):
    return jnp.dot(left, right, preferred_element_type=jnp.float32)


def matmul_tn(left, right):
    return lax.dot_general(
        left, right, (((0,), (0,)), ((), ())), preferred_element_type=jnp.float32
    )


def matmul_nt(left, right):
    return lax.dot_general(
        left, right, (((1,), (1,)), ((), ())), preferred_element_type=jnp.float32
    )


def norm_forward(values, scales):
    factor = lax.rsqrt(jnp.mean(values * values, axis=-1, keepdims=True) + epsilon)
    return (values * factor * scales, factor)


def norm_backward(values, factor, scales, upstream):
    scaled = upstream * scales
    cubed = factor * factor * factor
    d_values = factor * scaled - values * cubed * jnp.mean(scaled * values, axis=-1, keepdims=True)
    return (d_values, jnp.sum(upstream * values * factor, axis=0))


def block_scores(query_block, key_nope, key_rope, start, length, score_scale):
    scores = jnp.einsum(
        "qhd,khd->hqk", query_block[..., :NOPE], key_nope, preferred_element_type=jnp.float32
    )
    scores = scores + jnp.einsum(
        "qhd,kd->hqk", query_block[..., NOPE:], key_rope, preferred_element_type=jnp.float32
    )
    scores = scores * score_scale
    rows_here = query_block.shape[0]
    causal = (start + jnp.arange(rows_here))[:, None] >= jnp.arange(length)[None, :]
    return jnp.where(causal[None], scores, -1e30)


def send_slots(holding_area, slot_share):
    holding_area = lax.dynamic_slice_in_dim(
        holding_area, lax.axis_index("tensor") * slot_share, slot_share, 2
    )
    received_rows = lax.all_to_all(holding_area, "expert", split_axis=0, concat_axis=0, tiled=True)
    received_rows = lax.all_gather(received_rows, "tensor", axis=2, tiled=True)
    return received_rows


def return_summed(partial_value):
    summed = lax.psum_scatter(
        partial_value.astype(jnp.float32).astype(jnp.bfloat16),
        "tensor",
        scatter_dimension=2,
        tiled=True,
    ).astype(jnp.float32)
    moved = lax.all_to_all(
        summed.astype(jnp.bfloat16), "expert", split_axis=0, concat_axis=0, tiled=True
    ).astype(summed.dtype)
    return lax.all_gather(moved.astype(jnp.bfloat16), "tensor", axis=2, tiled=True).astype(
        moved.dtype
    )


def shards(
    layer_input,
    attn_gain,
    w_query,
    w_kv_down,
    kv_gain,
    w_kv_up,
    w_out,
    ffn_gain,
    w_router,
    routes,
    expert_gate,
    expert_up_projection,
    expert_down,
    shared_gate,
    shared_up,
    shared_down,
    cotangent,
):
    length = layer_input.shape[0]
    tensor_parts = lax.axis_size("tensor")
    expert_ranks = lax.axis_size("expert")
    rank_rows = length // tensor_parts
    row_start = lax.axis_index("tensor") * rank_rows
    qk_width = NOPE + ROPE
    heads_here = w_query.shape[1] // qk_width
    score_scale = qk_width ** (-0.5)
    cos_table, sin_table = tables(length)
    block_rows = min(length, 512)
    input_full = layer_input.astype(jnp.float32)
    normed_full, factor_one = norm_forward(input_full, attn_gain)
    normed_a = normed_full.astype(jnp.bfloat16)
    query_raw = matmul(normed_a, w_query).reshape(length, heads_here, qk_width)
    query_turned = rotate(query_raw[..., NOPE:], cos_table[:, None, :], sin_table[:, None, :])
    query = jnp.concatenate([query_raw[..., :NOPE], query_turned], axis=-1).astype(jnp.bfloat16)
    compressed = matmul(normed_a, w_kv_down)
    latent_raw = compressed[:, :KV_RANK]
    latent_normed, factor_kv = norm_forward(latent_raw, kv_gain)
    latent = latent_normed.astype(jnp.bfloat16)
    key_rope = rotate(compressed[:, KV_RANK:], cos_table, sin_table).astype(jnp.bfloat16)
    key_value = (
        matmul(latent, w_kv_up).astype(jnp.bfloat16).reshape(length, heads_here, NOPE + VDIM)
    )
    key_nope = key_value[..., :NOPE]
    values_all = key_value[..., NOPE:]
    block_index = 0
    start = block_index * block_rows
    scores = block_scores(query, key_nope, key_rope, start, length, score_scale)
    top_score = jnp.max(scores, axis=-1, keepdims=True)
    powered = jnp.exp(scores - top_score)
    total = jnp.sum(powered, axis=-1, keepdims=True)
    probs = (powered / total).astype(jnp.bfloat16)
    log_totals = [top_score + jnp.log(total)]
    head_blocks = jnp.einsum(
        "hqk,khd->qhd", probs, values_all, preferred_element_type=jnp.float32
    ).astype(jnp.bfloat16)
    heads_out = head_blocks.reshape(length, heads_here * VDIM)
    attn_part = matmul(heads_out, w_out)
    attended = sent_and_summed(attn_part.astype(jnp.bfloat16), "tensor", 0)
    input_rows = lax.dynamic_slice_in_dim(input_full, row_start, rank_rows, 0)
    residual = input_rows + attended
    normed_two, factor_two = norm_forward(residual, ffn_gain)
    normed_rows = normed_two.astype(jnp.bfloat16)
    normed_f, cot_all = sent_together((normed_rows, cotangent), "tensor", 0, 1)
    experts_total = w_router.shape[1]
    experts_here = expert_gate.shape[0]
    logits = matmul(normed_f, w_router)
    sigmoid_all = jax.nn.sigmoid(logits)
    picked = (
        routes[:, :, None] == jnp.arange(experts_total, dtype=jnp.int32)[None, None, :]
    ).astype(jnp.float32)
    selected = jnp.sum(sigmoid_all[:, None, :] * picked, axis=-1)
    sel_total = jnp.sum(selected, axis=-1, keepdims=True)
    gates = route_scale * selected / sel_total
    capacity = tensor_parts * max(1, length * TOP * 4 // (3 * experts_total * tensor_parts))
    slot_share = capacity // tensor_parts
    counts = jnp.sum(picked, axis=1).astype(jnp.bfloat16)
    lower = (jnp.arange(length)[:, None] > jnp.arange(length)[None, :]).astype(jnp.bfloat16)
    before = matmul(lower, counts)
    position = jnp.sum(before[:, None, :] * picked, axis=-1).astype(jnp.int32)
    target = routes * capacity + position
    target_rows = lax.dynamic_slice_in_dim(target, row_start, rank_rows, 0)
    gate_rows = lax.dynamic_slice_in_dim(gates, row_start, rank_rows, 0)
    send_buffer = jnp.zeros((experts_total * capacity, D), jnp.bfloat16)
    for route in range(TOP):
        send_buffer = send_buffer.at[target[:, route]].set(normed_f)
    send_buffer = send_buffer.reshape(expert_ranks, experts_here, capacity, D)
    received_rows = send_slots(send_buffer, slot_share)
    expert_gate_value = jnp.einsum(
        "sxcd,xdf->sxcf", received_rows, expert_gate, preferred_element_type=jnp.float32
    )
    expert_up_value = jnp.einsum(
        "sxcd,xdf->sxcf", received_rows, expert_up_projection, preferred_element_type=jnp.float32
    )
    expert_sigma = jax.nn.sigmoid(expert_gate_value)
    expert_swish = expert_gate_value * expert_sigma
    expert_hidden = (expert_swish * expert_up_value).astype(jnp.bfloat16)
    expert_part = jnp.einsum(
        "sxcf,xfd->sxcd", expert_hidden, expert_down, preferred_element_type=jnp.float32
    ).astype(jnp.bfloat16)
    shared_gate_value = matmul(normed_f, shared_gate)
    shared_up_value = matmul(normed_f, shared_up)
    shared_sigma = jax.nn.sigmoid(shared_gate_value)
    shared_silu = shared_gate_value * shared_sigma
    shared_act = (shared_silu * shared_up_value).astype(jnp.bfloat16)
    shared_part = matmul(shared_act, shared_down)
    cot_rows = cotangent.astype(jnp.float32)
    returned = return_summed(expert_part).reshape(experts_total * capacity, D)
    routed_rows = jnp.zeros((rank_rows, D), jnp.float32)
    gate_columns = []
    for route in range(TOP):
        fetched = returned[target_rows[:, route]]
        routed_rows = routed_rows + gate_rows[:, route : route + 1] * fetched
        gate_columns.append(jnp.sum(cot_rows * fetched, axis=-1))
    gate_grad_rows = jnp.stack(gate_columns, axis=1)
    moe_rows = sent_and_summed(shared_part.astype(jnp.bfloat16), "tensor", 0)
    moe_rows = moe_rows + routed_rows
    output = (residual + moe_rows).astype(jnp.bfloat16)
    cot_float = cot_all.astype(jnp.float32)
    grad_buffer = jnp.zeros((experts_total * capacity, D), jnp.bfloat16)
    for route in range(TOP):
        grad_buffer = grad_buffer.at[target[:, route]].set(
            (gates[:, route : route + 1] * cot_float).astype(jnp.bfloat16)
        )
    grad_buffer = grad_buffer.reshape(expert_ranks, experts_here, capacity, D)
    grad_arrived = send_slots(grad_buffer, slot_share)
    gradient_hidden_rows = jnp.einsum(
        "sxcd,xfd->sxcf", grad_arrived, expert_down, preferred_element_type=jnp.float32
    )
    grad_expert_down = jnp.einsum(
        "sxcf,sxcd->xfd", expert_hidden, grad_arrived, preferred_element_type=jnp.float32
    )
    silu_slope = expert_sigma * (1.0 + expert_gate_value * (1.0 - expert_sigma))
    grad_egate = (gradient_hidden_rows * expert_up_value * silu_slope).astype(jnp.bfloat16)
    gradient_expert_up = (gradient_hidden_rows * expert_swish).astype(jnp.bfloat16)
    grad_expert_gate = jnp.einsum(
        "uoeg,uoek->ogk", received_rows, grad_egate, preferred_element_type=jnp.float32
    )
    grad_expert_up = jnp.einsum(
        "uoeg,uoek->ogk", received_rows, gradient_expert_up, preferred_element_type=jnp.float32
    )
    grad_in = jnp.einsum(
        "liha,iwa->lihw", grad_egate, expert_gate, preferred_element_type=jnp.float32
    )
    grad_in = (
        grad_in
        + jnp.einsum(
            "liha,iwa->lihw",
            gradient_expert_up,
            expert_up_projection,
            preferred_element_type=jnp.float32,
        )
    ).astype(jnp.bfloat16)
    grad_shared_hidden = matmul_nt(cot_all, shared_down)
    grad_shared_down = matmul_tn(shared_act, cot_all)
    shared_slope = shared_sigma * (1.0 + shared_gate_value * (1.0 - shared_sigma))
    grad_sgate = (grad_shared_hidden * shared_up_value * shared_slope).astype(jnp.bfloat16)
    grad_sup = (grad_shared_hidden * shared_silu).astype(jnp.bfloat16)
    grad_shared_gate = matmul_tn(normed_f, grad_sgate)
    grad_shared_up = matmul_tn(normed_f, grad_sup)
    shared_back = matmul_nt(grad_sgate, shared_gate) + matmul_nt(grad_sup, shared_up)
    grad_back = return_summed(grad_in).reshape(experts_total * capacity, D)
    routed_back_rows = jnp.zeros((rank_rows, D), jnp.float32)
    for route in range(TOP):
        routed_back_rows = routed_back_rows + grad_back[target_rows[:, route]]
    shared_rows = sent_and_summed(shared_back.astype(jnp.bfloat16), "tensor", 0)
    grad_normed_rows = shared_rows + routed_back_rows
    sel_rows = lax.dynamic_slice_in_dim(selected, row_start, rank_rows, 0)
    total_rows = lax.dynamic_slice_in_dim(sel_total, row_start, rank_rows, 0)
    sigma_rows = lax.dynamic_slice_in_dim(sigmoid_all, row_start, rank_rows, 0)
    picked_rows = lax.dynamic_slice_in_dim(picked, row_start, rank_rows, 0)
    grad_sel = route_scale * (
        gate_grad_rows / total_rows
        - jnp.sum(gate_grad_rows * sel_rows, axis=-1, keepdims=True) / (total_rows * total_rows)
    )
    grad_sigma = jnp.sum(grad_sel[:, :, None] * picked_rows, axis=1)
    grad_logits = (grad_sigma * sigma_rows * (1.0 - sigma_rows)).astype(jnp.bfloat16)
    grad_w_router = matmul_tn(normed_rows, grad_logits)
    grad_normed = grad_normed_rows + matmul_nt(grad_logits, w_router)
    grad_from_norm, grad_ffn_gain = norm_backward(residual, factor_two, ffn_gain, grad_normed)
    grad_residual = cot_rows + grad_from_norm
    grad_attended = collect(grad_residual.astype(jnp.bfloat16), "tensor", 0)
    grad_w_out = matmul_tn(heads_out, grad_attended)
    grad_heads = (
        matmul_nt(grad_attended, w_out).astype(jnp.bfloat16).reshape(length, heads_here, VDIM)
    )
    block_index = 0
    start = block_index * block_rows
    scores = block_scores(query, key_nope, key_rope, start, length, score_scale)
    probs_full = jnp.exp(scores - log_totals[block_index])
    grad_probs = jnp.einsum(
        "qhd,khd->hqk", grad_heads, values_all, preferred_element_type=jnp.float32
    )
    grad_scores = (
        probs_full * (grad_probs - jnp.sum(grad_probs * probs_full, axis=-1, keepdims=True))
    ).astype(jnp.bfloat16)
    grad_query_nope = (
        jnp.einsum("hqk,khd->qhd", grad_scores, key_nope, preferred_element_type=jnp.float32)
        * score_scale
    )
    grad_query_rope = (
        jnp.einsum("hqk,kd->qhd", grad_scores, key_rope, preferred_element_type=jnp.float32)
        * score_scale
    )
    query_grads = jnp.concatenate([grad_query_nope, grad_query_rope], axis=-1)
    grad_key_nope = (
        jnp.einsum(
            "hqk,qhd->khd", grad_scores, query[..., :NOPE], preferred_element_type=jnp.float32
        )
        * score_scale
    )
    grad_key_rope = (
        jnp.einsum(
            "hqk,qhd->kd", grad_scores, query[..., NOPE:], preferred_element_type=jnp.float32
        )
        * score_scale
    )
    grad_values = jnp.einsum(
        "hqk,qhd->khd",
        probs_full.astype(jnp.bfloat16),
        grad_heads,
        preferred_element_type=jnp.float32,
    )
    grad_query_back = rotate_back(
        query_grads[..., NOPE:], cos_table[:, None, :], sin_table[:, None, :]
    )
    grad_query = (
        jnp.concatenate([query_grads[..., :NOPE], grad_query_back], axis=-1)
        .astype(jnp.bfloat16)
        .reshape(length, heads_here * qk_width)
    )
    grad_w_query = matmul_tn(normed_a, grad_query)
    grad_normed_a = matmul_nt(grad_query, w_query)
    grad_key_value = (
        jnp.concatenate([grad_key_nope, grad_values], axis=-1)
        .astype(jnp.bfloat16)
        .reshape(length, heads_here * (NOPE + VDIM))
    )
    grad_w_kv_up = matmul_tn(latent, grad_key_value)
    grad_latent_normed = matmul_nt(grad_key_value, w_kv_up)
    grad_latent, grad_kv_gain = norm_backward(latent_raw, factor_kv, kv_gain, grad_latent_normed)
    grad_rope_part = rotate_back(grad_key_rope, cos_table, sin_table)
    grad_compressed = jnp.concatenate([grad_latent, grad_rope_part], axis=-1)
    grad_normed_a_rows, grad_compressed_rows = tuple(
        (
            part.astype(jnp.float32)
            for part in sent_together_2(
                (grad_normed_a.astype(jnp.bfloat16), grad_compressed.astype(jnp.bfloat16)),
                "tensor",
                0,
                1,
            )
        )
    )
    grad_compressed_low = grad_compressed_rows.astype(jnp.bfloat16)
    normed_a_rows = lax.dynamic_slice_in_dim(normed_a, row_start, rank_rows, 0)
    grad_w_kv_down = matmul_tn(normed_a_rows, grad_compressed_low)
    grad_normed_one = grad_normed_a_rows + matmul_nt(grad_compressed_low, w_kv_down)
    factor_rows = lax.dynamic_slice_in_dim(factor_one, row_start, rank_rows, 0)
    grad_from_first, grad_attn_gain = norm_backward(
        input_rows, factor_rows, attn_gain, grad_normed_one
    )
    grad_input = grad_residual + grad_from_first
    grad_w_query, grad_w_kv_up, grad_w_out, grad_shared_gate, grad_shared_up, grad_shared_down = (
        lax.psum(grad_w_query.astype(jnp.bfloat16), "expert").astype(jnp.float32),
        lax.psum(grad_w_kv_up.astype(jnp.bfloat16), "expert").astype(jnp.float32),
        lax.psum(grad_w_out.astype(jnp.bfloat16), "expert").astype(jnp.float32),
        lax.psum(grad_shared_gate.astype(jnp.bfloat16), "expert").astype(jnp.float32),
        lax.psum(grad_shared_up.astype(jnp.bfloat16), "expert").astype(jnp.float32),
        lax.psum(grad_shared_down.astype(jnp.bfloat16), "expert").astype(jnp.float32),
    )
    grad_w_kv_down, grad_kv_gain, grad_attn_gain, grad_ffn_gain, grad_w_router = in_one(
        (grad_w_kv_down, grad_kv_gain, grad_attn_gain, grad_ffn_gain, grad_w_router),
        ("expert", "tensor"),
    )
    return (
        output,
        grad_input,
        grad_attn_gain,
        grad_w_query,
        grad_w_kv_down,
        grad_kv_gain,
        grad_w_kv_up,
        grad_w_out,
        grad_ffn_gain,
        grad_w_router,
        grad_expert_gate,
        grad_expert_up,
        grad_expert_down,
        grad_shared_gate,
        grad_shared_up,
        grad_shared_down,
    )


def solution(mesh):
    return jax.shard_map(
        shards,
        mesh=mesh,
        in_specs=(
            P("expert", None),
            P(),
            P(None, "tensor"),
            P(),
            P(),
            P(None, "tensor"),
            P("tensor", None),
            P(),
            P(),
            P("expert", None),
            P("expert", None, "tensor"),
            P("expert", None, "tensor"),
            P("expert", "tensor", None),
            P(None, "tensor"),
            P(None, "tensor"),
            P("tensor", None),
            P(("expert", "tensor"), None),
        ),
        out_specs=(
            P(("expert", "tensor"), None),
            P(("expert", "tensor"), None),
            P(),
            P(None, "tensor"),
            P(),
            P(),
            P(None, "tensor"),
            P("tensor", None),
            P(),
            P(),
            P("expert", None, "tensor"),
            P("expert", None, "tensor"),
            P("expert", "tensor", None),
            P(None, "tensor"),
            P(None, "tensor"),
            P("tensor", None),
        ),
        check_vma=False,
    )
```

profile of v0, /device:TPU:1, one launch (start us, length us, event | category | flops | bytes accessed | tf_op | source)
XLA Modules:
  0.0 1473.1 jit_solution(4318166924438091543)
XLA Ops:
  31.0 22.4 %all-to-all-done = bf16[8,64,2048]{2,1,0:T(8,128)(2,1)} async-done(((bf16[8,64,2048]{2,1,0:T(8,128)(2,1)}), bf16[8,64,2048]{2,1,0:T(8,128)(2,1)}, u32[]{:S(2)}, u32[]{:S(2)}) %all-to-all-start) | async-done | bytes 2097184 | tf_op jit(solution)/shard_map/all_to_all | solution.py:27
  59.7 32.9 %all-gather.6.cloned.1.call-done = bf16[512,4096]{1,0:T(8,128)(2,1)} async-done(((bf16[64,4096]{1,0:T(8,128)(2,1)}), bf16[512,4096]{1,0:T(8,128)(2,1)}) %all-gather.6.cloned.1.call-update) | async-done | bytes 4194320 | tf_op jit(solution)/shard_map/all_gather | solution.py:34
  95.6 14.4 scatter_custom_fusion
  110.0 19.8 %scatter_custom_fusion.1 = bf16[4096,2048]{1,0:T(8,128)(2,1)} fusion(bf16[4096,2048]{1,0:T(8,128)(2,1)} %scatter_custom_fusion, s32[512]{0:T(512)S(1)} %bitcast.271, bf16[512,4096]{1,0:T(8,128)(2,1)} %all-gather.6.cloned.1.call-done), kind=kCustom, calls=%fused_computation.281 | custom fusion | bytes 18874368 | tf_op jit(solution)/shard_map/scatter | solution.py:255
  129.8 19.8 %scatter_custom_fusion.2 = bf16[4096,2048]{1,0:T(8,128)(2,1)} fusion(bf16[4096,2048]{1,0:T(8,128)(2,1)} %scatter_custom_fusion.1, s32[512]{0:T(512)S(1)} %bitcast.269, bf16[512,4096]{1,0:T(8,128)(2,1)} %all-gather.6.cloned.1.call-done), kind=kCustom, calls=%fused_computation.279 | custom fusion | bytes 18874368 | tf_op jit(solution)/shard_map/scatter | solution.py:255
  149.7 20.1 %scatter_custom_fusion.3 = bf16[4096,2048]{1,0:T(8,128)(2,1)} fusion(bf16[4096,2048]{1,0:T(8,128)(2,1)} %scatter_custom_fusion.2, s32[512]{0:T(512)S(1)} %bitcast.267, bf16[512,4096]{1,0:T(8,128)(2,1)} %all-gather.6.cloned.1.call-done), kind=kCustom, calls=%fused_computation.277 | custom fusion | bytes 18874368 | tf_op jit(solution)/shard_map/scatter | solution.py:255
  169.7 19.8 %scatter_custom_fusion.4 = bf16[4096,2048]{1,0:T(8,128)(2,1)} fusion(bf16[4096,2048]{1,0:T(8,128)(2,1)} %scatter_custom_fusion.3, s32[512]{0:T(512)S(1)} %bitcast.265, bf16[512,4096]{1,0:T(8,128)(2,1)} %all-gather.6.cloned.1.call-done), kind=kCustom, calls=%fused_computation.275 | custom fusion | bytes 18874368 | tf_op jit(solution)/shard_map/scatter | solution.py:255
  189.5 19.6 %scatter_custom_fusion.5 = bf16[4096,2048]{1,0:T(8,128)(2,1)} fusion(bf16[4096,2048]{1,0:T(8,128)(2,1)} %scatter_custom_fusion.4, s32[512]{0:T(512)S(1)} %bitcast.263, bf16[512,4096]{1,0:T(8,128)(2,1)} %all-gather.6.cloned.1.call-done), kind=kCustom, calls=%fused_computation.273 | custom fusion | bytes 18874368 | tf_op jit(solution)/shard_map/scatter | solution.py:255
  210.9 33.6 %all_to_all.40 = bf16[16,2,16,2048]{3,2,1,0:T(8,128)(2,1)S(1)} all-to-all(bf16[16,2,16,2048]{3,2,1,0:T(8,128)(2,1)S(1)} %constant_dynamic-slice_fusion.2), channel_id=1, replica_groups=mesh['expert'=16,'tensor'=8] {'expert'}, dimensions={0} | all-to-all | bytes 4194304 | tf_op jit(solution)/shard_map/all_to_all | solution.py:150
  246.5 15.8 %scatter_custom_fusion.6 = bf16[4096,2048]{1,0:T(8,128)(2,1)} fusion(s32[512]{0:T(512)S(1)} %bitcast.274, bf16[]{:T(256)} %constant.32.clone.1, f32[512]{0:T(512)S(1)} %bitcast.256, bf16[512,4096]{1,0:T(8,128)(2,1)} %all-gather.6.cloned.1.call-done), kind=kCustom, calls=%fused_computation.35 | custom fusion | flops 3145728 | bytes 18876928 | tf_op jit(solution)/shard_map/scatter | solution.py:291
  262.3 20.6 %scatter_custom_fusion.7 = bf16[4096,2048]{1,0:T(8,128)(2,1)} fusion(bf16[4096,2048]{1,0:T(8,128)(2,1)} %scatter_custom_fusion.6, s32[512]{0:T(512)S(1)} %bitcast.272, f32[512]{0:T(512)S(1)} %bitcast.255, bf16[512,4096]{1,0:T(8,128)(2,1)} %all-gather.6.cloned.1.call-done), kind=kCustom, calls=%fused_computation.83 | custom fusion | flops 3145728 | bytes 18876416 | tf_op jit(solution)/shard_map/scatter | solution.py:291
  283.0 20.4 %scatter_custom_fusion.8 = bf16[4096,2048]{1,0:T(8,128)(2,1)} fusion(bf16[4096,2048]{1,0:T(8,128)(2,1)} %scatter_custom_fusion.7, s32[512]{0:T(512)S(1)} %bitcast.270, f32[512]{0:T(512)S(1)} %bitcast.254, bf16[512,4096]{1,0:T(8,128)(2,1)} %all-gather.6.cloned.1.call-done), kind=kCustom, calls=%fused_computation.82 | custom fusion | flops 3145728 | bytes 18876416 | tf_op jit(solution)/shard_map/scatter | solution.py:291
  303.3 20.2 %scatter_custom_fusion.9 = bf16[4096,2048]{1,0:T(8,128)(2,1)} fusion(bf16[4096,2048]{1,0:T(8,128)(2,1)} %scatter_custom_fusion.8, s32[512]{0:T(512)S(1)} %bitcast.268, f32[512]{0:T(512)S(1)} %bitcast.253, bf16[512,4096]{1,0:T(8,128)(2,1)} %all-gather.6.cloned.1.call-done), kind=kCustom, calls=%fused_computation.81 | custom fusion | flops 3145728 | bytes 18876416 | tf_op jit(solution)/shard_map/scatter | solution.py:291
  323.6 20.1 %scatter_custom_fusion.10 = bf16[4096,2048]{1,0:T(8,128)(2,1)} fusion(bf16[4096,2048]{1,0:T(8,128)(2,1)} %scatter_custom_fusion.9, s32[512]{0:T(512)S(1)} %bitcast.266, f32[512]{0:T(512)S(1)} %bitcast.252, bf16[512,4096]{1,0:T(8,128)(2,1)} %all-gather.6.cloned.1.call-done), kind=kCustom, calls=%fused_computation.80 | custom fusion | flops 3145728 | bytes 18876416 | tf_op jit(solution)/shard_map/scatter | solution.py:291
  343.6 19.7 %scatter_custom_fusion.11 = bf16[4096,2048]{1,0:T(8,128)(2,1)} fusion(bf16[4096,2048]{1,0:T(8,128)(2,1)} %scatter_custom_fusion.10, s32[512]{0:T(512)S(1)} %bitcast.264, f32[512]{0:T(512)S(1)} %bitcast.251, bf16[512,4096]{1,0:T(8,128)(2,1)} %all-gather.6.cloned.1.call-done), kind=kCustom, calls=%fused_computation.79 | custom fusion | flops 3145728 | bytes 18876416 | tf_op jit(solution)/shard_map/scatter | solution.py:291
  365.1 30.5 %all_to_all.41 = bf16[16,2,16,2048]{3,2,1,0:T(8,128)(2,1)S(1)} all-to-all(bf16[16,2,16,2048]{3,2,1,0:T(8,128)(2,1)S(1)} %constant_dynamic-slice_fusion), channel_id=1, replica_groups=mesh['expert'=16,'tensor'=8] {'expert'}, dimensions={0} | all-to-all | bytes 4194304 | tf_op jit(solution)/shard_map/all_to_all | solution.py:150
  420.4 61.4 %all-gather.12.cloned.1.call-done = bf16[16,2,128,2048]{3,2,0,1:T(8,128)(2,1)} async-done(((bf16[16,2,16,2048]{3,2,0,1:T(8,128)(2,1)}), bf16[16,2,128,2048]{3,2,0,1:T(8,128)(2,1)}) %all-gather.12.cloned.1.call-update) | async-done | bytes 16777232 | tf_op jit(solution)/shard_map/all_gather | solution.py:151
  506.9 18.8 %fusion.44 = f32[2,16,128,2048]{3,2,1,0:T(8,128)} fusion(bf16[16,2,128,176]{2,3,0,1:T(8,128)(2,1)} %get-tuple-element.110, bf16[2,2048,176]{1,2,0:T(8,128)(2,1)} %param.27), kind=kOutput, calls=%fused_computation.103 | convolution fusion | flops 2952790016 | bytes 36438016 | tf_op jit(solution)/shard_map/liha,iwa->lihw/dot_general | solution.py:311
  525.7 17.5 %fusion = bf16[16,2,128,2048]{3,2,0,1:T(8,128)(2,1)} fusion(f32[2,16,128,2048]{3,2,1,0:T(8,128)} %fusion.44, bf16[16,2,128,176]{2,3,0,1:T(8,128)(2,1)S(1)} %copy-done.8, bf16[2,2048,176]{1,2,0:T(8,128)(2,1)S(1)} %copy-done.38), kind=kOutput, calls=%fused_computation.25 | convolution fusion | flops 2969567232 | bytes 53215232 | tf_op jit(solution)/shard_map/liha,iwa->lihw/dot_general | solution.py:316
  543.3 54.9 %reduce-scatter.4.cloned.1.call-done = bf16[16,2,16,2048]{3,2,0,1:T(8,128)(2,1)} async-done(((bf16[16,2,128,2048]{3,2,0,1:T(8,128)(2,1)}), bf16[16,2,16,2048]{3,2,0,1:T(8,128)(2,1)}) %reduce-scatter.4.cloned.1.call-update) | async-done | bytes 2097168 | tf_op jit(solution)/shard_map/reduce_scatter | solution.py:156
  599.9 32.4 %all_to_all.42 = bf16[16,2,16,2048]{3,2,1,0:T(8,128)(2,1)} all-to-all(bf16[16,2,16,2048]{3,2,1,0:T(8,128)(2,1)S(1)} %copy.133), channel_id=1, replica_groups=mesh['expert'=16,'tensor'=8] {'expert'}, dimensions={0} | all-to-all | bytes 4194304 | tf_op jit(solution)/shard_map/all_to_all | solution.py:162
  632.3 59.5 %reduce-scatter.6.cloned.1.call-done = bf16[16,2,16,2048]{3,2,0,1:T(8,128)(2,1)} async-done(((bf16[16,2,128,2048]{3,2,0,1:T(8,128)(2,1)}), bf16[16,2,16,2048]{3,2,0,1:T(8,128)(2,1)}) %reduce-scatter.6.cloned.1.call-update) | async-done | bytes 2097168 | tf_op jit(solution)/shard_map/reduce_scatter | solution.py:156
  693.6 32.3 %all_to_all.43 = bf16[16,2,16,2048]{3,2,1,0:T(8,128)(2,1)} all-to-all(bf16[16,2,16,2048]{3,2,1,0:T(8,128)(2,1)S(1)} %copy.135), channel_id=1, replica_groups=mesh['expert'=16,'tensor'=8] {'expert'}, dimensions={0} | all-to-all | bytes 4194304 | tf_op jit(solution)/shard_map/all_to_all | solution.py:162
  748.6 43.4 %all-to-all-done.1 = bf16[8,64,2048]{2,1,0:T(8,128)(2,1)} async-done(((bf16[8,64,2048]{2,1,0:T(8,128)(2,1)}), bf16[8,64,2048]{2,1,0:T(8,128)(2,1)}, u32[]{:S(2)}, u32[]{:S(2)}) %all-to-all-start.1) | async-done | bytes 2097184 | tf_op jit(solution)/shard_map/all_to_all | solution.py:27
  801.9 22.3 %all-to-all-done.4 = bf16[8,64,2048]{2,1,0:T(8,128)(2,1)} async-done(((bf16[8,64,2048]{2,1,0:T(8,128)(2,1)}), bf16[8,64,2048]{2,1,0:T(8,128)(2,1)}, u32[]{:S(2)}, u32[]{:S(2)}) %all-to-all-start.4) | async-done | bytes 2097184 | tf_op jit(solution)/shard_map/all_to_all | solution.py:27
  827.0 18.9 %bitcast_convert_fusion.1 = f32[4096,2048]{1,0:T(8,128)} fusion(bf16[16,2,128,2048]{3,2,1,0:T(8,128)(2,1)} %all-gather.10.cloned.1.call-done), kind=kLoop, calls=%fused_computation.27 | loop fusion | flops 8388608 | bytes 50331648 | tf_op jit(solution)/shard_map/reshape | solution.py:277
  845.9 13.0 gather_fusion.5
  871.7 22.2 %all-gather.14.cloned.1.call-done = bf16[16,2,128,2048]{3,2,1,0:T(8,128)(2,1)} async-done(((bf16[16,2,16,2048]{3,2,1,0:T(8,128)(2,1)}), bf16[16,2,128,2048]{3,2,1,0:T(8,128)(2,1)}) %all-gather.14.cloned.1.call-update) | async-done | bytes 16777232 | tf_op jit(solution)/shard_map/all_gather | solution.py:165
  893.9 18.8 %bitcast_convert_fusion = f32[4096,2048]{1,0:T(8,128)} fusion(bf16[16,2,128,2048]{3,2,1,0:T(8,128)(2,1)} %all-gather.14.cloned.1.call-done), kind=kLoop, calls=%fused_computation.26 | loop fusion | flops 8388608 | bytes 50331648 | tf_op jit(solution)/shard_map/reshape | solution.py:331
  1053.7 26.0 %all-to-all-done.7 = bf16[8,64,2048]{2,1,0:T(8,128)(2,1)} async-done(((bf16[8,64,2048]{2,1,0:T(8,128)(2,1)}), bf16[8,64,2048]{2,1,0:T(8,128)(2,1)}, u32[]{:S(2)}, u32[]{:S(2)}) %all-to-all-start.7) | async-done | bytes 2097184 | tf_op jit(solution)/shard_map/all_to_all | solution.py:40
  1185.9 97.4 %all-reduce.6.cloned.1.call-done = (bf16[2048,384]{1,0:T(8,128)(2,1)}, bf16[512,512]{1,0:T(8,128)(2,1)}, bf16[256,2048]{1,0:T(8,128)(2,1)}, bf16[2048,352]{0,1:T...) async-done(((bf16[2048,384]{1,0:T(8,128)(2,1)}, bf16[512,512]{1,0:T(8,128)(2,1)}, bf16[256,2048]{1,0:T(8,128)(2,1)}, bf16[2048,352]{0,1:T(8,128)(2,1)}, ...) | async-done | bytes 7471120 | tf_op jit(solution)/shard_map/psum | solution.py:434
  1295.0 148.2 %all-reduce.4.cloned.1.call-done = f32[1249792]{0:T(1024)} async-done(((f32[1249792]{0:T(1024)}), f32[1249792]{0:T(1024)}) %all-reduce.4.cloned.1.call-update) | async-done | bytes 4999184 | tf_op jit(solution)/shard_map/psum | solution.py:67
  (345 shorter events, 421.1 us)
Async XLA Ops:
  20.9 32.4 %all-to-all-start = ((bf16[8,64,2048]{2,1,0:T(8,128)(2,1)}), bf16[8,64,2048]{2,1,0:T(8,128)(2,1)}, u32[]{:S(2)}, u32[]{:S(2)}) async-start(bf16[8,64,2048]{2,1,0:T(8,128)(2,1)} %bitcast.233), calls=%async_computation | async-start | bytes 4194304 | tf_op jit(solution)/shard_map/all_to_all | solution.py:27
  26.9 65.7 %all-gather.6.cloned.1.call-start = ((), (), s32[]{:S(2)}) async-start(), calls=%async_computation.11 | async-start | bytes 4718592 | tf_op jit(solution)/shard_map/all_gather | solution.py:34
  31.0 26.7 %copy-start.63 = (f32[2048]{0:T(1024)S(1)}, f32[2048]{0:T(1024)}, u32[]{:S(2)}) copy-start(f32[2048]{0:T(1024)} %param.24) | copy-start | bytes 24580
  31.0 27.5 %copy-start.18 = (bf16[64,2048]{1,0:T(8,128)(2,1)S(1)}, bf16[64,2048]{1,0:T(8,128)(2,1)}, u32[]{:S(2)}) copy-start(bf16[64,2048]{1,0:T(8,128)(2,1)} %param.33) | copy-start | bytes 786436
  55.4 37.3 %copy-start.60 = (bf16[2048,32]{0,1:T(8,128)(2,1)S(1)}, bf16[2048,32]{0,1:T(8,128)(2,1)}, u32[]{:S(2)}) copy-start(bf16[2048,32]{0,1:T(8,128)(2,1)} %param.25) | copy-start | bytes 393220
  58.5 36.5 %copy-start.58 = (s32[512,6]{0,1:T(8,128)S(1)}, s32[512,6]{0,1:T(8,128)}, u32[]{:S(2)}) copy-start(s32[512,6]{0,1:T(8,128)} %param.26) | copy-start | bytes 36868
  59.4 337.7 %all-gather.8.cloned.1.call-start = ((), (), s32[]{:S(2)}) async-start(), calls=%async_computation.12 | async-start | bytes 18874368 | tf_op jit(solution)/shard_map/all_gather | solution.py:151
  95.1 151.4 %copy-start.62 = (f32[512,6]{0,1:T(8,128)}, f32[512,6]{0,1:T(8,128)S(1)}, u32[]{:S(2)}) copy-start(f32[512,6]{0,1:T(8,128)S(1)} %get-tuple-element.93) | copy-start | bytes 36868
  95.1 151.4 %copy-start.77 = (f32[512]{0:T(512)}, f32[512]{0:T(512)S(1)}, u32[]{:S(2)}) copy-start(f32[512]{0:T(512)S(1)} %get-tuple-element.92) | copy-start | bytes 6148
  95.6 14.4 copy-start.67
  246.0 235.8 %all-gather.12.cloned.1.call-start = ((), (), s32[]{:S(2)}) async-start(), calls=%async_computation.15 | async-start | bytes 18874368 | tf_op jit(solution)/shard_map/all_gather | solution.py:151
  397.0 201.2 %reduce-scatter.4.cloned.1.call-start = ((), (), s32[]{:S(2)}) async-start(), calls=%async_computation.13 | async-start | bytes 18874368 | tf_op jit(solution)/shard_map/reduce_scatter | solution.py:156
  397.1 10.9 copy-start.37
  506.6 185.2 %reduce-scatter.6.cloned.1.call-start = ((), (), s32[]{:S(2)}) async-start(), calls=%async_computation.16 | async-start | bytes 18874368 | tf_op jit(solution)/shard_map/reduce_scatter | solution.py:156
  506.9 18.8 %copy-start.8 = (bf16[16,2,128,176]{2,3,0,1:T(8,128)(2,1)S(1)}, bf16[16,2,128,176]{2,3,0,1:T(8,128)(2,1)}, u32[]{:S(2)}) copy-start(bf16[16,2,128,176]{2,3,0,1:T(8,128)(2,1)} %get-tuple-element.109) | copy-start | bytes 4325380
  506.9 18.8 %copy-start.38 = (bf16[2,2048,176]{1,2,0:T(8,128)(2,1)S(1)}, bf16[2,2048,176]{1,2,0:T(8,128)(2,1)}, u32[]{:S(2)}) copy-start(bf16[2,2048,176]{1,2,0:T(8,128)(2,1)} %param.28) | copy-start | bytes 4325380
  543.2 283.8 %all-gather.10.cloned.1.call-start = ((), (), s32[]{:S(2)}) async-start(), calls=%async_computation.14 | async-start | bytes 18874368 | tf_op jit(solution)/shard_map/all_gather | solution.py:165
  632.3 261.6 %all-gather.14.cloned.1.call-start = ((), (), s32[]{:S(2)}) async-start(), calls=%async_computation.17 | async-start | bytes 18874368 | tf_op jit(solution)/shard_map/all_gather | solution.py:165
  732.5 10.4 copy-start.43
  732.5 13.4 copy-start.53
  735.1 56.9 %all-to-all-start.1 = ((bf16[8,64,2048]{2,1,0:T(8,128)(2,1)}), bf16[8,64,2048]{2,1,0:T(8,128)(2,1)}, u32[]{:S(2)}, u32[]{:S(2)}) async-start(bf16[8,64,2048]{2,1,0:T(8,128)(2,1)} %bitcast.244), calls=%async_computation.1 | async-start | bytes 4194304 | tf_op jit(solution)/shard_map/all_to_all | solution.py:27
  792.1 32.1 %all-to-all-start.4 = ((bf16[8,64,2048]{2,1,0:T(8,128)(2,1)}), bf16[8,64,2048]{2,1,0:T(8,128)(2,1)}, u32[]{:S(2)}, u32[]{:S(2)}) async-start(bf16[8,64,2048]{2,1,0:T(8,128)(2,1)} %bitcast.234), calls=%async_computation.5 | async-start | bytes 4194304 | tf_op jit(solution)/shard_map/all_to_all | solution.py:27
  1023.5 12.4 copy-start.12
  1023.5 12.4 copy-start.19
  1048.6 31.1 %copy-start.42 = (bf16[256,2048]{1,0:T(8,128)(2,1)S(1)}, bf16[256,2048]{1,0:T(8,128)(2,1)}, u32[]{:S(2)}) copy-start(bf16[256,2048]{1,0:T(8,128)(2,1)} %param.23) | copy-start | bytes 3145732
  1048.6 31.1 %all-to-all-start.7 = ((bf16[8,64,2048]{2,1,0:T(8,128)(2,1)}), bf16[8,64,2048]{2,1,0:T(8,128)(2,1)}, u32[]{:S(2)}, u32[]{:S(2)}) async-start(bf16[8,64,2048]{2,1,0:T(8,128)(2,1)} %broadcast_in_dim.20), calls=%async_computation.9 | async-start | bytes 4194304 | tf_op jit(solution)/shard_map/all_to_all | solution.py:40
  1053.2 88.6 %reduce-scatter.8.cloned.1.call-start = ((), (), s32[]{:S(2)}) async-start(), calls=%async_computation.18 | async-start | bytes 3096576 | tf_op jit(solution)/shard_map/reduce_scatter | solution.py:56
  1111.0 172.3 %all-reduce.6.cloned.1.call-start = ((), (), s32[]{:S(2)}) async-start(), calls=%async_computation.20 | async-start | bytes 14942208 | tf_op jit(solution)/shard_map/psum | solution.py:434
  1120.3 9.4 copy-start.21
  1141.6 301.6 %all-reduce.4.cloned.1.call-start = ((), (), s32[]{:S(2)}) async-start(), calls=%async_computation.19 | async-start | bytes 10002432 | tf_op jit(solution)/shard_map/psum | solution.py:67
  1174.3 9.6 copy-start.24
  1174.3 9.6 copy-start.86
  (73 other events, 209.1 us)
Sparse Core Ops, SparseCore 0:
  59.5 33.0 all-gather.5
  246.1 83.2 all-gather.7
  397.1 84.6 all-gather.11
  506.8 91.3 reduce-scatter.3
  600.5 91.3 reduce-scatter.5
  693.4 107.9 all-gather.9
  803.1 90.7 all-gather.13
  1111.1 30.2 reduce-scatter.7
  1147.4 135.8 all-reduce.5
  1288.1 155.0 all-reduce.3
where the time goes:
time: 1480 us; the launch traced here: 1470 us
  waiting for transfers between devices  591 us (40%)
  local copies, waits for them, and re-layouts  335 us (23%)
  other arithmetic  201 us (14%)
  matrix products  176 us (12%)
  blocking collectives  129 us (9%)
  starting transfers between devices  25.4 us (2%)
  between operations  15.4 us (1%)
    psum x1, waiting for transfers between devices, in_one(): total = lax.psum(jnp.concatenate([a.ravel() for a in arrays]), axis)  148 us
    scatter x6, other arithmetic, shards(): grad_buffer.at[target[:, route]]  117 us
    reduce_scatter x2, waiting for transfers between devices, return_summed(): lax.psum_scatter(partial_value.astype(jnp.float32).astype(jnp.bfloat16),...  114 us
    scatter x6, local copies, waits for them, and re-layouts, shards(): send_buffer = send_buffer.at[target[:, route]].set(normed_f)  113 us
    psum x1, waiting for transfers between devices, shards(): lax.psum(grad_w_query.astype(jnp.bfloat16), 'expert').astype(jnp.float32)  97.4 us
    all_to_all x3, waiting for transfers between devices, sent_and_summed(): tiles = lax.all_to_all(in_blocks(x, dim, size), axis, 0, 0, tiled=True)  88.1 us
    gather x6, local copies, waits for them, and re-layouts, shards(): fetched = returned[target_rows[:, route]]  75 us
    gather x6, local copies, waits for them, and re-layouts, shards(): routed_back_rows = routed_back_rows + grad_back[target_rows[:, route]]  74 us
  transfers between devices with their start and end apart: 14, of which 11 were waited for; matrix products, arithmetic and copies ran while one was open for 23% of the time, Pallas kernels for 0%

commit v1 on v0

v1 whole, which is shorter than its diff:
```python
import jax
import jax.numpy as jnp
from jax import lax
from jax.experimental import pallas as pl
from jax.experimental.pallas import tpu as pltpu
from jax.sharding import Mesh, PartitionSpec as P

D = 2048
NOPE = 128
ROPE = 64
VDIM = 128
KV_RANK = 512
TOP = 6
RANKS = 16
RINGS = 4
CORES = 2

epsilon = 1e-06
route_scale = 2.446
theta_base = 50000.0

EXPERT = ("x", "z")
GROUP = ("y", "core")
SWAP = [(0, 1), (1, 0)]
PAIRS = [(0, 1), (1, 0), (2, 3), (3, 2)]
OPPOSITE = [(0, 2), (2, 0), (1, 3), (3, 1)]
CROSS = [(1, 2), (2, 1), (3, 0), (0, 3)]


def after(x, *finished):
    return lax.optimization_barrier((x, *finished))[0]


def gather_rows(x):
    return lax.all_gather(x, GROUP, axis=0, tiled=True)


def gather_rows_directly(x, first_core):
    copies = jnp.broadcast_to(x[None], (RINGS, *x.shape))
    mine = lax.all_to_all(copies, "y", 0, 0, tiled=True)
    other = lax.ppermute(mine, "core", SWAP)
    first, second = jnp.where(first_core, mine, other), jnp.where(first_core, other, mine)
    return jnp.stack([first, second], axis=1).reshape(-1, x.shape[1])


def by_core(x, first_core):
    tiles = x.reshape(RINGS, CORES, x.shape[0] // (RINGS * CORES), x.shape[1])
    kept = jnp.where(first_core, tiles[:, 0], tiles[:, 1])
    given = jnp.where(first_core, tiles[:, 1], tiles[:, 0])
    return kept.reshape(-1, x.shape[1]), given.reshape(-1, x.shape[1])


def sum_rows(kept, given):
    other = lax.ppermute(given.astype(jnp.bfloat16), "core", SWAP)
    both = (kept.astype(jnp.float32) + other.astype(jnp.float32)).astype(jnp.bfloat16)
    tiles = both.reshape(RINGS, both.shape[0] // RINGS, both.shape[1])
    return lax.all_to_all(tiles, "y", 0, 0, tiled=True)


def sum_rows_directly(kept, given):
    other = lax.ppermute(given.astype(jnp.bfloat16), "core", SWAP)
    both = (kept.astype(jnp.float32) + other.astype(jnp.float32)).astype(jnp.bfloat16)
    tiles = both.reshape(RINGS, both.shape[0] // RINGS, both.shape[1])
    y = lax.axis_index("y")
    total = lax.dynamic_index_in_dim(tiles, y, 0, keepdims=False).astype(jnp.float32)
    for pairs in (PAIRS, CROSS, OPPOSITE):
        place = jnp.array([b for _, b in sorted(pairs)], jnp.int32)[y]
        tile = lax.dynamic_index_in_dim(tiles, place, 0, keepdims=False)
        total = total + lax.ppermute(tile, "y", pairs).astype(jnp.float32)
    return total


def total_of(tiles):
    return jnp.sum(tiles.astype(jnp.float32), axis=0)


def sum_ranks(x):
    tiles = lax.all_to_all(x, EXPERT, 0, 0, tiled=True)
    total = jnp.sum(tiles.astype(jnp.float32), axis=0).astype(jnp.bfloat16)
    return lax.all_to_all(jnp.broadcast_to(total[None], x.shape), EXPERT, 0, 0, tiled=True)


def angles_of(places):
    half_width = ROPE // 2
    steps_float = jnp.arange(half_width, dtype=jnp.float32) * (2.0 / ROPE)
    frequency = jnp.exp(-jnp.log(theta_base) * steps_float)
    angles = places.astype(jnp.float32)[:, None] * frequency[None, :]
    return (jnp.cos(angles), jnp.sin(angles))


def rotate(values, cos_table, sin_table):
    half_width = ROPE // 2
    first_half = values[..., :half_width]
    second_half = values[..., half_width:]
    return jnp.concatenate(
        [
            first_half * cos_table - second_half * sin_table,
            second_half * cos_table + first_half * sin_table,
        ],
        axis=-1,
    )


def rotate_back(upstream, cos_table, sin_table):
    half_width = ROPE // 2
    first_half = upstream[..., :half_width]
    second_half = upstream[..., half_width:]
    return jnp.concatenate(
        [
            first_half * cos_table + second_half * sin_table,
            second_half * cos_table - first_half * sin_table,
        ],
        axis=-1,
    )


def matmul(left, right):
    return jnp.dot(left, right, preferred_element_type=jnp.float32)


def matmul_tn(left, right):
    return lax.dot_general(
        left, right, (((0,), (0,)), ((), ())), preferred_element_type=jnp.float32
    )


def matmul_nt(left, right):
    return lax.dot_general(
        left, right, (((1,), (1,)), ((), ())), preferred_element_type=jnp.float32
    )


def norm_forward(values, scales):
    factor = lax.rsqrt(jnp.mean(values * values, axis=-1, keepdims=True) + epsilon)
    return (values * factor * scales, factor)


def norm_backward(values, factor, scales, upstream):
    scaled = upstream * scales
    cubed = factor * factor * factor
    d_values = factor * scaled - values * cubed * jnp.mean(scaled * values, axis=-1, keepdims=True)
    return (d_values, jnp.sum(upstream * values * factor, axis=0))


def split_float(v):
    high = v.astype(jnp.bfloat16)
    low = (v - high.astype(jnp.float32)).astype(jnp.bfloat16)
    return high, low


def to_owners(x):
    return lax.all_to_all(
        x.reshape(RANKS, x.shape[0] // RANKS, x.shape[1]), EXPERT, 0, 0, tiled=True
    ).reshape(x.shape)


HIDDEN = 176
TILE = 256
WIDTH = 512
LOW = 64
LONG = 100_000_000_000
SHORT = 18_000_000_000
VMEM_BYTES = 60 * 1024 * 1024


def dot_nt(left, right):
    return lax.dot_general(
        left, right, (((1,), (1,)), ((), ())), preferred_element_type=jnp.float32
    )


def dot_tn(left, right):
    return lax.dot_general(
        left, right, (((0,), (0,)), ((), ())), preferred_element_type=jnp.float32
    )


def hidden_loop(first, last, carry, step):
    return lax.fori_loop(
        first, last, lambda i, c: step(pl.multiple_of(i * TILE, TILE), TILE, c), carry
    )


def dispatch_kernel(map_ref, rows_ref, tail_ref, out):
    def some(j, carry):
        columns = pl.ds(pl.multiple_of(j * WIDTH, WIDTH), WIDTH)
        out[:, columns] = dot_tn(map_ref[...], rows_ref[:, columns]).astype(jnp.bfloat16)
        return carry

    lax.fori_loop(0, D // WIDTH, some, 0)
    out[:, D:] = dot_tn(map_ref[...], tail_ref[...]).astype(jnp.bfloat16)


def dispatch(slot_map, rows, tail):
    slots, width = slot_map.shape[1], rows.shape[1] + tail.shape[1]
    return pl.pallas_call(
        dispatch_kernel,
        out_shape=jax.ShapeDtypeStruct((slots, width), jnp.bfloat16),
        in_specs=[pl.BlockSpec(memory_space=pltpu.VMEM)] * 3,
        out_specs=pl.BlockSpec(memory_space=pltpu.VMEM),
        compiler_params=pltpu.CompilerParams(vmem_limit_bytes=VMEM_BYTES),
        cost_estimate=pl.CostEstimate(
            flops=2 * slots * slot_map.shape[0] * width, bytes_accessed=8 << 20, transcendentals=0
        ),
        name="dispatch",
    )(slot_map, rows, tail)


def shared_kernel(
    core,
    rows_ref,
    cot_ref,
    w_gate,
    w_up,
    w_down,
    gate_grads,
    up_grads,
    down_grads,
    act,
    kept,
    given,
    sgate,
    sup,
):
    block = rows_ref.shape[0] // (RINGS * CORES)
    gate_value = dot_nt(rows_ref[...], w_gate[...])
    up_value = dot_nt(rows_ref[...], w_up[...])
    back = dot_nt(cot_ref[...], w_down[...])
    sigma = jax.nn.sigmoid(gate_value)
    swish = gate_value * sigma
    act[...] = (swish * up_value).astype(jnp.bfloat16)
    slope = sigma * (1.0 + gate_value * (1.0 - sigma))
    sgate[...] = (back * up_value * slope).astype(jnp.bfloat16)
    sup[...] = (back * swish).astype(jnp.bfloat16)

    def some(j, carry):
        columns = pl.ds(pl.multiple_of(j * WIDTH, WIDTH), WIDTH)
        rows, cot = rows_ref[:, columns], cot_ref[:, columns]
        gate_grads[:, columns] = dot_tn(sgate[...], rows).astype(jnp.bfloat16)
        up_grads[:, columns] = dot_tn(sup[...], rows).astype(jnp.bfloat16)
        down_grads[:, columns] = dot_tn(act[...], cot).astype(jnp.bfloat16)
        value = jnp.dot(sgate[...], w_gate[:, columns], preferred_element_type=jnp.float32)
        value += jnp.dot(sup[...], w_up[:, columns], preferred_element_type=jnp.float32)
        for half in range(CORES):
            for target, chosen in ((kept, core[0] == half), (given, core[0] != half)):

                @pl.when(chosen)
                def _():
                    for chip in range(RINGS):
                        first = (chip * CORES + half) * block
                        target[chip * block : (chip + 1) * block, columns] = value[
                            first : first + block
                        ]

        return carry

    lax.fori_loop(0, D // WIDTH, some, 0)


def shared_experts(core, rows, cot, w_gate, w_up, w_down):
    length, width = rows.shape[0], w_gate.shape[0]
    half = jax.ShapeDtypeStruct((length // 2, D), jnp.float32)
    hidden = (length, width)
    vmem = pl.BlockSpec(memory_space=pltpu.VMEM)
    return pl.pallas_call(
        shared_kernel,
        out_shape=(jax.ShapeDtypeStruct((width, D), jnp.bfloat16),) * 3
        + (jax.ShapeDtypeStruct(hidden, jnp.bfloat16), half, half),
        in_specs=[pl.BlockSpec(memory_space=pltpu.SMEM)] + [vmem] * 5,
        out_specs=(vmem,) * 6,
        scratch_shapes=[pltpu.VMEM(hidden, jnp.bfloat16)] * 2,
        compiler_params=pltpu.CompilerParams(vmem_limit_bytes=VMEM_BYTES),
        cost_estimate=pl.CostEstimate(flops=SHORT, bytes_accessed=20 << 20, transcendentals=0),
        name="shared_experts",
    )(core, rows, cot, w_gate, w_up, w_down)


def kv_kernel(left, right, out):
    out[...] = jnp.dot(left[...], right[...], preferred_element_type=jnp.float32).astype(
        jnp.bfloat16
    )


def kv_product(left, right):
    vmem = pl.BlockSpec(memory_space=pltpu.VMEM)
    return pl.pallas_call(
        kv_kernel,
        out_shape=jax.ShapeDtypeStruct((left.shape[0], right.shape[1]), jnp.bfloat16),
        in_specs=[vmem] * 2,
        out_specs=vmem,
        compiler_params=pltpu.CompilerParams(vmem_limit_bytes=VMEM_BYTES),
        cost_estimate=pl.CostEstimate(flops=SHORT, bytes_accessed=4 << 20, transcendentals=0),
        name="kv_product",
    )(left, right)


def attention_kernel(
    core, query_ref, compressed_ref, x_ref, factor_ref, w_query, w_down, kept, given, gain
):
    block = x_ref.shape[0] // (RINGS * CORES)

    def some(j, carry):
        columns = pl.ds(pl.multiple_of(j * WIDTH, WIDTH), WIDTH)
        scaled = x_ref[:, columns].astype(jnp.float32) * factor_ref[...]
        value = dot_nt(query_ref[...], w_query[columns, :])
        value += jnp.dot(
            compressed_ref[...], w_down[:, columns], preferred_element_type=jnp.float32
        )
        gain[:, columns] = jnp.sum(value * scaled, axis=0, keepdims=True)
        value = value.astype(jnp.bfloat16)
        for half in range(CORES):
            for target, chosen in ((kept, core[0] == half), (given, core[0] != half)):

                @pl.when(chosen)
                def _():
                    for chip in range(RINGS):
                        first = (chip * CORES + half) * block
                        target[chip * block : (chip + 1) * block, columns] = value[
                            first : first + block
                        ]

        return carry

    lax.fori_loop(0, D // WIDTH, some, 0)


def attention_rows(core, query, compressed, x, factor, w_query, w_down):
    half = jax.ShapeDtypeStruct((x.shape[0] // 2, D), jnp.bfloat16)
    vmem = pl.BlockSpec(memory_space=pltpu.VMEM)
    return pl.pallas_call(
        attention_kernel,
        out_shape=(half, half, jax.ShapeDtypeStruct((1, D), jnp.float32)),
        in_specs=[pl.BlockSpec(memory_space=pltpu.SMEM)] + [vmem] * 6,
        out_specs=(vmem,) * 3,
        compiler_params=pltpu.CompilerParams(vmem_limit_bytes=VMEM_BYTES),
        cost_estimate=pl.CostEstimate(flops=LONG, bytes_accessed=10 << 20, transcendentals=0),
        name="attention_rows",
    )(core, query, compressed, x, factor, w_query, w_down)


def expert_kernel(*refs):
    expert, x_hbm, y_hbm = refs[:3]
    blocks = refs[3:11]
    back, gate_out, up_out, act_out = refs[11:15]
    x_ref, y_ref, w_gate, w_up, w_down, sems = refs[15:]
    total = w_gate.shape[0]
    copies = [
        pltpu.make_async_copy(x_hbm, x_ref, sems.at[0]),
        pltpu.make_async_copy(y_hbm, y_ref, sems.at[1]),
    ]
    for i, block in enumerate(blocks):
        rows = pl.ds(i * HIDDEN, HIDDEN)
        for m, w in enumerate((w_gate, w_up, w_down)):
            copies.append(
                pltpu.make_async_copy(
                    block.at[pl.ds(m * HIDDEN, HIDDEN)], w.at[rows], sems.at[2 + 3 * i + m]
                )
            )
    for copy in copies:
        copy.start()
    half = 2 + len(copies[2:]) // 2
    for copy in copies[:half]:
        copy.wait()
    lanes = lax.broadcasted_iota(jnp.int32, (x_ref.shape[0], 128), 1)
    high_lane, low_lane = lanes == expert[0], lanes == expert[0] + LOW
    tail = x_ref[:, D:].astype(jnp.float32)
    gate = jnp.sum(jnp.where(high_lane | low_lane, tail, 0.0), axis=-1, keepdims=True)

    def hidden(start, width, summed):
        rows = pl.ds(start, width)
        x = x_ref[:, :D]
        gate_value = dot_nt(x, w_gate[rows, :])
        up_value = dot_nt(x, w_up[rows, :])
        raw = dot_nt(y_ref[...], w_down[rows, :])
        sigma = jax.nn.sigmoid(gate_value)
        swish = gate_value * sigma
        act = swish * up_value
        summed = summed + jnp.sum(raw * act, axis=-1, keepdims=True)
        raw = raw * gate
        slope = sigma * (1.0 + gate_value * (1.0 - sigma))
        gate_out[:, rows] = (raw * up_value * slope).astype(jnp.bfloat16)
        up_out[:, rows] = (raw * swish).astype(jnp.bfloat16)
        act_out[:, rows] = (act * gate).astype(jnp.bfloat16)
        return summed

    ready = (total // 2) // TILE
    whole = total // TILE
    summed = hidden_loop(0, ready, jnp.zeros((x_ref.shape[0], 1), jnp.float32), hidden)
    for copy in copies[half:]:
        copy.wait()
    summed = hidden_loop(ready, whole, summed, hidden)
    if total % TILE:
        summed = hidden(whole * TILE, total % TILE, summed)
    high = summed.astype(jnp.bfloat16).astype(jnp.float32)
    back[:, D:] = jnp.where(
        high_lane, high, jnp.where(low_lane, summed - high, 0.0)
    ).astype(jnp.bfloat16)

    def inward(j, carry):
        columns = pl.ds(pl.multiple_of(j * WIDTH, WIDTH), WIDTH)
        value = jnp.dot(gate_out[...], w_gate[:, columns], preferred_element_type=jnp.float32)
        value += jnp.dot(up_out[...], w_up[:, columns], preferred_element_type=jnp.float32)
        back[:, columns] = value.astype(jnp.bfloat16)
        return carry

    lax.fori_loop(0, D // WIDTH, inward, 0)


def expert_rows(expert, x, g_y, blocks):
    slots = x.shape[0]
    total = HIDDEN * len(blocks)
    bf16 = jnp.bfloat16
    anywhere = pl.BlockSpec(memory_space=pl.ANY)
    vmem = pl.BlockSpec(memory_space=pltpu.VMEM)
    return pl.pallas_call(
        expert_kernel,
        out_shape=(jax.ShapeDtypeStruct(x.shape, bf16),)
        + (jax.ShapeDtypeStruct((slots, total), bf16),) * 3,
        in_specs=[pl.BlockSpec(memory_space=pltpu.SMEM)] + [anywhere] * (2 + len(blocks)),
        out_specs=(vmem,) * 4,
        scratch_shapes=[
            pltpu.VMEM(x.shape, bf16),
            pltpu.VMEM((slots, D), bf16),
            pltpu.VMEM((total, D), bf16),
            pltpu.VMEM((total, D), bf16),
            pltpu.VMEM((total, D), bf16),
            pltpu.SemaphoreType.DMA((2 + 3 * len(blocks),)),
        ],
        compiler_params=pltpu.CompilerParams(vmem_limit_bytes=VMEM_BYTES),
        cost_estimate=pl.CostEstimate(
            flops=10 * slots * total * D, bytes_accessed=28 << 20, transcendentals=slots * total
        ),
        name="expert_rows",
    )(expert, x, g_y, *blocks)


def expert_weights_kernel(*refs):
    x_ref, y_ref, gate_ref, up_ref, act_ref = refs[:5]
    blocks = refs[5:13]
    out, places = refs[13], refs[14:19]
    w_down, holds, sems = refs[19], refs[20:23], refs[23]
    total = gate_ref.shape[1]
    loads = []
    for i, block in enumerate(blocks):
        loads.append(
            pltpu.make_async_copy(
                block.at[pl.ds(2 * HIDDEN, HIDDEN)],
                w_down.at[pl.ds(i * HIDDEN, HIDDEN)],
                sems.at[i],
            )
        )
        loads[-1].start()
    copies = []
    for m, (left, right) in enumerate(((gate_ref, x_ref), (up_ref, x_ref), (act_ref, y_ref))):

        def hidden(start, width, carry):
            rows = pl.ds(start, width)
            holds[m][rows, :] = dot_tn(left[:, rows], right[:, :D]).astype(jnp.bfloat16)
            return carry

        hidden_loop(0, total // TILE, 0, hidden)
        if total % TILE:
            hidden(total // TILE * TILE, total % TILE, 0)
        for i in range(len(blocks)):
            first = m + 3 * max(i - RINGS, 0)
            place = places[min(i, RINGS)].at[pl.ds(first * HIDDEN, HIDDEN)]
            source = holds[m].at[pl.ds(i * HIDDEN, HIDDEN)]
            copies.append(
                pltpu.make_async_copy(source, place, sems.at[len(blocks) * (m + 1) + i])
            )
            copies[-1].start()
    for load in loads:
        load.wait()

    def outward(j, carry):
        columns = pl.ds(pl.multiple_of(j * WIDTH, WIDTH), WIDTH)
        value = jnp.dot(act_ref[...], w_down[:, columns], preferred_element_type=jnp.float32)
        out[:, columns] = value.astype(jnp.bfloat16)
        return carry

    lax.fori_loop(0, D // WIDTH, outward, 0)
    for copy in copies:
        copy.wait()


def expert_weights(x, g_y, gate, up, act, blocks):
    slots, total = gate.shape
    bf16 = jnp.bfloat16
    anywhere = pl.BlockSpec(memory_space=pl.ANY)
    vmem = pl.BlockSpec(memory_space=pltpu.VMEM)
    sizes = (3 * HIDDEN,) * RINGS + (3 * HIDDEN * RINGS,)
    return pl.pallas_call(
        expert_weights_kernel,
        out_shape=(jax.ShapeDtypeStruct((slots, D), bf16),)
        + tuple(jax.ShapeDtypeStruct((size, D), bf16) for size in sizes),
        in_specs=[vmem] * 5 + [anywhere] * len(blocks),
        out_specs=(vmem,) + (anywhere,) * 5,
        scratch_shapes=[pltpu.VMEM((total, D), bf16)] * 4
        + [pltpu.SemaphoreType.DMA((4 * len(blocks),))],
        compiler_params=pltpu.CompilerParams(vmem_limit_bytes=VMEM_BYTES),
        cost_estimate=pl.CostEstimate(
            flops=LONG, bytes_accessed=34 << 20, transcendentals=0
        ),
        name="expert_weights",
    )(x, g_y, gate, up, act, *blocks)


def shards(
    layer_input,
    attn_gain,
    w_query,
    w_kv_down,
    kv_gain,
    w_kv_up,
    w_out,
    ffn_gain,
    w_router,
    routes,
    expert_gate,
    expert_up_projection,
    expert_down,
    shared_gate,
    shared_up,
    shared_down,
    cotangent,
):
    length = layer_input.shape[0]
    rows = length // (RINGS * CORES)
    y, core = lax.axis_index("y"), lax.axis_index("core")
    qk_width = NOPE + ROPE
    heads_here = w_query.shape[1] // qk_width
    score_scale = qk_width ** (-0.5)
    experts_total = w_router.shape[1]
    first_core = core == 0
    second_expert = y >= RINGS // 2

    def block_of(expert):
        parts = (
            jnp.swapaxes(expert_gate, 1, 2),
            jnp.swapaxes(expert_up_projection, 1, 2),
            expert_down,
        )
        return jnp.concatenate(
            [lax.dynamic_index_in_dim(part, expert, 0, keepdims=False) for part in parts], axis=0
        )

    same = second_expert.astype(jnp.int32)
    same_block, other_block = block_of(same), block_of(1 - same)
    weights = [
        same_block,
        lax.ppermute(same_block, "y", PAIRS),
        lax.ppermute(other_block, "y", CROSS),
    ]

    places = jnp.arange(length, dtype=jnp.int32)
    own_start = (y * CORES + core) * rows
    cot_all = gather_rows(cotangent)
    cot_rows = cotangent.astype(jnp.float32)

    def own(table):
        return lax.dynamic_slice_in_dim(table, own_start, rows, 0)

    def parts_of(table):
        return by_core(table, first_core)

    expert_ids = jnp.arange(experts_total, dtype=jnp.int32)
    picked = jnp.zeros((length, experts_total), jnp.float32)
    for route in range(TOP):
        picked = picked + (routes[:, route : route + 1] == expert_ids[None, :]).astype(jnp.float32)
    earlier = (places[:, None] > places[None, :]).astype(jnp.bfloat16)
    before = matmul(earlier, picked.astype(jnp.bfloat16))
    share = 128 // RINGS
    quarter = (y % 2) * CORES + core
    slots = jnp.arange(RANKS * share, dtype=jnp.int32)
    expert_of_slot = (experts_total // RANKS) * (slots // share) + same
    spread = (expert_ids[:, None] == expert_of_slot[None, :]).astype(jnp.bfloat16)
    place_of = matmul((picked * (before + 1.0)).astype(jnp.bfloat16), spread)
    slot_number = (slots % share + share * quarter + 1).astype(jnp.float32)
    slot_map = (place_of == slot_number[None, :]).astype(jnp.bfloat16)
    slot_parts = parts_of(slot_map)
    g_y_sent = matmul_tn(slot_map, cot_all).astype(jnp.bfloat16)
    g_y = to_owners(g_y_sent)

    cos_table, sin_table = angles_of(places)
    input_full = layer_input.astype(jnp.float32)
    normed_full, factor_one = norm_forward(input_full, attn_gain)
    normed_a = normed_full.astype(jnp.bfloat16)
    query_raw = matmul(normed_a, w_query).reshape(length, heads_here, qk_width)
    query_turned = rotate(query_raw[..., NOPE:], cos_table[:, None, :], sin_table[:, None, :])
    query = jnp.concatenate([query_raw[..., :NOPE], query_turned], axis=-1).astype(jnp.bfloat16)
    compressed = matmul(normed_a, w_kv_down)
    latent_raw = compressed[:, :KV_RANK]
    latent_normed, factor_kv = norm_forward(latent_raw, kv_gain)
    latent = latent_normed.astype(jnp.bfloat16)
    key_rope = rotate(compressed[:, KV_RANK:], cos_table, sin_table).astype(jnp.bfloat16)
    key_value = (
        matmul(latent, w_kv_up).astype(jnp.bfloat16).reshape(length, heads_here, NOPE + VDIM)
    )
    key_nope = key_value[..., :NOPE]
    values_all = key_value[..., NOPE:]
    causal = places[:, None] >= places[None, :]

    def scores_of(query):
        scores = jnp.einsum(
            "qhd,khd->hqk", query[..., :NOPE], key_nope, preferred_element_type=jnp.float32
        )
        scores = scores + jnp.einsum(
            "qhd,kd->hqk", query[..., NOPE:], key_rope, preferred_element_type=jnp.float32
        )
        return jnp.where(causal[None], scores * score_scale, -1e30)

    scores = scores_of(query)
    top_score = jnp.max(scores, axis=-1, keepdims=True)
    powered = jnp.exp(scores - top_score)
    total = jnp.sum(powered, axis=-1, keepdims=True)
    probs = (powered / total).astype(jnp.bfloat16)
    log_totals = top_score + jnp.log(total)
    heads_out = (
        jnp.einsum("hqk,khd->qhd", probs, values_all, preferred_element_type=jnp.float32)
        .astype(jnp.bfloat16)
        .reshape(length, heads_here * VDIM)
    )
    attn_kept, attn_given = parts_of(matmul(heads_out, w_out).astype(jnp.bfloat16))
    attended = sum_rows_directly(after(attn_kept, g_y_sent, *weights[1:]), attn_given)
    residual = own(input_full) + attended
    normed_two, factor_two = norm_forward(residual, ffn_gain)
    normed_rows = normed_two.astype(jnp.bfloat16)
    normed_f = gather_rows(normed_rows)
    weights.append(lax.ppermute(after(other_block, normed_f), "y", OPPOSITE))

    sigmoid_all = jax.nn.sigmoid(matmul(normed_f, w_router))
    selected = sigmoid_all * picked
    sel_total = jnp.sum(selected, axis=-1, keepdims=True)
    gates = route_scale * selected / sel_total
    high, low = split_float(gates)
    gap = jnp.zeros((length, LOW - experts_total), jnp.bfloat16)
    sent = dispatch(slot_map, normed_f, jnp.concatenate([high, gap, low, gap], axis=1))
    arrived = to_owners(after(sent, g_y))

    core_index = core.reshape(1).astype(jnp.int32)
    *grads_shared, shared_act, kept_back, given_back = shared_experts(
        core_index,
        after(normed_f, sent),
        cot_all,
        jnp.swapaxes(shared_gate, 0, 1),
        jnp.swapaxes(shared_up, 0, 1),
        shared_down,
    )

    shared_back = (kept_back, given_back)

    arrived = after(arrived, *shared_back)
    last = after(weights[-1], arrived)
    weights = weights + [lax.ppermute(w, "core", SWAP) for w in (*weights[:-1], last)]
    expert_here = 2 * lax.axis_index("x") * 4 + 2 * lax.axis_index("z") + same
    back, g_gate, g_up, act = expert_rows(
        expert_here.reshape(1).astype(jnp.int32), arrived, g_y, weights
    )
    out, *block_grads = expert_weights(
        arrived, g_y, g_gate, g_up, act, weights
    )
    back = after(to_owners(back), *block_grads)

    taken_grads = lax.ppermute(block_grads[RINGS], "core", SWAP)
    taken_grads = [taken_grads[3 * HIDDEN * r : 3 * HIDDEN * (r + 1)] for r in range(RINGS)]
    grads_sent = [
        (mine.astype(jnp.float32) + taken.astype(jnp.float32)).astype(jnp.bfloat16)
        for mine, taken in zip(block_grads[1:RINGS], taken_grads[1:])
    ]

    summed = sum_rows_directly(
        *(
            matmul(a, back) + jnp.pad(b, ((0, 0), (0, 128)))
            for a, b in zip(slot_parts, shared_back)
        )
    )
    g_gate_rows = summed[:, D : D + experts_total] + summed[:, D + LOW : D + LOW + experts_total]

    sigma_rows, picked_rows, total_rows = own(sigmoid_all), own(picked), own(sel_total)
    sel_rows = sigma_rows * picked_rows
    grad_sel = route_scale * (
        g_gate_rows / total_rows
        - jnp.sum(g_gate_rows * sel_rows, axis=-1, keepdims=True) / (total_rows * total_rows)
    )
    grad_logits = (grad_sel * picked_rows * sigma_rows * (1.0 - sigma_rows)).astype(jnp.bfloat16)
    grad_w_router = matmul_tn(grad_logits, normed_rows)
    grad_normed = summed[:, :D] + matmul_nt(grad_logits, w_router)
    grad_from_norm, grad_ffn_gain = norm_backward(residual, factor_two, ffn_gain, grad_normed)
    grad_residual = cot_rows + grad_from_norm
    grad_residual_low = grad_residual.astype(jnp.bfloat16)
    grad_attended = gather_rows(grad_residual_low)
    returned = to_owners(after(out, grad_residual_low))

    grad_attended, *grads_sent = lax.optimization_barrier((grad_attended, *grads_sent))
    grads_got = [lax.ppermute(g, "y", pairs) for g, pairs in zip(grads_sent, (PAIRS, CROSS))]
    grad_w_out = matmul_tn(heads_out, grad_attended).astype(jnp.bfloat16)

    grad_heads = (
        matmul_nt(grad_attended, w_out).astype(jnp.bfloat16).reshape(length, heads_here, VDIM)
    )
    probs_full = jnp.exp(scores_of(query) - log_totals)
    grad_probs = jnp.einsum(
        "qhd,khd->hqk", grad_heads, values_all, preferred_element_type=jnp.float32
    )
    grad_scores = (
        probs_full * (grad_probs - jnp.sum(grad_probs * probs_full, axis=-1, keepdims=True))
    ).astype(jnp.bfloat16)
    grad_query_nope = (
        jnp.einsum("hqk,khd->qhd", grad_scores, key_nope, preferred_element_type=jnp.float32)
        * score_scale
    )
    grad_query_rope = (
        jnp.einsum("hqk,kd->qhd", grad_scores, key_rope, preferred_element_type=jnp.float32)
        * score_scale
    )
    grad_key_nope = (
        jnp.einsum(
            "hqk,qhd->khd", grad_scores, query[..., :NOPE], preferred_element_type=jnp.float32
        )
        * score_scale
    )
    grad_key_rope = (
        jnp.einsum(
            "hqk,qhd->kd", grad_scores, query[..., NOPE:], preferred_element_type=jnp.float32
        )
        * score_scale
    )
    grad_values = jnp.einsum(
        "hqk,qhd->khd",
        probs_full.astype(jnp.bfloat16),
        grad_heads,
        preferred_element_type=jnp.float32,
    )
    grad_query_back = rotate_back(
        grad_query_rope, cos_table[:, None, :], sin_table[:, None, :]
    )
    grad_query = (
        jnp.concatenate([grad_query_nope, grad_query_back], axis=-1)
        .astype(jnp.bfloat16)
        .reshape(length, heads_here * qk_width)
    )
    returned = after(returned, grad_query)
    act_parts = parts_of(shared_act)
    routed_and_shared = sum_rows_directly(
        *(matmul(a, returned) + matmul(b, shared_down) for a, b in zip(slot_parts, act_parts))
    )
    output = (residual + routed_and_shared).astype(jnp.bfloat16)
    grad_w_query = matmul_tn(normed_a, grad_query).astype(jnp.bfloat16)
    grad_key_value = (
        jnp.concatenate([grad_key_nope, grad_values], axis=-1)
        .astype(jnp.bfloat16)
        .reshape(length, heads_here * (NOPE + VDIM))
    )
    grad_w_kv_up = matmul_tn(latent, grad_key_value).astype(jnp.bfloat16)
    grad_latent_normed = matmul_nt(grad_key_value, w_kv_up)
    grad_latent, grad_kv_gain = norm_backward(latent_raw, factor_kv, kv_gain, grad_latent_normed)
    grad_rope_part = rotate_back(grad_key_rope, cos_table, sin_table)
    grad_compressed = jnp.concatenate([grad_latent, grad_rope_part], axis=-1).astype(jnp.bfloat16)
    local_grads = (grad_w_out, grad_w_query, grad_w_kv_up, *grads_shared)
    grad_w_out, grad_w_query, grad_w_kv_up, *grads_shared = lax.psum(local_grads, EXPERT)
    kept, given, grad_attn_gain = attention_rows(
        core_index,
        grad_query,
        grad_compressed,
        layer_input,
        factor_one,
        w_query,
        jnp.swapaxes(w_kv_down, 0, 1),
    )

    parts = RINGS * CORES
    kv_share = grad_compressed.shape[1] // parts
    columns = D // parts
    gains = jnp.concatenate(
        [
            grad_attn_gain.reshape(parts, columns),
            grad_ffn_gain.reshape(parts, columns),
            grad_kv_gain.reshape(parts, KV_RANK // parts),
        ],
        axis=1,
    )
    gains = jnp.pad(gains, ((0, 0), (0, 16 * length // 2 - gains.shape[1])))
    bundle = jnp.concatenate(
        [
            jnp.swapaxes(grad_compressed, 0, 1).reshape(parts, kv_share, length),
            jnp.swapaxes(grad_w_router.reshape(experts_total, parts, columns), 0, 1)
            .reshape(parts, experts_total * columns // length, length)
            .astype(jnp.bfloat16),
            gains.reshape(parts, 8, length).astype(jnp.bfloat16),
        ],
        axis=1,
    )
    bundle = after(bundle, returned, *local_grads)
    bundle = jnp.sum(
        lax.all_to_all(bundle, GROUP, 0, 0, tiled=True).astype(jnp.float32), axis=0
    ).astype(jnp.bfloat16)
    grads_got.append(lax.ppermute(after(grads_sent[2], bundle), "y", OPPOSITE))
    grad_normed_one = sum_rows_directly(kept, given)
    grad_from_first, _ = norm_backward(
        own(input_full), own(factor_one), attn_gain, grad_normed_one
    )
    grad_input = grad_residual + grad_from_first
    kv_slice = kv_product(bundle[:kv_share], normed_a)
    other_rows = bundle[kv_share:].reshape(-1, D)
    replicated = jnp.concatenate(
        [kv_slice, other_rows, jnp.zeros((80 - kv_share - other_rows.shape[0], D), jnp.bfloat16)],
        axis=0,
    )
    replicated = jnp.swapaxes(replicated.reshape(80, RANKS, D // RANKS), 0, 1)
    replicated = sum_ranks(replicated)
    def by_expert(m):
        part = slice(m * HIDDEN, (m + 1) * HIDDEN)
        ours = block_grads[0][part].astype(jnp.float32) + taken_grads[0][part].astype(jnp.float32)
        ours = ours + grads_got[0][part].astype(jnp.float32)
        others = grads_got[1][part].astype(jnp.float32) + grads_got[2][part].astype(jnp.float32)
        return jnp.stack(
            [jnp.where(second_expert, others, ours), jnp.where(second_expert, ours, others)]
        )

    expert_grads = [by_expert(m) for m in range(3)]
    replicated = gather_rows_directly(replicated.reshape(RANKS * 80, D // RANKS), first_core)
    replicated = replicated.reshape(parts, RANKS, 80, D // RANKS)
    replicated = jnp.swapaxes(replicated, 1, 2).reshape(parts, 80, D).astype(jnp.float32)
    grad_w_kv_down = jnp.swapaxes(replicated[:, :kv_share].reshape(-1, D), 0, 1)
    others = replicated[:, kv_share:]
    router_rows = experts_total * columns // D
    grad_w_router = (
        jnp.swapaxes(others[:, :router_rows].reshape(parts, experts_total, columns), 0, 1)
        .reshape(experts_total, D)
        .T
    )
    gains = others[:, router_rows]
    grad_attn_gain = gains[:, :columns].reshape(D)
    grad_ffn_gain = gains[:, columns : 2 * columns].reshape(D)
    grad_kv_gain = gains[:, 2 * columns : 2 * columns + KV_RANK // parts].reshape(KV_RANK)
    grads_shared = [grad.astype(jnp.float32) for grad in grads_shared]
    return (
        output,
        grad_input,
        grad_attn_gain,
        grad_w_query.astype(jnp.float32),
        grad_w_kv_down,
        grad_kv_gain,
        grad_w_kv_up.astype(jnp.float32),
        grad_w_out.astype(jnp.float32),
        grad_ffn_gain,
        grad_w_router,
        jnp.swapaxes(expert_grads[0], 1, 2),
        jnp.swapaxes(expert_grads[1], 1, 2),
        expert_grads[2],
        grads_shared[0].T,
        grads_shared[1].T,
        grads_shared[2],
    )


def solution(mesh):
    split = Mesh(mesh.devices.reshape(4, 4, RINGS, CORES), ("x", "z", "y", "core"))
    return jax.shard_map(
        shards,
        mesh=split,
        in_specs=(
            P(EXPERT, None),
            P(),
            P(None, GROUP),
            P(),
            P(),
            P(None, GROUP),
            P(GROUP, None),
            P(),
            P(),
            P(EXPERT, None),
            P(EXPERT, None, GROUP),
            P(EXPERT, None, GROUP),
            P(EXPERT, GROUP, None),
            P(None, GROUP),
            P(None, GROUP),
            P(GROUP, None),
            P(("x", "z", "y", "core"), None),
        ),
        out_specs=(
            P(("x", "z", "y", "core"), None),
            P(("x", "z", "y", "core"), None),
            P(),
            P(None, GROUP),
            P(),
            P(),
            P(None, GROUP),
            P(GROUP, None),
            P(),
            P(),
            P(EXPERT, None, GROUP),
            P(EXPERT, None, GROUP),
            P(EXPERT, GROUP, None),
            P(None, GROUP),
            P(None, GROUP),
            P(GROUP, None),
        ),
        check_vma=False,
    )
```

time: 1480 us -> 539 us (0.36)
  waiting for transfers between devices: 591 us -> 198 us
  local copies, waits for them, and re-layouts: 335 us -> 29.1 us
  matrix products: 176 us -> 42 us
  blocking collectives: 129 us -> 0 us
  other arithmetic: 201 us -> 79.6 us
  Pallas kernels: 0 us -> 79.2 us
  starting transfers between devices: 25.4 us -> 82 us
    psum x2 -> x1, waiting for transfers between devices: 246 us -> 0.01 us  [shards(): lax.psum(local_grads, EXPERT)]
    gather x12 -> x0, local copies, waits for them, and re-layouts: 149 us -> none  [the longest x6 75 us: shards(): fetched = returned[target_rows[:, route]]]
    ppermute x0 -> x28, waiting for transfers between devices: none -> 131 us  [the longest x12 101 us: sum_rows_directly(): total = total + lax.ppermute(tile, 'y', pairs).astype(jnp.float32)]
    all_to_all x4 -> x0, blocking collectives: 129 us -> none  [the longest x2 64.7 us: return_summed(): lax.all_to_all(summed.astype(jnp.bfloat16), 'expert', split_axis=0, conca...]
    scatter x6 -> x0, other arithmetic: 117 us -> none  [shards(): grad_buffer.at[target[:, route]]]
    reduce_scatter x3 -> x0, waiting for transfers between devices: 114 us -> none  [the longest x2 114 us: return_summed(): lax.psum_scatter(partial_value.astype(jnp.float32).astype(jnp.bfloat16),...]
    scatter x6 -> x0, local copies, waits for them, and re-layouts: 113 us -> none  [shards(): send_buffer = send_buffer.at[target[:, route]].set(normed_f)]
    dot_general x11 -> x2, matrix products: 114 us -> 1.19 us  [the longest x1 0.73 us: scores_of(): jnp.einsum('qhd,kd->hqk', query[..., NOPE:], key_rope, preferred_element_...]
  transfers between devices with their start and end apart: 14 -> 40, of which waited for: 11 -> 21; matrix products, arithmetic and copies ran while one was open for 23% -> 24% of each run, Pallas kernels for 0% -> 10%
where the time goes in v1:
time: 539 us; the launch traced here: 531 us
  waiting for transfers between devices  198 us (37%)
  starting transfers between devices  82 us (15%)
  other arithmetic  79.6 us (15%)
  Pallas kernels  79.2 us (15%)
  matrix products  42 us (8%)
  local copies, waits for them, and re-layouts  29.1 us (5%)
  between operations  21.2 us (4%)
    ppermute x12, waiting for transfers between devices, sum_rows_directly(): total = total + lax.ppermute(tile, 'y', pairs).astype(jnp.float32)  101 us
    all_gather x3, waiting for transfers between devices, gather_rows(): return lax.all_gather(x, GROUP, axis=0, tiled=True)  32.3 us
    all_to_all x4, starting transfers between devices, to_owners(): lax.all_to_all(x.reshape(RANKS, x.shape[0] // RANKS, x.shape[1]), EXPERT,...  25.7 us
    pallas_call x1, Pallas kernels, expert_rows(): pl.pallas_call(expert_kernel, out_shape=(jax.ShapeDtypeStruct(x.shape, bf...  25.5 us
    pallas_call x1, Pallas kernels, expert_weights(): pl.pallas_call(expert_weights_kernel, out_shape=(jax.ShapeDtypeStruct((sl...  21.7 us
    all_to_all x4, waiting for transfers between devices, to_owners(): lax.all_to_all(x.reshape(RANKS, x.shape[0] // RANKS, x.shape[1]), EXPERT,...  20.6 us
    dot_general x12, matrix products, matmul(): return jnp.dot(left, right, preferred_element_type=jnp.float32)  20.2 us
    ppermute x1, waiting for transfers between devices, shards(): lax.ppermute(same_block, 'y', PAIRS)  19.2 us
  transfers between devices with their start and end apart: 40, of which 21 were waited for; matrix products, arithmetic and copies ran while one was open for 24% of the time, Pallas kernels for 10%

profile of v1, /device:TPU:1, one launch (start us, length us, event | category | flops | bytes accessed | tf_op | source)
XLA Modules:
  0.0 530.6 jit_solution(12259325646046700719)
XLA Ops:
  45.4 4.3 convolution_convert_fusion.1
  49.7 19.2 %collective-permute-done.refs_4_.refs_6_ = bf16[528,2048]{1,0:T(8,128)(2,1)} collective-permute-done((bf16[528,2048]{1,0:T(8,128)(2,1)}, bf16[528,2048]{1,0:T(8,128)(2,1)}, u32[]{:S(2)}, u32[]{:S(2)}) %collective-permute-start) | collective-permute-done | bytes 2162720 | tf_op jit(solution)/shard_map/ppermute | solution.py:551
  68.9 3.9 collective-permute-done.1.refs_5_.refs_7_
  84.0 6.0 %collective-permute-done.5 = bf16[64,2048]{1,0:T(8,128)(2,1)} collective-permute-done((bf16[64,2048]{1,0:T(8,128)(2,1)}, bf16[64,2048]{1,0:T(8,128)(2,1)}, u32[]{:S(2)}, u32[]{:S(2)}) %collective-permute-start.5) | collective-permute-done | bytes 262176 | tf_op jit(solution)/shard_map/ppermute | solution.py:69
  93.2 7.7 %all-to-all-start = ((bf16[16,32,2048]{2,1,0:T(8,128)(2,1)}), bf16[16,32,2048]{2,1,0:T(8,128)(2,1)S(1)}, u32[]{:S(2)}, u32[]{:S(2)}) async-start(bf16[16,32,2048]{2,1,0:T(8,128)(2,1)} %bitcast.286), calls=%async_computation | async-start | bytes 4194304 | tf_op jit(solution)/shard_map/all_to_all | solution.py:152
  101.0 21.1 %all-gather.6.cloned.1.call-done.rows_ref = bf16[512,2048]{1,0:T(8,128)(2,1)} async-done(((bf16[64,2048]{1,0:T(8,128)(2,1)}), bf16[512,2048]{1,0:T(8,128)(2,1)}) %all-gather.6.cloned.1.call-update) | async-done | bytes 2097168 | tf_op jit(solution)/shard_map/all_gather | solution.py:35
  128.3 5.3 dispatch.1
  134.9 6.7 %all-to-all-start.1 = ((bf16[16,32,2176]{2,1,0:T(8,128)(2,1)}), bf16[16,32,2176]{2,1,0:T(8,128)(2,1)S(1)}, u32[]{:S(2)}, u32[]{:S(2)}) async-start(bf16[16,32,2176]{2,1,0:T(8,128)(2,1)} %bitcast.253), calls=%async_computation.1 | async-start | bytes 4456448 | tf_op jit(solution)/shard_map/all_to_all | solution.py:152
  143.0 15.8 %shared_experts.1 = (bf16[352,2048]{1,0:T(8,128)(2,1)}, bf16[352,2048]{1,0:T(8,128)(2,1)}, bf16[352,2048]{1,0:T(8,128)(2,1)}, bf16[512,352]{1,0:T(8,128)(2,1)}, ...) custom-call(s32[1]{0:T(128)} %bitcast.39.core, bf16[512,2048]{1,0:T(8,128)(2,1)} %all-gather.6.cloned.1.call-done.rows_ref, ...), custom_call_target="tpu_custom_call" | custom-call | flops 17999998976 | bytes 20971520 | tf_op jit(solution)/shard_map/shared_experts/pallas_call | solution.py:265
  158.7 13.2 %all-to-all-done.1 = bf16[16,32,2176]{2,1,0:T(8,128)(2,1)S(1)} async-done(((bf16[16,32,2176]{2,1,0:T(8,128)(2,1)}), bf16[16,32,2176]{2,1,0:T(8,128)(2,1)S(1)}, u32[]{:S(2)}, u32[]{:S(2)}) %all-to-all-start.1) | async-done | bytes 2228256 | tf_op jit(solution)/shard_map/all_to_all | solution.py:152
  174.8 4.2 collective-permute-done.10.refs_10_.refs_12_
  179.0 25.5 %expert_rows.1 = (bf16[512,2176]{1,0:T(8,128)(2,1)}, bf16[512,1408]{1,0:T(8,128)(2,1)}, bf16[512,1408]{1,0:T(8,128)(2,1)}, bf16[512,1408]{1,0:T(8,128)(2,1)}) custom-call(s32[1]{0:T(128)} %bitcast.42.refs_0_, bf16[512,2176]{1,0:T(8,128)(2,1)} %bitcast.276, bf16[512,2048]{1,0:T(8,128)(2,1)} %bitcast.284, bf16[528,2048]{1,0:T(8,128)(2,1)} %pad_maximum_fusion.2.refs_3_.refs_5_, ...), custom_call_target="tpu_custom_call" | custom-call | flops 14763950080 | bytes 29360128 | tf_op jit(solution)/shard_map/expert_rows/pallas_call | solution.py:415
  204.5 5.3 %all-to-all-start.2 = ((bf16[16,32,2176]{2,1,0:T(8,128)(2,1)}), bf16[16,32,2176]{2,1,0:T(8,128)(2,1)S(1)}, u32[]{:S(2)}, u32[]{:S(2)}) async-start(bf16[16,32,2176]{2,1,0:T(8,128)(2,1)} %bitcast.278), calls=%async_computation.2 | async-start | bytes 4456448 | tf_op jit(solution)/shard_map/all_to_all | solution.py:152
  209.9 21.7 %expert_weights.1 = (bf16[512,2048]{1,0:T(8,128)(2,1)}, bf16[528,2048]{1,0:T(8,128)(2,1)}, bf16[528,2048]{1,0:T(8,128)(2,1)}, bf16[528,2048]{1,0:T(8,128)(2,1)},...) custom-call(bf16[512,2176]{1,0:T(8,128)(2,1)} %bitcast.277, bf16[512,2048]{1,0:T(8,128)(2,1)} %bitcast.285, ...), custom_call_target="tpu_custom_call" | custom-call | flops 99999997952 | bytes 35651584 | tf_op jit(solution)/shard_map/expert_weights/pallas_call | solution.py:492
  233.1 7.4 %all-to-all-done.2 = bf16[16,32,2176]{2,1,0:T(8,128)(2,1)S(1)} async-done(((bf16[16,32,2176]{2,1,0:T(8,128)(2,1)}), bf16[16,32,2176]{2,1,0:T(8,128)(2,1)S(1)}, u32[]{:S(2)}, u32[]{:S(2)}) %all-to-all-start.2) | async-done | bytes 2228256 | tf_op jit(solution)/shard_map/all_to_all | solution.py:152
  252.6 4.4 collective-permute-done.12
  258.4 5.3 %collective-permute-done.14 = bf16[64,2176]{1,0:T(8,128)(2,1)S(1)} collective-permute-done((bf16[64,2176]{1,0:T(8,128)(2,1)S(1)}, bf16[64,2176]{1,0:T(8,128)(2,1)S(1)}, u32[]{:S(2)}, u32[]{:S(2)}) %collective-permute-start.14) | collective-permute-done | bytes 278560 | tf_op jit(solution)/shard_map/ppermute | solution.py:69
  269.8 6.0 %all-to-all-start.3 = ((bf16[16,32,2048]{2,1,0:T(8,128)(2,1)}), bf16[16,32,2048]{2,1,0:T(8,128)(2,1)S(1)}, u32[]{:S(2)}, u32[]{:S(2)}) async-start(bf16[16,32,2048]{2,1,0:T(8,128)(2,1)} %bitcast.283), calls=%async_computation.3 | async-start | bytes 4194304 | tf_op jit(solution)/shard_map/all_to_all | solution.py:152
  275.8 8.4 %add_convert_fusion = (bf16[528,2048]{1,0:T(8,128)(2,1)}, bf16[528,2048]{1,0:T(8,128)(2,1)}, bf16[528,2048]{1,0:T(8,128)(2,1)}) fusion(bf16[528,2048]{1,0:T(8,128)(2,1)} %get-tuple-element.66, bf16[2112,2048]{1,0:T(8,128)(2,1)} %collective-permute-done.15, bf16[528,2048]{1,0:T(8,128)(2,1)} %get-tuple-element.65, bf16[528,2048]{1,0:T(8,128)(2,1)} %get-tuple-element.64), kind=kLoop, calls=%fused_computation.2 | loop fusion | flops 12976128 | bytes 19464192 | tf_op jit(solution)/shard_map/convert_element_type | solution.py:667
  284.3 9.7 %all-gather.8.cloned.1.call-done = bf16[512,2048]{1,0:T(8,128)(2,1)} async-done(((bf16[64,2048]{1,0:T(8,128)(2,1)}), bf16[512,2048]{1,0:T(8,128)(2,1)}) %all-gather.8.cloned.1.call-update) | async-done | bytes 2097168 | tf_op jit(solution)/shard_map/all_gather | solution.py:35
  311.5 8.2 %attention_rows.1 = (bf16[256,2048]{1,0:T(8,128)(2,1)}, bf16[256,2048]{1,0:T(8,128)(2,1)}, f32[1,2048]{1,0:T(1,128)}) custom-call(s32[1]{0:T(128)} %bitcast.39.core, bf16[512,384]{1,0:T(8,128)(2,1)} %copy.185.query_ref, bf16[512,576]{1,0:T(8,128)(2,1)} %pad_maximum_fusion.5.compressed_ref, bf16[512,2048]{1,0:T(8,128)(2,1)} %x_ref.1, ...), custom_call_target="tpu_custom_call" | custom-call | flops 99999997952 | bytes 10485760 | tf_op jit(solution)/shard_map/attention_rows/pallas_call | solution.py:330
  333.6 3.7 all-to-all-start.4
  345.6 4.0 all-to-all-done.4
  355.3 6.6 %all-to-all-start.5 = ((bf16[16,80,128]{2,1,0:T(8,128)(2,1)}), bf16[16,80,128]{2,1,0:T(8,128)(2,1)S(1)}, u32[]{:S(2)}, u32[]{:S(2)}) async-start(bf16[16,80,128]{2,1,0:T(8,128)(2,1)} %maximum_bitcast_fusion.2), calls=%async_computation.5 | async-start | bytes 655360 | tf_op jit(solution)/shard_map/all_to_all | solution.py:78
  364.2 8.4 %all-to-all-done.5 = bf16[16,80,128]{2,1,0:T(8,128)(2,1)S(1)} async-done(((bf16[16,80,128]{2,1,0:T(8,128)(2,1)}), bf16[16,80,128]{2,1,0:T(8,128)(2,1)S(1)}, u32[]{:S(2)}, u32[]{:S(2)}) %all-to-all-start.5) | async-done | bytes 327712 | tf_op jit(solution)/shard_map/all_to_all | solution.py:78
  373.4 5.3 %all-to-all-start.6 = ((bf16[16,80,128]{2,1,0:T(8,128)(2,1)}), bf16[16,80,128]{2,1,0:T(8,128)(2,1)S(1)}, u32[]{:S(2)}, u32[]{:S(2)}) async-start(bf16[16,80,128]{2,1,0:T(8,128)(2,1)} %broadcast_in_dim.26), calls=%async_computation.6 | async-start | bytes 655360 | tf_op jit(solution)/shard_map/all_to_all | solution.py:80
  385.8 60.6 %collective-permute-done.21 = bf16[64,2048]{1,0:T(8,128)(2,1)S(1)} collective-permute-done((bf16[64,2048]{1,0:T(8,128)(2,1)S(1)}, bf16[64,2048]{1,0:T(8,128)(2,1)S(1)}, u32[]{:S(2)}, u32[]{:S(2)}) %collective-permute-start.21) | collective-permute-done | bytes 262176 | tf_op jit(solution)/shard_map/ppermute | solution.py:69
  450.9 4.5 all-to-all-start.7
  463.2 19.8 %collective-permute-done.18 = bf16[64,2048]{1,0:T(8,128)(2,1)S(1)} collective-permute-done((bf16[64,2048]{1,0:T(8,128)(2,1)}, bf16[64,2048]{1,0:T(8,128)(2,1)S(1)}, u32[]{:S(2)}, u32[]{:S(2)}) %collective-permute-start.18) | collective-permute-done | bytes 262176 | tf_op jit(solution)/shard_map/ppermute | solution.py:69
  489.4 4.4 select_bitcast_fusion
  493.8 4.4 select_bitcast_fusion.1
  512.1 3.4 convert_element_type.464
  (386 shorter events, 175.0 us)
Async XLA Ops:
  7.2 38.2 %all-gather.4.cloned.1.call-start = ((), (), s32[]{:S(2)}) async-start(), calls=%async_computation.8 | async-start | bytes 2359296 | tf_op jit(solution)/shard_map/all_gather | solution.py:35
  7.9 114.1 %all-gather.6.cloned.1.call-start = ((), (), s32[]{:S(2)}) async-start(), calls=%async_computation.9 | async-start | bytes 2359296 | tf_op jit(solution)/shard_map/all_gather | solution.py:35
  11.7 57.2 %collective-permute-start = (bf16[528,2048]{1,0:T(8,128)(2,1)}, bf16[528,2048]{1,0:T(8,128)(2,1)}, u32[]{:S(2)}, u32[]{:S(2)}) collective-permute-start(bf16[528,2048]{1,0:T(8,128)(2,1)} %pad_maximum_fusion.2.refs_3_.refs_5_), channel_id=1, source_target_pairs={{0,2},{2,0},{4,6},{6,4},{1,3},{3,1},{5,7},{7,5},{8,10},{10,8},{12,... | collective-permute-start | bytes 6488072 | tf_op jit(solution)/shard_map/ppermute | solution.py:551
  15.3 57.5 %collective-permute-start.1 = (bf16[528,2048]{1,0:T(8,128)(2,1)}, bf16[528,2048]{1,0:T(8,128)(2,1)}, u32[]{:S(2)}, u32[]{:S(2)}) collective-permute-start(bf16[528,2048]{1,0:T(8,128)(2,1)} %pad_maximum_fusion.3), channel_id=1, source_target_pairs={{2,4},{4,2},{6,0},{0,6},{3,5},{5,3},{7,1},{1,7},{10,12},{12,10},{1... | collective-permute-start | bytes 6488072 | tf_op jit(solution)/shard_map/ppermute | solution.py:552
  32.6 40.3 %collective-permute-start.2 = (bf16[256,2048]{1,0:T(8,128)(2,1)}, bf16[256,2048]{1,0:T(8,128)(2,1)}, u32[]{:S(2)}, u32[]{:S(2)}) collective-permute-start(bf16[256,2048]{1,0:T(8,128)(2,1)} %bitcast.24), channel_id=1, source_target_pairs={{0,1},{1,0},{2,3},{3,2},{4,5},{5,4},{6,7},{7,6},{8,9},{9,8},{10,11... | collective-permute-start | bytes 3145736 | tf_op jit(solution)/shard_map/ppermute | solution.py:61
  78.4 11.6 %collective-permute-start.5 = (bf16[64,2048]{1,0:T(8,128)(2,1)}, bf16[64,2048]{1,0:T(8,128)(2,1)}, u32[]{:S(2)}, u32[]{:S(2)}) collective-permute-start(bf16[64,2048]{1,0:T(8,128)(2,1)} %get-tuple-element.135), channel_id=1, source_target_pairs={{0,4},{4,0},{2,6},{6,2},{1,5},{5,1},{3,7},{7,3},{8,12},{12,8},{10,... | collective-permute-start | bytes 786440 | tf_op jit(solution)/shard_map/ppermute | solution.py:69
  93.2 40.3 %all-to-all-start = ((bf16[16,32,2048]{2,1,0:T(8,128)(2,1)}), bf16[16,32,2048]{2,1,0:T(8,128)(2,1)S(1)}, u32[]{:S(2)}, u32[]{:S(2)}) async-start(bf16[16,32,2048]{2,1,0:T(8,128)(2,1)} %bitcast.286), calls=%async_computation | async-start | bytes 4194304 | tf_op jit(solution)/shard_map/all_to_all | solution.py:152
  122.1 50.2 %collective-permute-start.6 = (bf16[528,2048]{1,0:T(8,128)(2,1)}, bf16[528,2048]{1,0:T(8,128)(2,1)}, u32[]{:S(2)}, u32[]{:S(2)}) collective-permute-start(bf16[528,2048]{1,0:T(8,128)(2,1)} %pad_maximum_fusion.3), channel_id=1, source_target_pairs={{0,4},{4,0},{2,6},{6,2},{1,5},{5,1},{3,7},{7,3},{8,12},{12,8},{10,... | collective-permute-start | bytes 6488072 | tf_op jit(solution)/shard_map/ppermute | solution.py:629
  134.9 37.1 %all-to-all-start.1 = ((bf16[16,32,2176]{2,1,0:T(8,128)(2,1)}), bf16[16,32,2176]{2,1,0:T(8,128)(2,1)S(1)}, u32[]{:S(2)}, u32[]{:S(2)}) async-start(bf16[16,32,2176]{2,1,0:T(8,128)(2,1)} %bitcast.253), calls=%async_computation.1 | async-start | bytes 4456448 | tf_op jit(solution)/shard_map/all_to_all | solution.py:152
  141.5 33.3 %collective-permute-start.7 = (bf16[528,2048]{1,0:T(8,128)(2,1)}, bf16[528,2048]{1,0:T(8,128)(2,1)}, u32[]{:S(2)}, u32[]{:S(2)}) collective-permute-start(bf16[528,2048]{1,0:T(8,128)(2,1)} %pad_maximum_fusion.2.refs_3_.refs_5_), channel_id=1, source_target_pairs={{0,1},{1,0},{2,3},{3,2},{4,5},{5,4},{6,7},{7,6},{8,9},{9,8},{10,11... | collective-permute-start | bytes 6488072 | tf_op jit(solution)/shard_map/ppermute | solution.py:654
  142.5 32.3 %collective-permute-start.8 = (bf16[528,2048]{1,0:T(8,128)(2,1)}, bf16[528,2048]{1,0:T(8,128)(2,1)}, u32[]{:S(2)}, u32[]{:S(2)}) collective-permute-start(bf16[528,2048]{1,0:T(8,128)(2,1)} %collective-permute-done.refs_4_.refs_6_), channel_id=1, source_target_pairs={{0,1},{1,0},{2,3},{3,2},{4,5},{5,4},{6,7},{7,6},{8,9},{9,8},{10,11... | collective-permute-start | bytes 6488072 | tf_op jit(solution)/shard_map/ppermute | solution.py:654
  142.5 32.2 %collective-permute-start.9 = (bf16[528,2048]{1,0:T(8,128)(2,1)}, bf16[528,2048]{1,0:T(8,128)(2,1)}, u32[]{:S(2)}, u32[]{:S(2)}) collective-permute-start(bf16[528,2048]{1,0:T(8,128)(2,1)} %collective-permute-done.1.refs_5_.refs_7_), channel_id=1, source_target_pairs={{0,1},{1,0},{2,3},{3,2},{4,5},{5,4},{6,7},{7,6},{8,9},{9,8},{10,11... | collective-permute-start | bytes 6488072 | tf_op jit(solution)/shard_map/ppermute | solution.py:654
  204.5 36.0 %all-to-all-start.2 = ((bf16[16,32,2176]{2,1,0:T(8,128)(2,1)}), bf16[16,32,2176]{2,1,0:T(8,128)(2,1)S(1)}, u32[]{:S(2)}, u32[]{:S(2)}) async-start(bf16[16,32,2176]{2,1,0:T(8,128)(2,1)} %bitcast.278), calls=%async_computation.2 | async-start | bytes 4456448 | tf_op jit(solution)/shard_map/all_to_all | solution.py:152
  209.8 84.1 %all-gather.8.cloned.1.call-start = ((), (), s32[]{:S(2)}) async-start(), calls=%async_computation.10 | async-start | bytes 2359296 | tf_op jit(solution)/shard_map/all_gather | solution.py:35
  231.6 44.2 %collective-permute-start.15 = (bf16[2112,2048]{1,0:T(8,128)(2,1)}, bf16[2112,2048]{1,0:T(8,128)(2,1)}, u32[]{:S(2)}, u32[]{:S(2)}) collective-permute-start(bf16[2112,2048]{1,0:T(8,128)(2,1)} %get-tuple-element.67), channel_id=1, source_target_pairs={{0,1},{1,0},{2,3},{3,2},{4,5},{5,4},{6,7},{7,6},{8,9},{9,8},{10,11... | collective-permute-start | bytes 25952264 | tf_op jit(solution)/shard_map/ppermute | solution.py:664
  251.2 12.6 %collective-permute-start.14 = (bf16[64,2176]{1,0:T(8,128)(2,1)S(1)}, bf16[64,2176]{1,0:T(8,128)(2,1)S(1)}, u32[]{:S(2)}, u32[]{:S(2)}) collective-permute-start(bf16[64,2176]{1,0:T(8,128)(2,1)S(1)} %get-tuple-element.126), channel_id=1, source_target_pairs={{0,4},{4,0},{2,6},{6,2},{1,5},{5,1},{3,7},{7,3},{8,12},{12,8},{10,... | collective-permute-start | bytes 835592 | tf_op jit(solution)/shard_map/ppermute | solution.py:69
  269.8 62.8 %all-to-all-start.3 = ((bf16[16,32,2048]{2,1,0:T(8,128)(2,1)}), bf16[16,32,2048]{2,1,0:T(8,128)(2,1)S(1)}, u32[]{:S(2)}, u32[]{:S(2)}) async-start(bf16[16,32,2048]{2,1,0:T(8,128)(2,1)} %bitcast.283), calls=%async_computation.3 | async-start | bytes 4194304 | tf_op jit(solution)/shard_map/all_to_all | solution.py:152
  333.6 16.0 %all-to-all-start.4 = ((bf16[8,96,512]{2,1,0:T(8,128)(2,1)}), bf16[8,96,512]{2,1,0:T(8,128)(2,1)S(1)}, u32[]{:S(2)}, u32[]{:S(2)}) async-start(bf16[8,96,512]{2,1,0:T(8,128)(2,1)} %pad_maximum_fusion.4), calls=%async_computation.4 | async-start | bytes 1572864 | tf_op jit(solution)/shard_map/all_to_all | solution.py:795
  337.3 174.8 %all-reduce.6.cloned.1.call-start = ((), (), s32[]{:S(2)}) async-start(), calls=%async_computation.11 | async-start | bytes 14942208 | tf_op jit(solution)/shard_map/psum | solution.py:760
  339.0 150.3 %collective-permute-start.25 = (bf16[528,2048]{1,0:T(8,128)(2,1)}, bf16[528,2048]{1,0:T(8,128)(2,1)}, u32[]{:S(2)}, u32[]{:S(2)}) collective-permute-start(bf16[528,2048]{1,0:T(8,128)(2,1)} %get-tuple-element.80), channel_id=1, source_target_pairs={{2,4},{4,2},{6,0},{0,6},{3,5},{5,3},{7,1},{1,7},{10,12},{12,10},{1... | collective-permute-start | bytes 6488072 | tf_op jit(solution)/shard_map/ppermute | solution.py:695
  341.6 147.7 %collective-permute-start.27 = (bf16[528,2048]{1,0:T(8,128)(2,1)}, bf16[528,2048]{1,0:T(8,128)(2,1)}, u32[]{:S(2)}, u32[]{:S(2)}) collective-permute-start(bf16[528,2048]{1,0:T(8,128)(2,1)} %get-tuple-element.83), channel_id=1, source_target_pairs={{0,2},{2,0},{4,6},{6,4},{1,3},{3,1},{5,7},{7,5},{8,10},{10,8},{12,... | collective-permute-start | bytes 6488072 | tf_op jit(solution)/shard_map/ppermute | solution.py:695
  341.6 37.1 %collective-permute-start.20 = (bf16[256,2048]{1,0:T(8,128)(2,1)}, bf16[256,2048]{1,0:T(8,128)(2,1)}, u32[]{:S(2)}, u32[]{:S(2)}) collective-permute-start(bf16[256,2048]{1,0:T(8,128)(2,1)} %get-tuple-element.74), channel_id=1, source_target_pairs={{0,1},{1,0},{2,3},{3,2},{4,5},{5,4},{6,7},{7,6},{8,9},{9,8},{10,11... | collective-permute-start | bytes 3145736 | tf_op jit(solution)/shard_map/ppermute | solution.py:61
  345.3 35.8 %collective-permute-start.16 = (bf16[256,2048]{1,0:T(8,128)(2,1)}, bf16[256,2048]{1,0:T(8,128)(2,1)}, u32[]{:S(2)}, u32[]{:S(2)}) collective-permute-start(bf16[256,2048]{1,0:T(8,128)(2,1)} %fusion.1), channel_id=1, source_target_pairs={{0,1},{1,0},{2,3},{3,2},{4,5},{5,4},{6,7},{7,6},{8,9},{9,8},{10,11... | collective-permute-start | bytes 3145736 | tf_op jit(solution)/shard_map/ppermute | solution.py:61
  355.3 17.2 %all-to-all-start.5 = ((bf16[16,80,128]{2,1,0:T(8,128)(2,1)}), bf16[16,80,128]{2,1,0:T(8,128)(2,1)S(1)}, u32[]{:S(2)}, u32[]{:S(2)}) async-start(bf16[16,80,128]{2,1,0:T(8,128)(2,1)} %maximum_bitcast_fusion.2), calls=%async_computation.5 | async-start | bytes 655360 | tf_op jit(solution)/shard_map/all_to_all | solution.py:78
  363.9 125.4 %collective-permute-start.26 = (bf16[528,2048]{1,0:T(8,128)(2,1)}, bf16[528,2048]{1,0:T(8,128)(2,1)}, u32[]{:S(2)}, u32[]{:S(2)}) collective-permute-start(bf16[528,2048]{1,0:T(8,128)(2,1)} %get-tuple-element.82), channel_id=1, source_target_pairs={{0,4},{4,0},{2,6},{6,2},{1,5},{5,1},{3,7},{7,3},{8,12},{12,8},{10,... | collective-permute-start | bytes 6488072 | tf_op jit(solution)/shard_map/ppermute | solution.py:797
  373.4 76.3 %all-to-all-start.6 = ((bf16[16,80,128]{2,1,0:T(8,128)(2,1)}), bf16[16,80,128]{2,1,0:T(8,128)(2,1)S(1)}, u32[]{:S(2)}, u32[]{:S(2)}) async-start(bf16[16,80,128]{2,1,0:T(8,128)(2,1)} %broadcast_in_dim.26), calls=%async_computation.6 | async-start | bytes 655360 | tf_op jit(solution)/shard_map/all_to_all | solution.py:80
  381.0 65.4 %collective-permute-start.21 = (bf16[64,2048]{1,0:T(8,128)(2,1)S(1)}, bf16[64,2048]{1,0:T(8,128)(2,1)S(1)}, u32[]{:S(2)}, u32[]{:S(2)}) collective-permute-start(bf16[64,2048]{1,0:T(8,128)(2,1)S(1)} %get-tuple-element.128), channel_id=1, source_target_pairs={{0,2},{2,0},{4,6},{6,4},{1,3},{3,1},{5,7},{7,5},{8,10},{10,8},{12,... | collective-permute-start | bytes 786440 | tf_op jit(solution)/shard_map/ppermute | solution.py:69
  381.1 67.8 %collective-permute-start.22 = (bf16[64,2048]{1,0:T(8,128)(2,1)S(1)}, bf16[64,2048]{1,0:T(8,128)(2,1)S(1)}, u32[]{:S(2)}, u32[]{:S(2)}) collective-permute-start(bf16[64,2048]{1,0:T(8,128)(2,1)S(1)} %get-tuple-element.130), channel_id=1, source_target_pairs={{2,4},{4,2},{6,0},{0,6},{3,5},{5,3},{7,1},{1,7},{10,12},{12,10},{1... | collective-permute-start | bytes 786440 | tf_op jit(solution)/shard_map/ppermute | solution.py:69
  450.9 36.2 %all-to-all-start.7 = ((bf16[4,1280,128]{2,1,0:T(8,128)(2,1)}), bf16[4,1280,128]{2,1,0:T(8,128)(2,1)}, u32[]{:S(2)}, u32[]{:S(2)}) async-start(bf16[4,1280,128]{2,1,0:T(8,128)(2,1)} %broadcast_in_dim.32), calls=%async_computation.7 | async-start | bytes 2621440 | tf_op jit(solution)/shard_map/all_to_all | solution.py:40
  455.4 27.6 %collective-permute-start.18 = (bf16[64,2048]{1,0:T(8,128)(2,1)}, bf16[64,2048]{1,0:T(8,128)(2,1)S(1)}, u32[]{:S(2)}, u32[]{:S(2)}) collective-permute-start(bf16[64,2048]{1,0:T(8,128)(2,1)} %get-tuple-element.133), channel_id=1, source_target_pairs={{2,4},{4,2},{6,0},{0,6},{3,5},{5,3},{7,1},{1,7},{10,12},{12,10},{1... | collective-permute-start | bytes 786440 | tf_op jit(solution)/shard_map/ppermute | solution.py:69
  460.0 22.9 %collective-permute-start.19 = (bf16[64,2048]{1,0:T(8,128)(2,1)}, bf16[64,2048]{1,0:T(8,128)(2,1)S(1)}, u32[]{:S(2)}, u32[]{:S(2)}) collective-permute-start(bf16[64,2048]{1,0:T(8,128)(2,1)} %get-tuple-element.132), channel_id=1, source_target_pairs={{0,4},{4,0},{2,6},{6,2},{1,5},{5,1},{3,7},{7,3},{8,12},{12,8},{10,... | collective-permute-start | bytes 786440 | tf_op jit(solution)/shard_map/ppermute | solution.py:69
  487.0 16.8 %collective-permute-start.24 = (bf16[4,1280,128]{2,1,0:T(8,128)(2,1)}, bf16[4,1280,128]{2,1,0:T(8,128)(2,1)S(1)}, u32[]{:S(2)}, u32[]{:S(2)}) collective-permute-start(bf16[4,1280,128]{2,1,0:T(8,128)(2,1)} %all-to-all-done.7), channel_id=1, source_target_pairs={{0,1},{1,0},{2,3},{3,2},{4,5},{5,4},{6,7},{7,6},{8,9},{9,8},{10,11... | collective-permute-start | bytes 3932168 | tf_op jit(solution)/shard_map/ppermute | solution.py:41
  (103 other events, 686.2 us)
Sparse Core Ops, SparseCore 0:
  9.8 35.5 all-gather.3
  93.3 28.6 all-gather.5
  267.5 26.3 all-gather.7
  345.7 140.6 all-reduce.5

commit v2 on v1

--- a/solution.py
+++ b/solution.py
@@ -35,12 +35,20 @@
     return lax.all_gather(x, GROUP, axis=0, tiled=True)
 
 
-def gather_rows_directly(x, first_core):
+def gather_rows_directly(x, first_core, beside):
     copies = jnp.broadcast_to(x[None], (RINGS, *x.shape))
     mine = lax.all_to_all(copies, "y", 0, 0, tiled=True)
+    mine = after(mine, *beside)
     other = lax.ppermute(mine, "core", SWAP)
     first, second = jnp.where(first_core, mine, other), jnp.where(first_core, other, mine)
     return jnp.stack([first, second], axis=1).reshape(-1, x.shape[1])
+
+
+def as_unit(work, always):
+    shapes = jax.eval_shape(work)
+    return lax.cond(
+        always, work, lambda: jax.tree.map(lambda a: jnp.zeros(a.shape, a.dtype), shapes)
+    )
 
 
 def by_core(x, first_core):
@@ -275,6 +283,35 @@
     )(core, rows, cot, w_gate, w_up, w_down)
 
 
+def expert_outputs_kernel(same, own, taken_hbm, pair, cross, far, *refs):
+    outs, taken, sem = refs[:3], refs[3], refs[4]
+    copy = pltpu.make_async_copy(taken_hbm.at[pl.ds(0, 3 * HIDDEN)], taken, sem)
+    copy.start()
+    copy.wait()
+    for m, out in enumerate(outs):
+        rows = slice(m * HIDDEN, (m + 1) * HIDDEN)
+        ours = own[rows, :].astype(jnp.float32) + taken[rows, :].astype(jnp.float32)
+        ours += pair[rows, :].astype(jnp.float32)
+        others = cross[rows, :].astype(jnp.float32) + far[rows, :].astype(jnp.float32)
+        out[same[0]] = ours
+        out[1 - same[0]] = others
+
+
+def expert_outputs(same, own, taken, pair, cross, far):
+    vmem = pl.BlockSpec(memory_space=pltpu.VMEM)
+    first = pl.BlockSpec(memory_space=pl.ANY)
+    return pl.pallas_call(
+        expert_outputs_kernel,
+        out_shape=(jax.ShapeDtypeStruct((CORES, HIDDEN, D), jnp.float32),) * 3,
+        in_specs=[pl.BlockSpec(memory_space=pltpu.SMEM), vmem, first] + [vmem] * 3,
+        out_specs=(vmem,) * 3,
+        scratch_shapes=[pltpu.VMEM((3 * HIDDEN, D), jnp.bfloat16), pltpu.SemaphoreType.DMA],
+        compiler_params=pltpu.CompilerParams(vmem_limit_bytes=VMEM_BYTES),
+        cost_estimate=pl.CostEstimate(flops=0, bytes_accessed=20 << 20, transcendentals=0),
+        name="expert_outputs",
+    )(same, own, taken, pair, cross, far)
+
+
 def kv_kernel(left, right, out):
     out[...] = jnp.dot(left[...], right[...], preferred_element_type=jnp.float32).astype(
         jnp.bfloat16
@@ -289,7 +326,7 @@
         in_specs=[vmem] * 2,
         out_specs=vmem,
         compiler_params=pltpu.CompilerParams(vmem_limit_bytes=VMEM_BYTES),
-        cost_estimate=pl.CostEstimate(flops=SHORT, bytes_accessed=4 << 20, transcendentals=0),
+        cost_estimate=pl.CostEstimate(flops=LONG, bytes_accessed=4 << 20, transcendentals=0),
         name="kv_product",
     )(left, right)
 
@@ -662,10 +699,12 @@
     back = after(to_owners(back), *block_grads)
 
     taken_grads = lax.ppermute(block_grads[RINGS], "core", SWAP)
-    taken_grads = [taken_grads[3 * HIDDEN * r : 3 * HIDDEN * (r + 1)] for r in range(RINGS)]
     grads_sent = [
-        (mine.astype(jnp.float32) + taken.astype(jnp.float32)).astype(jnp.bfloat16)
-        for mine, taken in zip(block_grads[1:RINGS], taken_grads[1:])
+        (
+            block_grads[r].astype(jnp.float32)
+            + taken_grads[3 * HIDDEN * r : 3 * HIDDEN * (r + 1)].astype(jnp.float32)
+        ).astype(jnp.bfloat16)
+        for r in range(1, RINGS)
     ]
 
     summed = sum_rows_directly(
@@ -691,8 +730,6 @@
     grad_attended = gather_rows(grad_residual_low)
     returned = to_owners(after(out, grad_residual_low))
 
-    grad_attended, *grads_sent = lax.optimization_barrier((grad_attended, *grads_sent))
-    grads_got = [lax.ppermute(g, "y", pairs) for g, pairs in zip(grads_sent, (PAIRS, CROSS))]
     grad_w_out = matmul_tn(heads_out, grad_attended).astype(jnp.bfloat16)
 
     grad_heads = (
@@ -739,12 +776,6 @@
         .astype(jnp.bfloat16)
         .reshape(length, heads_here * qk_width)
     )
-    returned = after(returned, grad_query)
-    act_parts = parts_of(shared_act)
-    routed_and_shared = sum_rows_directly(
-        *(matmul(a, returned) + matmul(b, shared_down) for a, b in zip(slot_parts, act_parts))
-    )
-    output = (residual + routed_and_shared).astype(jnp.bfloat16)
     grad_w_query = matmul_tn(normed_a, grad_query).astype(jnp.bfloat16)
     grad_key_value = (
         jnp.concatenate([grad_key_nope, grad_values], axis=-1)
@@ -791,34 +822,45 @@
         axis=1,
     )
     bundle = after(bundle, returned, *local_grads)
-    bundle = jnp.sum(
-        lax.all_to_all(bundle, GROUP, 0, 0, tiled=True).astype(jnp.float32), axis=0
-    ).astype(jnp.bfloat16)
-    grads_got.append(lax.ppermute(after(grads_sent[2], bundle), "y", OPPOSITE))
-    grad_normed_one = sum_rows_directly(kept, given)
-    grad_from_first, _ = norm_backward(
-        own(input_full), own(factor_one), attn_gain, grad_normed_one
-    )
-    grad_input = grad_residual + grad_from_first
-    kv_slice = kv_product(bundle[:kv_share], normed_a)
-    other_rows = bundle[kv_share:].reshape(-1, D)
-    replicated = jnp.concatenate(
-        [kv_slice, other_rows, jnp.zeros((80 - kv_share - other_rows.shape[0], D), jnp.bfloat16)],
-        axis=0,
-    )
-    replicated = jnp.swapaxes(replicated.reshape(80, RANKS, D // RANKS), 0, 1)
-    replicated = sum_ranks(replicated)
-    def by_expert(m):
-        part = slice(m * HIDDEN, (m + 1) * HIDDEN)
-        ours = block_grads[0][part].astype(jnp.float32) + taken_grads[0][part].astype(jnp.float32)
-        ours = ours + grads_got[0][part].astype(jnp.float32)
-        others = grads_got[1][part].astype(jnp.float32) + grads_got[2][part].astype(jnp.float32)
-        return jnp.stack(
-            [jnp.where(second_expert, others, ours), jnp.where(second_expert, ours, others)]
-        )
-
-    expert_grads = [by_expert(m) for m in range(3)]
-    replicated = gather_rows_directly(replicated.reshape(RANKS * 80, D // RANKS), first_core)
+
+    def last_sums():
+        tiles = lax.all_to_all(bundle, GROUP, 0, 0, tiled=True)
+        slices = total_of(tiles).astype(jnp.bfloat16)
+        pair_grads = lax.ppermute(grads_sent[0], "y", PAIRS)
+        cross_grads = lax.ppermute(grads_sent[1], "y", CROSS)
+        grad_normed_one = sum_rows_directly(kept, given)
+        act_parts = parts_of(shared_act)
+        routed_and_shared = sum_rows_directly(
+            *(matmul(a, returned) + matmul(b, shared_down) for a, b in zip(slot_parts, act_parts))
+        )
+        output = (residual + routed_and_shared).astype(jnp.bfloat16)
+        grad_from_first, _ = norm_backward(
+            own(input_full), own(factor_one), attn_gain, grad_normed_one
+        )
+        grad_input = grad_residual + grad_from_first
+        far_grads = lax.ppermute(
+            after(grads_sent[2], slices), "y", OPPOSITE
+        )
+        kv_slice = kv_product(slices[:kv_share], normed_a)
+        other_rows = slices[kv_share:].reshape(-1, D)
+        rest = jnp.zeros((80 - kv_share - other_rows.shape[0], D), jnp.bfloat16)
+        replicated = jnp.concatenate([kv_slice, other_rows, rest], axis=0)
+        replicated = jnp.swapaxes(replicated.reshape(80, RANKS, D // RANKS), 0, 1)
+        replicated = sum_ranks(replicated)
+        expert_grads = expert_outputs(
+            same.reshape(1), block_grads[0], taken_grads, pair_grads, cross_grads, far_grads
+        )
+        replicated = after(
+            replicated, pair_grads, cross_grads, far_grads
+        )
+        replicated = gather_rows_directly(
+            replicated.reshape(RANKS * 80, D // RANKS), first_core, expert_grads
+        )
+        return grad_input, replicated, output, expert_grads
+
+    grad_input, replicated, output, expert_grads = as_unit(
+        last_sums, routes[0, 0] >= 0
+    )
     replicated = replicated.reshape(parts, RANKS, 80, D // RANKS)
     replicated = jnp.swapaxes(replicated, 1, 2).reshape(parts, 80, D).astype(jnp.float32)
     grad_w_kv_down = jnp.swapaxes(replicated[:, :kv_share].reshape(-1, D), 0, 1)

time: 539 us -> 528 us (0.980)
  waiting for transfers between devices: 198 us -> 175 us
  other arithmetic: 79.6 us -> 61.2 us
  loops' own time: 0 us -> 12.1 us
  Pallas kernels: 79.2 us -> 88.2 us
    ppermute x12, waiting for transfers between devices: 101 us -> 31.4 us  [sum_rows_directly(): total = total + lax.ppermute(tile, 'y', pairs).astype(jnp.float32)]
    ppermute x3, waiting for transfers between devices: 0.01 us -> 43.4 us  [the longest x1 43.4 us: last_sums(): far_grads = lax.ppermute(after(grads_sent[2], slices), 'y', OPPOSITE)]
    another operation x9 -> x6, other arithmetic: 16 us -> 3.52 us  [the longest x3 10.7 us: by_expert(): jnp.stack([jnp.where(second_expert, others, ours), jnp.where(second_exper...]
    another operation x0 -> x1, loops' own time: none -> 12.1 us  [as_unit(): lax.cond(always, work, lambda: jax.tree.map(lambda a: jnp.zeros(a.shape,...]
    pallas_call x0 -> x1, Pallas kernels: none -> 9.32 us  [expert_outputs(): pl.pallas_call(expert_outputs_kernel, out_shape=(jax.ShapeDtypeStruct((CO...]
    all_to_all x1, waiting for transfers between devices: 8.37 us -> 0.01 us  [sum_ranks(): tiles = lax.all_to_all(x, EXPERT, 0, 0, tiled=True)]
    all_to_all x1, waiting for transfers between devices: 0.01 us -> 6.17 us  [sum_ranks(): lax.all_to_all(jnp.broadcast_to(total[None], x.shape), EXPERT, 0, 0, tile...]
  transfers between devices with their start and end apart: 40 -> 40, of which waited for: 21 -> 18; matrix products, arithmetic and copies ran while one was open for 24% -> 20% of each run, Pallas kernels for 10% -> 12%
where the time goes in v2:
time: 528 us; the launch traced here: 520 us
  waiting for transfers between devices  175 us (33%)
  Pallas kernels  88.2 us (17%)
  starting transfers between devices  86.5 us (16%)
  other arithmetic  61.2 us (12%)
  matrix products  43.6 us (8%)
  local copies, waits for them, and re-layouts  31.5 us (6%)
  between operations  21.6 us (4%)
  loops' own time  12.1 us (2%)
    ppermute x1, waiting for transfers between devices, last_sums(): far_grads = lax.ppermute(after(grads_sent[2], slices), 'y', OPPOSITE)  43.4 us
    all_gather x3, waiting for transfers between devices, gather_rows(): return lax.all_gather(x, GROUP, axis=0, tiled=True)  36.9 us
    ppermute x12, waiting for transfers between devices, sum_rows_directly(): total = total + lax.ppermute(tile, 'y', pairs).astype(jnp.float32)  31.4 us
    pallas_call x1, Pallas kernels, expert_rows(): pl.pallas_call(expert_kernel, out_shape=(jax.ShapeDtypeStruct(x.shape, bf...  25.5 us
    all_to_all x4, starting transfers between devices, to_owners(): lax.all_to_all(x.reshape(RANKS, x.shape[0] // RANKS, x.shape[1]), EXPERT,...  24.1 us
    dot_general x12, matrix products, matmul(): return jnp.dot(left, right, preferred_element_type=jnp.float32)  23.6 us
    all_to_all x4, waiting for transfers between devices, to_owners(): lax.all_to_all(x.reshape(RANKS, x.shape[0] // RANKS, x.shape[1]), EXPERT,...  22.6 us
    pallas_call x1, Pallas kernels, expert_weights(): pl.pallas_call(expert_weights_kernel, out_shape=(jax.ShapeDtypeStruct((sl...  21.6 us
  transfers between devices with their start and end apart: 40, of which 18 were waited for; matrix products, arithmetic and copies ran while one was open for 20% of the time, Pallas kernels for 12%

profile of v2, /device:TPU:1, one launch (start us, length us, event | category | flops | bytes accessed | tf_op | source)
XLA Modules:
  0.0 519.6 jit_solution(6259275847008527703)
XLA Ops:
  45.4 4.3 convolution_convert_fusion.1
  49.7 19.2 %collective-permute-done.12.refs_4_.refs_6_ = bf16[528,2048]{1,0:T(8,128)(2,1)} collective-permute-done((bf16[528,2048]{1,0:T(8,128)(2,1)}, bf16[528,2048]{1,0:T(8,128)(2,1)}, u32[]{:S(2)}, u32[]{:S(2)}) %collective-permute-start.12) | collective-permute-done | bytes 2162720 | tf_op jit(solution)/shard_map/ppermute | solution.py:588
  68.9 3.9 collective-permute-done.13.refs_5_.refs_7_
  84.2 7.8 %collective-permute-done.16 = bf16[64,2048]{1,0:T(8,128)(2,1)} collective-permute-done((bf16[64,2048]{1,0:T(8,128)(2,1)}, bf16[64,2048]{1,0:T(8,128)(2,1)}, u32[]{:S(2)}, u32[]{:S(2)}) %collective-permute-start.16) | collective-permute-done | bytes 262176 | tf_op jit(solution)/shard_map/ppermute | solution.py:77
  95.2 7.7 %all-to-all-start.4 = ((bf16[16,32,2048]{2,1,0:T(8,128)(2,1)}), bf16[16,32,2048]{2,1,0:T(8,128)(2,1)S(1)}, u32[]{:S(2)}, u32[]{:S(2)}) async-start(bf16[16,32,2048]{2,1,0:T(8,128)(2,1)} %bitcast.275), calls=%async_computation.4 | async-start | bytes 4194304 | tf_op jit(solution)/shard_map/all_to_all | solution.py:160
  103.0 19.3 %all-gather.6.cloned.1.call-done.rows_ref = bf16[512,2048]{1,0:T(8,128)(2,1)} async-done(((bf16[64,2048]{1,0:T(8,128)(2,1)}), bf16[512,2048]{1,0:T(8,128)(2,1)}) %all-gather.6.cloned.1.call-update) | async-done | bytes 2097168 | tf_op jit(solution)/shard_map/all_gather | solution.py:35
  128.6 5.3 %dispatch.1 = bf16[512,2176]{1,0:T(8,128)(2,1)} custom-call(bf16[512,512]{1,0:T(8,128)(2,1)} %get-tuple-element.278.map_ref, bf16[512,2048]{1,0:T(8,128)(2,1)} %all-gather.6.cloned.1.call-done.rows_ref, bf16[512,128]{1,0:T(8,128)(2,1)} %pad_maximum_fusion.8.tail_ref), custom_call_target="tpu_custom_call" | custom-call | flops 1140850688 | bytes 8388608 | tf_op jit(solution)/shard_map/dispatch/pallas_call | solution.py:204
  135.2 6.8 %all-to-all-start.5 = ((bf16[16,32,2176]{2,1,0:T(8,128)(2,1)}), bf16[16,32,2176]{2,1,0:T(8,128)(2,1)}, u32[]{:S(2)}, u32[]{:S(2)}) async-start(bf16[16,32,2176]{2,1,0:T(8,128)(2,1)} %bitcast.244), calls=%async_computation.5 | async-start | bytes 4456448 | tf_op jit(solution)/shard_map/all_to_all | solution.py:160
  143.5 15.5 %shared_experts.1 = (bf16[352,2048]{1,0:T(8,128)(2,1)}, bf16[352,2048]{1,0:T(8,128)(2,1)}, bf16[352,2048]{1,0:T(8,128)(2,1)}, bf16[512,352]{1,0:T(8,128)(2,1)}, ...) custom-call(s32[1]{0:T(128)} %bitcast.30.core, bf16[512,2048]{1,0:T(8,128)(2,1)} %all-gather.6.cloned.1.call-done.rows_ref, ...), custom_call_target="tpu_custom_call" | custom-call | flops 17999998976 | bytes 20971520 | tf_op jit(solution)/shard_map/shared_experts/pallas_call | solution.py:273
  158.9 13.6 %all-to-all-done.5 = bf16[16,32,2176]{2,1,0:T(8,128)(2,1)} async-done(((bf16[16,32,2176]{2,1,0:T(8,128)(2,1)}), bf16[16,32,2176]{2,1,0:T(8,128)(2,1)}, u32[]{:S(2)}, u32[]{:S(2)}) %all-to-all-start.5) | async-done | bytes 2228256 | tf_op jit(solution)/shard_map/all_to_all | solution.py:160
  176.1 3.5 collective-permute-done.22.refs_10_.refs_12_
  179.6 25.5 %expert_rows.1 = (bf16[512,2176]{1,0:T(8,128)(2,1)}, bf16[512,1408]{1,0:T(8,128)(2,1)}, bf16[512,1408]{1,0:T(8,128)(2,1)}, bf16[512,1408]{1,0:T(8,128)(2,1)}) custom-call(s32[1]{0:T(128)} %bitcast.66.refs_0_, bf16[512,2176]{1,0:T(8,128)(2,1)} %bitcast.70.refs_1_.refs_0_, bf16[512,2048]{1,0:T(8,128)(2,1)} %bitcast.273, ...), custom_call_target="tpu_custom_call" | custom-call | flops 14763950080 | bytes 29360128 | tf_op jit(solution)/shard_map/expert_rows/pallas_call | solution.py:452
  205.1 5.1 all-to-all-start.6
  210.2 21.6 %expert_weights.1 = (bf16[512,2048]{1,0:T(8,128)(2,1)}, bf16[528,2048]{1,0:T(8,128)(2,1)}, bf16[528,2048]{1,0:T(8,128)(2,1)}, bf16[528,2048]{1,0:T(8,128)(2,1)},...) custom-call(bf16[512,2176]{1,0:T(8,128)(2,1)} %bitcast.70.refs_1_.refs_0_, bf16[512,2048]{1,0:T(8,128)(2,1)} %bitcast.274, ...), custom_call_target="tpu_custom_call" | custom-call | flops 99999997952 | bytes 35651584 | tf_op jit(solution)/shard_map/expert_weights/pallas_call | solution.py:529
  231.8 9.1 %all-to-all-done.6 = bf16[16,32,2176]{2,1,0:T(8,128)(2,1)S(1)} async-done(((bf16[16,32,2176]{2,1,0:T(8,128)(2,1)}), bf16[16,32,2176]{2,1,0:T(8,128)(2,1)S(1)}, u32[]{:S(2)}, u32[]{:S(2)}) %all-to-all-start.6) | async-done | bytes 2228256 | tf_op jit(solution)/shard_map/all_to_all | solution.py:160
  252.5 6.4 %collective-permute-done.26 = bf16[64,2176]{1,0:T(8,128)(2,1)S(1)} collective-permute-done((bf16[64,2176]{1,0:T(8,128)(2,1)S(1)}, bf16[64,2176]{1,0:T(8,128)(2,1)S(1)}, u32[]{:S(2)}, u32[]{:S(2)}) %collective-permute-start.26) | collective-permute-done | bytes 278560 | tf_op jit(solution)/shard_map/ppermute | solution.py:77
  258.9 6.6 %collective-permute-done.25 = bf16[64,2176]{1,0:T(8,128)(2,1)S(1)} collective-permute-done((bf16[64,2176]{1,0:T(8,128)(2,1)S(1)}, bf16[64,2176]{1,0:T(8,128)(2,1)S(1)}, u32[]{:S(2)}, u32[]{:S(2)}) %collective-permute-start.25) | collective-permute-done | bytes 278560 | tf_op jit(solution)/shard_map/ppermute | solution.py:77
  271.6 4.4 all-to-all-start.7
  276.1 15.9 %all-gather.8.cloned.1.call-done = bf16[512,2048]{1,0:T(8,128)(2,1)} async-done(((bf16[64,2048]{1,0:T(8,128)(2,1)}), bf16[512,2048]{1,0:T(8,128)(2,1)}) %all-gather.8.cloned.1.call-update) | async-done | bytes 2097168 | tf_op jit(solution)/shard_map/all_gather | solution.py:35
  305.6 8.2 %attention_rows.1 = (bf16[256,2048]{1,0:T(8,128)(2,1)}, bf16[256,2048]{1,0:T(8,128)(2,1)}, f32[1,2048]{1,0:T(1,128)}) custom-call(s32[1]{0:T(128)} %bitcast.30.core, bf16[512,384]{1,0:T(8,128)(2,1)} %copy.194.query_ref, bf16[512,576]{1,0:T(8,128)(2,1)} %pad_maximum_fusion.4.compressed_ref, bf16[512,2048]{1,0:T(8,128)(2,1)} %x_ref.1, ...), custom_call_target="tpu_custom_call" | custom-call | flops 99999997952 | bytes 10485760 | tf_op jit(solution)/shard_map/attention_rows/pallas_call | solution.py:367
  326.5 7.1 %add_convert_fusion.2 = (bf16[528,2048]{1,0:T(8,128)(2,1)}, bf16[528,2048]{1,0:T(8,128)(2,1)}, bf16[528,2048]{1,0:T(8,128)(2,1)}) fusion(bf16[528,2048]{1,0:T(8,128)(2,1)} %get-tuple-element.155, bf16[2112,2048]{1,0:T(8,128)(2,1)} %collective-permute-done.27, bf16[528,2048]{1,0:T(8,128)(2,1)} %get-tuple-element.154, bf16[528,2048]{1,0:T(8,128)(2,1)S(1)} %copy-done.27), kind=kLoop, calls=%fused_computation.36 | loop fusion | flops 12976128 | bytes 19464192 | tf_op jit(solution)/shard_map/convert_element_type | solution.py:706
  333.7 161.1 %conditional.1 = (f32[64,2048]{1,0:T(8,128)}, bf16[10240,128]{1,0:T(8,128)(2,1)S(1)}, bf16[64,2048]{1,0:T(8,128)(2,1)}, f32[2,176,2048]{2,1,0:T(8,128)}, f32[2,1...) conditional(s32[]{:T(128)} %bitcast.28, () %tuple.28, (s32[]{:T(128)}, f32[512,1]{0,1:T(1,128)}, ...), branch_computations={%region_12.13_spmd, %region_13.17_spmd} | conditional | flops 101825658880 | bytes 151080944 | solution.py:49
  334.6 3.7 all-to-all-start
  346.1 4.5 all-to-all-done
  356.7 6.3 %all-to-all-start.1 = ((bf16[16,80,128]{2,1,0:T(8,128)(2,1)}), bf16[16,80,128]{2,1,0:T(8,128)(2,1)S(1)}, u32[]{:S(2)}, u32[]{:S(2)}) async-start(bf16[16,80,128]{2,1,0:T(8,128)(2,1)} %maximum_bitcast_fusion), calls=%async_computation.1 | async-start | bytes 655360 | tf_op jit(solution)/shard_map/cond/branch_1_fun/all_to_all | solution.py:86
  384.5 6.9 %all-to-all-start.2 = ((bf16[16,80,128]{2,1,0:T(8,128)(2,1)}), bf16[16,80,128]{2,1,0:T(8,128)(2,1)S(1)}, u32[]{:S(2)}, u32[]{:S(2)}) async-start(bf16[16,80,128]{2,1,0:T(8,128)(2,1)} %broadcast_in_dim.14), calls=%async_computation.2 | async-start | bytes 655360 | tf_op jit(solution)/shard_map/cond/branch_1_fun/all_to_all | solution.py:88
  393.8 6.2 %all-to-all-done.2 = bf16[16,80,128]{2,1,0:T(8,128)(2,1)S(1)} async-done(((bf16[16,80,128]{2,1,0:T(8,128)(2,1)}), bf16[16,80,128]{2,1,0:T(8,128)(2,1)S(1)}, u32[]{:S(2)}, u32[]{:S(2)}) %all-to-all-start.2) | async-done | bytes 327712 | tf_op jit(solution)/shard_map/cond/branch_1_fun/all_to_all | solution.py:88
  400.0 43.4 %collective-permute-done.6.far = bf16[528,2048]{1,0:T(8,128)(2,1)} collective-permute-done((bf16[528,2048]{1,0:T(8,128)(2,1)}, bf16[528,2048]{1,0:T(8,128)(2,1)}, u32[]{:S(2)}, u32[]{:S(2)}) %collective-permute-start.6) | collective-permute-done | bytes 2162720 | tf_op jit(solution)/shard_map/cond/branch_1_fun/ppermute | solution.py:841
  444.7 4.3 all-to-all-start.3
  462.7 9.3 %expert_outputs.1 = (f32[2,176,2048]{2,1,0:T(8,128)}, f32[2,176,2048]{2,1,0:T(8,128)}, f32[2,176,2048]{2,1,0:T(8,128)}) custom-call(s32[1]{0:T(128)} %bitcast.12.same, bf16[528,2048]{1,0:T(8,128)(2,1)} %get-tuple-element.75.own, bf16[2112,2048]{1,0:T(8,128)(2,1)} %get-tuple-element.76.taken_hbm, bf16[528,2048]{1,0:T(8,128)(2,1)} %collective-permute-done.4.pair, ...), custom_call_target="tpu_custom_call" | custom-call | bytes 20971520 | tf_op jit(solution)/shard_map/cond/branch_1_fun/expert_outputs/pallas_call | solution.py:303
  472.1 5.3 %collective-permute-done.2 = bf16[64,2048]{1,0:T(8,128)(2,1)S(1)} collective-permute-done((bf16[64,2048]{1,0:T(8,128)(2,1)}, bf16[64,2048]{1,0:T(8,128)(2,1)S(1)}, u32[]{:S(2)}, u32[]{:S(2)}) %collective-permute-start.2) | collective-permute-done | bytes 262176 | tf_op jit(solution)/shard_map/cond/branch_1_fun/ppermute | solution.py:77
  477.4 7.1 %collective-permute-start.7 = (bf16[4,1280,128]{2,1,0:T(8,128)(2,1)}, bf16[4,1280,128]{2,1,0:T(8,128)(2,1)S(1)}, u32[]{:S(2)}, u32[]{:S(2)}) collective-permute-start(bf16[4,1280,128]{2,1,0:T(8,128)(2,1)} %all-to-all-done.3), channel_id=1, source_target_pairs={{0,1},{1,0},{2,3},{3,2},{4,5},{5,4},{6,7},{7,6},{8,9},{9,8},{10,11... | collective-permute-start | bytes 3932168 | tf_op jit(solution)/shard_map/cond/branch_1_fun/ppermute | solution.py:42
  (389 shorter events, 171.9 us)
Async XLA Ops:
  7.2 38.2 %all-gather.4.cloned.1.call-start = ((), (), s32[]{:S(2)}) async-start(), calls=%async_computation.8 | async-start | bytes 2359296 | tf_op jit(solution)/shard_map/all_gather | solution.py:35
  7.9 114.4 %all-gather.6.cloned.1.call-start = ((), (), s32[]{:S(2)}) async-start(), calls=%async_computation.9 | async-start | bytes 2359296 | tf_op jit(solution)/shard_map/all_gather | solution.py:35
  11.7 57.2 %collective-permute-start.12 = (bf16[528,2048]{1,0:T(8,128)(2,1)}, bf16[528,2048]{1,0:T(8,128)(2,1)}, u32[]{:S(2)}, u32[]{:S(2)}) collective-permute-start(bf16[528,2048]{1,0:T(8,128)(2,1)} %pad_maximum_fusion.1.refs_3_.refs_5_), channel_id=1, source_target_pairs={{0,2},{2,0},{4,6},{6,4},{1,3},{3,1},{5,7},{7,5},{8,10},{10,8},{12,... | collective-permute-start | bytes 6488072 | tf_op jit(solution)/shard_map/ppermute | solution.py:588
  15.3 57.5 %collective-permute-start.13 = (bf16[528,2048]{1,0:T(8,128)(2,1)}, bf16[528,2048]{1,0:T(8,128)(2,1)}, u32[]{:S(2)}, u32[]{:S(2)}) collective-permute-start(bf16[528,2048]{1,0:T(8,128)(2,1)} %pad_maximum_fusion.2), channel_id=1, source_target_pairs={{2,4},{4,2},{6,0},{0,6},{3,5},{5,3},{7,1},{1,7},{10,12},{12,10},{1... | collective-permute-start | bytes 6488072 | tf_op jit(solution)/shard_map/ppermute | solution.py:589
  32.5 40.4 %collective-permute-start.14 = (bf16[256,2048]{1,0:T(8,128)(2,1)}, bf16[256,2048]{1,0:T(8,128)(2,1)}, u32[]{:S(2)}, u32[]{:S(2)}) collective-permute-start(bf16[256,2048]{1,0:T(8,128)(2,1)} %bitcast.55), channel_id=1, source_target_pairs={{0,1},{1,0},{2,3},{3,2},{4,5},{5,4},{6,7},{7,6},{8,9},{9,8},{10,11... | collective-permute-start | bytes 3145736 | tf_op jit(solution)/shard_map/ppermute | solution.py:69
  95.2 38.6 %all-to-all-start.4 = ((bf16[16,32,2048]{2,1,0:T(8,128)(2,1)}), bf16[16,32,2048]{2,1,0:T(8,128)(2,1)S(1)}, u32[]{:S(2)}, u32[]{:S(2)}) async-start(bf16[16,32,2048]{2,1,0:T(8,128)(2,1)} %bitcast.275), calls=%async_computation.4 | async-start | bytes 4194304 | tf_op jit(solution)/shard_map/all_to_all | solution.py:160
  122.3 50.2 %collective-permute-start.18 = (bf16[528,2048]{1,0:T(8,128)(2,1)}, bf16[528,2048]{1,0:T(8,128)(2,1)}, u32[]{:S(2)}, u32[]{:S(2)}) collective-permute-start(bf16[528,2048]{1,0:T(8,128)(2,1)} %pad_maximum_fusion.2), channel_id=1, source_target_pairs={{0,4},{4,0},{2,6},{6,2},{1,5},{5,1},{3,7},{7,3},{8,12},{12,8},{10,... | collective-permute-start | bytes 6488072 | tf_op jit(solution)/shard_map/ppermute | solution.py:666
  135.2 37.3 %all-to-all-start.5 = ((bf16[16,32,2176]{2,1,0:T(8,128)(2,1)}), bf16[16,32,2176]{2,1,0:T(8,128)(2,1)}, u32[]{:S(2)}, u32[]{:S(2)}) async-start(bf16[16,32,2176]{2,1,0:T(8,128)(2,1)} %bitcast.244), calls=%async_computation.5 | async-start | bytes 4456448 | tf_op jit(solution)/shard_map/all_to_all | solution.py:160
  142.0 34.1 %collective-permute-start.19 = (bf16[528,2048]{1,0:T(8,128)(2,1)}, bf16[528,2048]{1,0:T(8,128)(2,1)}, u32[]{:S(2)}, u32[]{:S(2)}) collective-permute-start(bf16[528,2048]{1,0:T(8,128)(2,1)} %pad_maximum_fusion.1.refs_3_.refs_5_), channel_id=1, source_target_pairs={{0,1},{1,0},{2,3},{3,2},{4,5},{5,4},{6,7},{7,6},{8,9},{9,8},{10,11... | collective-permute-start | bytes 6488072 | tf_op jit(solution)/shard_map/ppermute | solution.py:691
  143.0 33.1 %collective-permute-start.20 = (bf16[528,2048]{1,0:T(8,128)(2,1)}, bf16[528,2048]{1,0:T(8,128)(2,1)}, u32[]{:S(2)}, u32[]{:S(2)}) collective-permute-start(bf16[528,2048]{1,0:T(8,128)(2,1)} %collective-permute-done.12.refs_4_.refs_6_), channel_id=1, source_target_pairs={{0,1},{1,0},{2,3},{3,2},{4,5},{5,4},{6,7},{7,6},{8,9},{9,8},{10,11... | collective-permute-start | bytes 6488072 | tf_op jit(solution)/shard_map/ppermute | solution.py:691
  143.0 33.1 %collective-permute-start.21 = (bf16[528,2048]{1,0:T(8,128)(2,1)}, bf16[528,2048]{1,0:T(8,128)(2,1)}, u32[]{:S(2)}, u32[]{:S(2)}) collective-permute-start(bf16[528,2048]{1,0:T(8,128)(2,1)} %collective-permute-done.13.refs_5_.refs_7_), channel_id=1, source_target_pairs={{0,1},{1,0},{2,3},{3,2},{4,5},{5,4},{6,7},{7,6},{8,9},{9,8},{10,11... | collective-permute-start | bytes 6488072 | tf_op jit(solution)/shard_map/ppermute | solution.py:691
  205.1 35.8 %all-to-all-start.6 = ((bf16[16,32,2176]{2,1,0:T(8,128)(2,1)}), bf16[16,32,2176]{2,1,0:T(8,128)(2,1)S(1)}, u32[]{:S(2)}, u32[]{:S(2)}) async-start(bf16[16,32,2176]{2,1,0:T(8,128)(2,1)} %bitcast.267), calls=%async_computation.6 | async-start | bytes 4456448 | tf_op jit(solution)/shard_map/all_to_all | solution.py:160
  210.2 81.9 %all-gather.8.cloned.1.call-start = ((), (), s32[]{:S(2)}) async-start(), calls=%async_computation.10 | async-start | bytes 2359296 | tf_op jit(solution)/shard_map/all_gather | solution.py:35
  270.1 56.4 %collective-permute-start.27 = (bf16[2112,2048]{1,0:T(8,128)(2,1)}, bf16[2112,2048]{1,0:T(8,128)(2,1)}, u32[]{:S(2)}, u32[]{:S(2)}) collective-permute-start(bf16[2112,2048]{1,0:T(8,128)(2,1)} %get-tuple-element.156), channel_id=1, source_target_pairs={{0,1},{1,0},{2,3},{3,2},{4,5},{5,4},{6,7},{7,6},{8,9},{9,8},{10,11... | collective-permute-start | bytes 25952264 | tf_op jit(solution)/shard_map/ppermute | solution.py:701
  271.6 52.8 %all-to-all-start.7 = ((bf16[16,32,2048]{2,1,0:T(8,128)(2,1)}), bf16[16,32,2048]{2,1,0:T(8,128)(2,1)}, u32[]{:S(2)}, u32[]{:S(2)}) async-start(bf16[16,32,2048]{2,1,0:T(8,128)(2,1)} %bitcast.272), calls=%async_computation.7 | async-start | bytes 4194304 | tf_op jit(solution)/shard_map/all_to_all | solution.py:160
  276.1 225.0 %all-reduce.6.cloned.1.call-start = ((), (), s32[]{:S(2)}) async-start(), calls=%async_computation.11 | async-start | bytes 14942208 | tf_op jit(solution)/shard_map/psum | solution.py:791
  334.6 16.1 %all-to-all-start = ((bf16[8,96,512]{2,1,0:T(8,128)(2,1)}), bf16[8,96,512]{2,1,0:T(8,128)(2,1)S(1)}, u32[]{:S(2)}, u32[]{:S(2)}) async-start(bf16[8,96,512]{2,1,0:T(8,128)(2,1)} %get-tuple-element.67), calls=%async_computation | async-start | bytes 1572864 | tf_op jit(solution)/shard_map/cond/branch_1_fun/all_to_all | solution.py:827
  338.3 110.8 %collective-permute-start = (bf16[256,2048]{1,0:T(8,128)(2,1)}, bf16[256,2048]{1,0:T(8,128)(2,1)}, u32[]{:S(2)}, u32[]{:S(2)}) collective-permute-start(bf16[256,2048]{1,0:T(8,128)(2,1)} %get-tuple-element.60), channel_id=1, source_target_pairs={{0,1},{1,0},{2,3},{3,2},{4,5},{5,4},{6,7},{7,6},{8,9},{9,8},{10,11... | collective-permute-start | bytes 3145736 | tf_op jit(solution)/shard_map/cond/branch_1_fun/ppermute | solution.py:69
  338.4 61.6 %collective-permute-start.4 = (bf16[528,2048]{1,0:T(8,128)(2,1)}, bf16[528,2048]{1,0:T(8,128)(2,1)}, u32[]{:S(2)}, u32[]{:S(2)}) collective-permute-start(bf16[528,2048]{1,0:T(8,128)(2,1)} %get-tuple-element.69), channel_id=1, source_target_pairs={{0,2},{2,0},{4,6},{6,4},{1,3},{3,1},{5,7},{7,5},{8,10},{10,8},{12,... | collective-permute-start | bytes 6488072 | tf_op jit(solution)/shard_map/cond/branch_1_fun/ppermute | solution.py:829
  340.0 60.0 %collective-permute-start.5 = (bf16[528,2048]{1,0:T(8,128)(2,1)}, bf16[528,2048]{1,0:T(8,128)(2,1)}, u32[]{:S(2)}, u32[]{:S(2)}) collective-permute-start(bf16[528,2048]{1,0:T(8,128)(2,1)} %get-tuple-element.70), channel_id=1, source_target_pairs={{2,4},{4,2},{6,0},{0,6},{3,5},{5,3},{7,1},{1,7},{10,12},{12,10},{1... | collective-permute-start | bytes 6488072 | tf_op jit(solution)/shard_map/cond/branch_1_fun/ppermute | solution.py:830
  351.4 92.0 %collective-permute-start.6 = (bf16[528,2048]{1,0:T(8,128)(2,1)}, bf16[528,2048]{1,0:T(8,128)(2,1)}, u32[]{:S(2)}, u32[]{:S(2)}) collective-permute-start(bf16[528,2048]{1,0:T(8,128)(2,1)} %get-tuple-element.72), channel_id=1, source_target_pairs={{0,4},{4,0},{2,6},{6,2},{1,5},{5,1},{3,7},{7,3},{8,12},{12,8},{10,... | collective-permute-start | bytes 6488072 | tf_op jit(solution)/shard_map/cond/branch_1_fun/ppermute | solution.py:841
  356.7 27.0 %all-to-all-start.1 = ((bf16[16,80,128]{2,1,0:T(8,128)(2,1)}), bf16[16,80,128]{2,1,0:T(8,128)(2,1)S(1)}, u32[]{:S(2)}, u32[]{:S(2)}) async-start(bf16[16,80,128]{2,1,0:T(8,128)(2,1)} %maximum_bitcast_fusion), calls=%async_computation.1 | async-start | bytes 655360 | tf_op jit(solution)/shard_map/cond/branch_1_fun/all_to_all | solution.py:86
  366.2 89.6 %collective-permute-start.8 = (bf16[256,2048]{1,0:T(8,128)(2,1)}, bf16[256,2048]{1,0:T(8,128)(2,1)}, u32[]{:S(2)}, u32[]{:S(2)}) collective-permute-start(bf16[256,2048]{1,0:T(8,128)(2,1)} %fusion), channel_id=1, source_target_pairs={{0,1},{1,0},{2,3},{3,2},{4,5},{5,4},{6,7},{7,6},{8,9},{9,8},{10,11... | collective-permute-start | bytes 3145736 | tf_op jit(solution)/shard_map/cond/branch_1_fun/ppermute | solution.py:69
  384.5 15.4 %all-to-all-start.2 = ((bf16[16,80,128]{2,1,0:T(8,128)(2,1)}), bf16[16,80,128]{2,1,0:T(8,128)(2,1)S(1)}, u32[]{:S(2)}, u32[]{:S(2)}) async-start(bf16[16,80,128]{2,1,0:T(8,128)(2,1)} %broadcast_in_dim.14), calls=%async_computation.2 | async-start | bytes 655360 | tf_op jit(solution)/shard_map/cond/branch_1_fun/all_to_all | solution.py:88
  444.7 27.3 %all-to-all-start.3 = ((bf16[4,1280,128]{2,1,0:T(8,128)(2,1)}), bf16[4,1280,128]{2,1,0:T(8,128)(2,1)}, u32[]{:S(2)}, u32[]{:S(2)}) async-start(bf16[4,1280,128]{2,1,0:T(8,128)(2,1)} %broadcast_in_dim.16), calls=%async_computation.3 | async-start | bytes 2621440 | tf_op jit(solution)/shard_map/cond/branch_1_fun/all_to_all | solution.py:40
  452.1 19.9 %collective-permute-start.3 = (bf16[64,2048]{1,0:T(8,128)(2,1)}, bf16[64,2048]{1,0:T(8,128)(2,1)S(1)}, u32[]{:S(2)}, u32[]{:S(2)}) collective-permute-start(bf16[64,2048]{1,0:T(8,128)(2,1)} %get-tuple-element.226), channel_id=1, source_target_pairs={{0,4},{4,0},{2,6},{6,2},{1,5},{5,1},{3,7},{7,3},{8,12},{12,8},{10,... | collective-permute-start | bytes 786440 | tf_op jit(solution)/shard_map/cond/branch_1_fun/ppermute | solution.py:77
  455.0 22.5 %collective-permute-start.2 = (bf16[64,2048]{1,0:T(8,128)(2,1)}, bf16[64,2048]{1,0:T(8,128)(2,1)S(1)}, u32[]{:S(2)}, u32[]{:S(2)}) collective-permute-start(bf16[64,2048]{1,0:T(8,128)(2,1)} %get-tuple-element.227), channel_id=1, source_target_pairs={{2,4},{4,2},{6,0},{0,6},{3,5},{5,3},{7,1},{1,7},{10,12},{12,10},{1... | collective-permute-start | bytes 786440 | tf_op jit(solution)/shard_map/cond/branch_1_fun/ppermute | solution.py:77
  455.9 28.7 %collective-permute-start.1 = (bf16[64,2048]{1,0:T(8,128)(2,1)}, bf16[64,2048]{1,0:T(8,128)(2,1)S(1)}, u32[]{:S(2)}, u32[]{:S(2)}) collective-permute-start(bf16[64,2048]{1,0:T(8,128)(2,1)} %get-tuple-element.225), channel_id=1, source_target_pairs={{0,2},{2,0},{4,6},{6,4},{1,3},{3,1},{5,7},{7,5},{8,10},{10,8},{12,... | collective-permute-start | bytes 786440 | tf_op jit(solution)/shard_map/cond/branch_1_fun/ppermute | solution.py:77
  458.8 27.2 %collective-permute-start.11 = (bf16[64,2048]{1,0:T(8,128)(2,1)}, bf16[64,2048]{1,0:T(8,128)(2,1)}, u32[]{:S(2)}, u32[]{:S(2)}) collective-permute-start(bf16[64,2048]{1,0:T(8,128)(2,1)} %get-tuple-element.223), channel_id=1, source_target_pairs={{0,4},{4,0},{2,6},{6,2},{1,5},{5,1},{3,7},{7,3},{8,12},{12,8},{10,... | collective-permute-start | bytes 786440 | tf_op jit(solution)/shard_map/cond/branch_1_fun/ppermute | solution.py:77
  461.8 27.0 %collective-permute-start.10 = (bf16[64,2048]{1,0:T(8,128)(2,1)S(1)}, bf16[64,2048]{1,0:T(8,128)(2,1)}, u32[]{:S(2)}, u32[]{:S(2)}) collective-permute-start(bf16[64,2048]{1,0:T(8,128)(2,1)S(1)} %get-tuple-element.224), channel_id=1, source_target_pairs={{2,4},{4,2},{6,0},{0,6},{3,5},{5,3},{7,1},{1,7},{10,12},{12,10},{1... | collective-permute-start | bytes 786440 | tf_op jit(solution)/shard_map/cond/branch_1_fun/ppermute | solution.py:77
  472.0 16.7 %collective-permute-start.9 = (bf16[64,2048]{1,0:T(8,128)(2,1)S(1)}, bf16[64,2048]{1,0:T(8,128)(2,1)S(1)}, u32[]{:S(2)}, u32[]{:S(2)}) collective-permute-start(bf16[64,2048]{1,0:T(8,128)(2,1)S(1)} %get-tuple-element.222), channel_id=1, source_target_pairs={{0,2},{2,0},{4,6},{6,4},{1,3},{3,1},{5,7},{7,5},{8,10},{10,8},{12,... | collective-permute-start | bytes 786440 | tf_op jit(solution)/shard_map/cond/branch_1_fun/ppermute | solution.py:77
  477.4 15.4 %collective-permute-start.7 = (bf16[4,1280,128]{2,1,0:T(8,128)(2,1)}, bf16[4,1280,128]{2,1,0:T(8,128)(2,1)S(1)}, u32[]{:S(2)}, u32[]{:S(2)}) collective-permute-start(bf16[4,1280,128]{2,1,0:T(8,128)(2,1)} %all-to-all-done.3), channel_id=1, source_target_pairs={{0,1},{1,0},{2,3},{3,2},{4,5},{5,4},{6,7},{7,6},{8,9},{9,8},{10,11... | collective-permute-start | bytes 3932168 | tf_op jit(solution)/shard_map/cond/branch_1_fun/ppermute | solution.py:42
  (102 other events, 649.8 us)
Sparse Core Ops, SparseCore 0:
  9.8 35.5 all-gather.3
  95.4 26.9 all-gather.5
  269.3 22.6 all-gather.7
  324.5 133.7 all-reduce.5

commit v3 on v2

--- a/solution.py
+++ b/solution.py
@@ -828,11 +828,16 @@
         slices = total_of(tiles).astype(jnp.bfloat16)
         pair_grads = lax.ppermute(grads_sent[0], "y", PAIRS)
         cross_grads = lax.ppermute(grads_sent[1], "y", CROSS)
-        grad_normed_one = sum_rows_directly(kept, given)
         act_parts = parts_of(shared_act)
-        routed_and_shared = sum_rows_directly(
-            *(matmul(a, returned) + matmul(b, shared_down) for a, b in zip(slot_parts, act_parts))
-        )
+        both_sums = sum_rows_directly(
+            *(
+                jnp.concatenate(
+                    [c, (matmul(a, returned) + matmul(b, shared_down)).astype(jnp.bfloat16)], axis=1
+                )
+                for a, b, c in zip(slot_parts, act_parts, (kept, given))
+            )
+        )
+        grad_normed_one, routed_and_shared = both_sums[:, :D], both_sums[:, D:]
         output = (residual + routed_and_shared).astype(jnp.bfloat16)
         grad_from_first, _ = norm_backward(
             own(input_full), own(factor_one), attn_gain, grad_normed_one
@@ -851,7 +856,7 @@
             same.reshape(1), block_grads[0], taken_grads, pair_grads, cross_grads, far_grads
         )
         replicated = after(
-            replicated, pair_grads, cross_grads, far_grads
+            replicated, pair_grads
         )
         replicated = gather_rows_directly(
             replicated.reshape(RANKS * 80, D // RANKS), first_core, expert_grads
@@ -862,16 +867,21 @@
         last_sums, routes[0, 0] >= 0
     )
     replicated = replicated.reshape(parts, RANKS, 80, D // RANKS)
-    replicated = jnp.swapaxes(replicated, 1, 2).reshape(parts, 80, D).astype(jnp.float32)
-    grad_w_kv_down = jnp.swapaxes(replicated[:, :kv_share].reshape(-1, D), 0, 1)
-    others = replicated[:, kv_share:]
+
+    def unpacked(first, last):
+        piece = jnp.swapaxes(replicated[:, :, first:last], 1, 2)
+        return piece.reshape(parts, last - first, D).astype(jnp.float32)
+
+    grad_w_kv_down = jnp.swapaxes(unpacked(0, kv_share).reshape(-1, D), 0, 1)
     router_rows = experts_total * columns // D
     grad_w_router = (
-        jnp.swapaxes(others[:, :router_rows].reshape(parts, experts_total, columns), 0, 1)
+        jnp.swapaxes(
+            unpacked(kv_share, kv_share + router_rows).reshape(parts, experts_total, columns), 0, 1
+        )
         .reshape(experts_total, D)
         .T
     )
-    gains = others[:, router_rows]
+    gains = unpacked(kv_share + router_rows, kv_share + router_rows + 1)[:, 0]
     grad_attn_gain = gains[:, :columns].reshape(D)
     grad_ffn_gain = gains[:, columns : 2 * columns].reshape(D)
     grad_kv_gain = gains[:, 2 * columns : 2 * columns + KV_RANK // parts].reshape(KV_RANK)

time: 528 us -> 520 us (0.985)
  starting transfers between devices: 86.5 us -> 77.1 us
  waiting for transfers between devices: 175 us -> 184 us
  loops' own time: 12.1 us -> 6.53 us
    ppermute x12 -> x9, waiting for transfers between devices: 31.4 us -> 40.4 us  [sum_rows_directly(): total = total + lax.ppermute(tile, 'y', pairs).astype(jnp.float32)]
    ppermute x1, waiting for transfers between devices: 43.4 us -> 36.7 us  [last_sums(): far_grads = lax.ppermute(after(grads_sent[2], slices), 'y', OPPOSITE)]
    ppermute x1, starting transfers between devices: 7.14 us -> 1.04 us  [gather_rows_directly(): other = lax.ppermute(mine, 'core', SWAP)]
    another operation x1, loops' own time: 12.1 us -> 6.53 us  [as_unit(): lax.cond(always, work, lambda: jax.tree.map(lambda a: jnp.zeros(a.shape,...]
    unnamed x174 -> x185, local copies, waits for them, and re-layouts: 7.17 us -> 11.9 us
    ppermute x12 -> x9, starting transfers between devices: 13.5 us -> 10.5 us  [sum_rows_directly(): total = total + lax.ppermute(tile, 'y', pairs).astype(jnp.float32)]
  transfers between devices with their start and end apart: 40 -> 36, of which waited for: 18 -> 23; matrix products, arithmetic and copies ran while one was open for 20% -> 20% of each run, Pallas kernels for 12% -> 12%
where the time goes in v3:
time: 520 us; the launch traced here: 512 us
  waiting for transfers between devices  184 us (35%)
  Pallas kernels  88.5 us (17%)
  starting transfers between devices  77.1 us (15%)
  other arithmetic  62.6 us (12%)
  matrix products  40.9 us (8%)
  local copies, waits for them, and re-layouts  30.7 us (6%)
  between operations  22 us (4%)
  loops' own time  6.53 us (1%)
    ppermute x9, waiting for transfers between devices, sum_rows_directly(): total = total + lax.ppermute(tile, 'y', pairs).astype(jnp.float32)  40.4 us
    all_gather x3, waiting for transfers between devices, gather_rows(): return lax.all_gather(x, GROUP, axis=0, tiled=True)  39.4 us
    ppermute x1, waiting for transfers between devices, last_sums(): far_grads = lax.ppermute(after(grads_sent[2], slices), 'y', OPPOSITE)  36.7 us
    pallas_call x1, Pallas kernels, expert_rows(): pl.pallas_call(expert_kernel, out_shape=(jax.ShapeDtypeStruct(x.shape, bf...  25.5 us
    all_to_all x4, starting transfers between devices, to_owners(): lax.all_to_all(x.reshape(RANKS, x.shape[0] // RANKS, x.shape[1]), EXPERT,...  24.1 us
    dot_general x12, matrix products, matmul(): return jnp.dot(left, right, preferred_element_type=jnp.float32)  22.5 us
    all_to_all x4, waiting for transfers between devices, to_owners(): lax.all_to_all(x.reshape(RANKS, x.shape[0] // RANKS, x.shape[1]), EXPERT,...  22.4 us
    pallas_call x1, Pallas kernels, expert_weights(): pl.pallas_call(expert_weights_kernel, out_shape=(jax.ShapeDtypeStruct((sl...  21.5 us
  transfers between devices with their start and end apart: 36, of which 23 were waited for; matrix products, arithmetic and copies ran while one was open for 20% of the time, Pallas kernels for 12%

profile of v3, /device:TPU:1, one launch (start us, length us, event | category | flops | bytes accessed | tf_op | source)
XLA Modules:
  0.0 512.0 jit_solution(1101741539718261507)
XLA Ops:
  45.4 4.3 convolution_convert_fusion.1
  49.7 19.3 %collective-permute-done.8.refs_4_.refs_6_ = bf16[528,2048]{1,0:T(8,128)(2,1)} collective-permute-done((bf16[528,2048]{1,0:T(8,128)(2,1)}, bf16[528,2048]{1,0:T(8,128)(2,1)}, u32[]{:S(2)}, u32[]{:S(2)}) %collective-permute-start.8) | collective-permute-done | bytes 2162720 | tf_op jit(solution)/shard_map/ppermute | solution.py:588
  68.9 3.9 collective-permute-done.9.refs_5_.refs_7_
  84.0 6.0 %collective-permute-done.13 = bf16[64,2048]{1,0:T(8,128)(2,1)} collective-permute-done((bf16[64,2048]{1,0:T(8,128)(2,1)}, bf16[64,2048]{1,0:T(8,128)(2,1)}, u32[]{:S(2)}, u32[]{:S(2)}) %collective-permute-start.13) | collective-permute-done | bytes 262176 | tf_op jit(solution)/shard_map/ppermute | solution.py:77
  93.3 7.7 %all-to-all-start.4 = ((bf16[16,32,2048]{2,1,0:T(8,128)(2,1)}), bf16[16,32,2048]{2,1,0:T(8,128)(2,1)S(1)}, u32[]{:S(2)}, u32[]{:S(2)}) async-start(bf16[16,32,2048]{2,1,0:T(8,128)(2,1)} %bitcast.262), calls=%async_computation.4 | async-start | bytes 4194304 | tf_op jit(solution)/shard_map/all_to_all | solution.py:160
  101.0 21.1 %all-gather.6.cloned.1.call-done.rows_ref = bf16[512,2048]{1,0:T(8,128)(2,1)} async-done(((bf16[64,2048]{1,0:T(8,128)(2,1)}), bf16[512,2048]{1,0:T(8,128)(2,1)}) %all-gather.6.cloned.1.call-update) | async-done | bytes 2097168 | tf_op jit(solution)/shard_map/all_gather | solution.py:35
  128.3 5.3 %dispatch.1 = bf16[512,2176]{1,0:T(8,128)(2,1)} custom-call(bf16[512,512]{1,0:T(8,128)(2,1)} %get-tuple-element.261.map_ref, bf16[512,2048]{1,0:T(8,128)(2,1)} %all-gather.6.cloned.1.call-done.rows_ref, bf16[512,128]{1,0:T(8,128)(2,1)} %pad_maximum_fusion.9.tail_ref), custom_call_target="tpu_custom_call" | custom-call | flops 1140850688 | bytes 8388608 | tf_op jit(solution)/shard_map/dispatch/pallas_call | solution.py:204
  134.9 6.8 %all-to-all-start.5 = ((bf16[16,32,2176]{2,1,0:T(8,128)(2,1)}), bf16[16,32,2176]{2,1,0:T(8,128)(2,1)}, u32[]{:S(2)}, u32[]{:S(2)}) async-start(bf16[16,32,2176]{2,1,0:T(8,128)(2,1)} %bitcast.234), calls=%async_computation.5 | async-start | bytes 4456448 | tf_op jit(solution)/shard_map/all_to_all | solution.py:160
  143.1 15.7 %shared_experts.1 = (bf16[352,2048]{1,0:T(8,128)(2,1)}, bf16[352,2048]{1,0:T(8,128)(2,1)}, bf16[352,2048]{1,0:T(8,128)(2,1)}, bf16[512,352]{1,0:T(8,128)(2,1)}, ...) custom-call(s32[1]{0:T(128)} %bitcast.61.core, bf16[512,2048]{1,0:T(8,128)(2,1)} %all-gather.6.cloned.1.call-done.rows_ref, ...), custom_call_target="tpu_custom_call" | custom-call | flops 17999998976 | bytes 20971520 | tf_op jit(solution)/shard_map/shared_experts/pallas_call | solution.py:273
  158.8 13.4 %all-to-all-done.5 = bf16[16,32,2176]{2,1,0:T(8,128)(2,1)} async-done(((bf16[16,32,2176]{2,1,0:T(8,128)(2,1)}), bf16[16,32,2176]{2,1,0:T(8,128)(2,1)}, u32[]{:S(2)}, u32[]{:S(2)}) %all-to-all-start.5) | async-done | bytes 2228256 | tf_op jit(solution)/shard_map/all_to_all | solution.py:160
  179.5 25.5 %expert_rows.1 = (bf16[512,2176]{1,0:T(8,128)(2,1)}, bf16[512,1408]{1,0:T(8,128)(2,1)}, bf16[512,1408]{1,0:T(8,128)(2,1)}, bf16[512,1408]{1,0:T(8,128)(2,1)}) custom-call(s32[1]{0:T(128)} %bitcast.64.refs_0_, bf16[512,2176]{1,0:T(8,128)(2,1)} %bitcast.60.refs_1_.refs_0_, bf16[512,2048]{1,0:T(8,128)(2,1)} %bitcast.260, ...), custom_call_target="tpu_custom_call" | custom-call | flops 14763950080 | bytes 29360128 | tf_op jit(solution)/shard_map/expert_rows/pallas_call | solution.py:452
  205.0 5.1 all-to-all-start.6
  210.1 21.5 %expert_weights.1 = (bf16[512,2048]{1,0:T(8,128)(2,1)}, bf16[528,2048]{1,0:T(8,128)(2,1)}, bf16[528,2048]{1,0:T(8,128)(2,1)}, bf16[528,2048]{1,0:T(8,128)(2,1)},...) custom-call(bf16[512,2176]{1,0:T(8,128)(2,1)} %bitcast.60.refs_1_.refs_0_, bf16[512,2048]{1,0:T(8,128)(2,1)} %bitcast.261, ...), custom_call_target="tpu_custom_call" | custom-call | flops 99999997952 | bytes 35651584 | tf_op jit(solution)/shard_map/expert_weights/pallas_call | solution.py:529
  231.7 9.0 %all-to-all-done.6 = bf16[16,32,2176]{2,1,0:T(8,128)(2,1)S(1)} async-done(((bf16[16,32,2176]{2,1,0:T(8,128)(2,1)}), bf16[16,32,2176]{2,1,0:T(8,128)(2,1)S(1)}, u32[]{:S(2)}, u32[]{:S(2)}) %all-to-all-start.6) | async-done | bytes 2228256 | tf_op jit(solution)/shard_map/all_to_all | solution.py:160
  252.7 4.5 collective-permute-done.20
  258.5 5.6 %collective-permute-done.22 = bf16[64,2176]{1,0:T(8,128)(2,1)S(1)} collective-permute-done((bf16[64,2176]{1,0:T(8,128)(2,1)S(1)}, bf16[64,2176]{1,0:T(8,128)(2,1)S(1)}, u32[]{:S(2)}, u32[]{:S(2)}) %collective-permute-start.22) | collective-permute-done | bytes 278560 | tf_op jit(solution)/shard_map/ppermute | solution.py:77
  271.3 4.5 all-to-all-start.7
  275.8 16.4 %all-gather.8.cloned.1.call-done = bf16[512,2048]{1,0:T(8,128)(2,1)} async-done(((bf16[64,2048]{1,0:T(8,128)(2,1)}), bf16[512,2048]{1,0:T(8,128)(2,1)}) %all-gather.8.cloned.1.call-update) | async-done | bytes 2097168 | tf_op jit(solution)/shard_map/all_gather | solution.py:35
  305.8 8.2 %attention_rows.1 = (bf16[256,2048]{1,0:T(8,128)(2,1)}, bf16[256,2048]{1,0:T(8,128)(2,1)}, f32[1,2048]{1,0:T(1,128)}) custom-call(s32[1]{0:T(128)} %bitcast.61.core, bf16[512,384]{1,0:T(8,128)(2,1)} %copy.194.query_ref, bf16[512,576]{1,0:T(8,128)(2,1)} %pad_maximum_fusion.5.compressed_ref, bf16[512,2048]{1,0:T(8,128)(2,1)} %x_ref.1, ...), custom_call_target="tpu_custom_call" | custom-call | flops 99999997952 | bytes 10485760 | tf_op jit(solution)/shard_map/attention_rows/pallas_call | solution.py:367
  323.6 7.1 %add_convert_fusion.1 = (bf16[528,2048]{1,0:T(8,128)(2,1)}, bf16[528,2048]{1,0:T(8,128)(2,1)}, bf16[528,2048]{1,0:T(8,128)(2,1)}) fusion(bf16[528,2048]{1,0:T(8,128)(2,1)} %get-tuple-element.147, bf16[2112,2048]{1,0:T(8,128)(2,1)} %collective-permute-done.23, bf16[528,2048]{1,0:T(8,128)(2,1)} %get-tuple-element.146, bf16[528,2048]{1,0:T(8,128)(2,1)S(1)} %copy-done.23), kind=kLoop, calls=%fused_computation.30 | loop fusion | flops 12976128 | bytes 19464192 | tf_op jit(solution)/shard_map/convert_element_type | solution.py:706
  330.8 154.3 %conditional.1 = (f32[64,2048]{1,0:T(8,128)}, bf16[10240,128]{1,0:T(8,128)(2,1)S(1)}, bf16[64,2048]{1,0:T(8,128)(2,1)}, f32[2,176,2048]{2,1,0:T(8,128)}, f32[2,1...) conditional(s32[]{:T(128)} %bitcast.20, () %tuple.28, (s32[]{:T(128)}, f32[512,1]{0,1:T(1,128)}, ...), branch_computations={%region_12.13_spmd, %region_13.17_spmd} | conditional | flops 101833129984 | bytes 149835328 | solution.py:49
  354.8 6.6 %all-to-all-start.1 = ((bf16[16,80,128]{2,1,0:T(8,128)(2,1)}), bf16[16,80,128]{2,1,0:T(8,128)(2,1)S(1)}, u32[]{:S(2)}, u32[]{:S(2)}) async-start(bf16[16,80,128]{2,1,0:T(8,128)(2,1)} %maximum_bitcast_fusion), calls=%async_computation.1 | async-start | bytes 655360 | tf_op jit(solution)/shard_map/cond/branch_1_fun/all_to_all | solution.py:86
  373.0 6.6 %all-to-all-start.2 = ((bf16[16,80,128]{2,1,0:T(8,128)(2,1)}), bf16[16,80,128]{2,1,0:T(8,128)(2,1)S(1)}, u32[]{:S(2)}, u32[]{:S(2)}) async-start(bf16[16,80,128]{2,1,0:T(8,128)(2,1)} %broadcast_in_dim.14), calls=%async_computation.2 | async-start | bytes 655360 | tf_op jit(solution)/shard_map/cond/branch_1_fun/all_to_all | solution.py:88
  382.5 6.3 %all-to-all-done.2 = bf16[16,80,128]{2,1,0:T(8,128)(2,1)S(1)} async-done(((bf16[16,80,128]{2,1,0:T(8,128)(2,1)}), bf16[16,80,128]{2,1,0:T(8,128)(2,1)S(1)}, u32[]{:S(2)}, u32[]{:S(2)}) %all-to-all-start.2) | async-done | bytes 327712 | tf_op jit(solution)/shard_map/cond/branch_1_fun/all_to_all | solution.py:88
  388.9 3.7 collective-permute-done.4.pair
  393.9 4.3 all-to-all-start.3
  403.9 36.7 %collective-permute-done.6.far = bf16[528,2048]{1,0:T(8,128)(2,1)} collective-permute-done((bf16[528,2048]{1,0:T(8,128)(2,1)}, bf16[528,2048]{1,0:T(8,128)(2,1)}, u32[]{:S(2)}, u32[]{:S(2)}) %collective-permute-start.6) | collective-permute-done | bytes 2162720 | tf_op jit(solution)/shard_map/cond/branch_1_fun/ppermute | solution.py:846
  440.6 9.5 %expert_outputs.1 = (f32[2,176,2048]{2,1,0:T(8,128)}, f32[2,176,2048]{2,1,0:T(8,128)}, f32[2,176,2048]{2,1,0:T(8,128)}) custom-call(s32[1]{0:T(128)} %bitcast.15.same, bf16[528,2048]{1,0:T(8,128)(2,1)} %get-tuple-element.71.own, bf16[2112,2048]{1,0:T(8,128)(2,1)} %get-tuple-element.72.taken_hbm, bf16[528,2048]{1,0:T(8,128)(2,1)} %collective-permute-done.4.pair, ...), custom_call_target="tpu_custom_call" | custom-call | bytes 20971520 | tf_op jit(solution)/shard_map/cond/branch_1_fun/expert_outputs/pallas_call | solution.py:303
  450.1 4.8 all-to-all-done.3
  455.9 8.4 %collective-permute-done.1 = bf16[64,4096]{1,0:T(8,128)(2,1)} collective-permute-done((bf16[64,4096]{1,0:T(8,128)(2,1)}, bf16[64,4096]{1,0:T(8,128)(2,1)}, u32[]{:S(2)}, u32[]{:S(2)}) %collective-permute-start.1) | collective-permute-done | bytes 524320 | tf_op jit(solution)/shard_map/cond/branch_1_fun/ppermute | solution.py:77
  466.8 10.4 %collective-permute-done.3 = bf16[64,4096]{1,0:T(8,128)(2,1)} collective-permute-done((bf16[64,4096]{1,0:T(8,128)(2,1)S(1)}, bf16[64,4096]{1,0:T(8,128)(2,1)}, u32[]{:S(2)}, u32[]{:S(2)}) %collective-permute-start.3) | collective-permute-done | bytes 524320 | tf_op jit(solution)/shard_map/cond/branch_1_fun/ppermute | solution.py:77
  485.8 4.4 copy.239
  (384 shorter events, 170.8 us)
Async XLA Ops:
  7.2 38.2 %all-gather.4.cloned.1.call-start = ((), (), s32[]{:S(2)}) async-start(), calls=%async_computation.8 | async-start | bytes 2359296 | tf_op jit(solution)/shard_map/all_gather | solution.py:35
  7.9 114.1 %all-gather.6.cloned.1.call-start = ((), (), s32[]{:S(2)}) async-start(), calls=%async_computation.9 | async-start | bytes 2359296 | tf_op jit(solution)/shard_map/all_gather | solution.py:35
  11.7 57.2 %collective-permute-start.8 = (bf16[528,2048]{1,0:T(8,128)(2,1)}, bf16[528,2048]{1,0:T(8,128)(2,1)}, u32[]{:S(2)}, u32[]{:S(2)}) collective-permute-start(bf16[528,2048]{1,0:T(8,128)(2,1)} %pad_maximum_fusion.2.refs_3_.refs_5_), channel_id=1, source_target_pairs={{0,2},{2,0},{4,6},{6,4},{1,3},{3,1},{5,7},{7,5},{8,10},{10,8},{12,... | collective-permute-start | bytes 6488072 | tf_op jit(solution)/shard_map/ppermute | solution.py:588
  15.3 57.5 %collective-permute-start.9 = (bf16[528,2048]{1,0:T(8,128)(2,1)}, bf16[528,2048]{1,0:T(8,128)(2,1)}, u32[]{:S(2)}, u32[]{:S(2)}) collective-permute-start(bf16[528,2048]{1,0:T(8,128)(2,1)} %pad_maximum_fusion.3), channel_id=1, source_target_pairs={{2,4},{4,2},{6,0},{0,6},{3,5},{5,3},{7,1},{1,7},{10,12},{12,10},{1... | collective-permute-start | bytes 6488072 | tf_op jit(solution)/shard_map/ppermute | solution.py:589
  32.6 40.3 %collective-permute-start.10 = (bf16[256,2048]{1,0:T(8,128)(2,1)}, bf16[256,2048]{1,0:T(8,128)(2,1)}, u32[]{:S(2)}, u32[]{:S(2)}) collective-permute-start(bf16[256,2048]{1,0:T(8,128)(2,1)} %bitcast.48), channel_id=1, source_target_pairs={{0,1},{1,0},{2,3},{3,2},{4,5},{5,4},{6,7},{7,6},{8,9},{9,8},{10,11... | collective-permute-start | bytes 3145736 | tf_op jit(solution)/shard_map/ppermute | solution.py:69
  78.4 11.6 %collective-permute-start.13 = (bf16[64,2048]{1,0:T(8,128)(2,1)}, bf16[64,2048]{1,0:T(8,128)(2,1)}, u32[]{:S(2)}, u32[]{:S(2)}) collective-permute-start(bf16[64,2048]{1,0:T(8,128)(2,1)} %get-tuple-element.236), channel_id=1, source_target_pairs={{0,4},{4,0},{2,6},{6,2},{1,5},{5,1},{3,7},{7,3},{8,12},{12,8},{10,... | collective-permute-start | bytes 786440 | tf_op jit(solution)/shard_map/ppermute | solution.py:77
  93.3 40.3 %all-to-all-start.4 = ((bf16[16,32,2048]{2,1,0:T(8,128)(2,1)}), bf16[16,32,2048]{2,1,0:T(8,128)(2,1)S(1)}, u32[]{:S(2)}, u32[]{:S(2)}) async-start(bf16[16,32,2048]{2,1,0:T(8,128)(2,1)} %bitcast.262), calls=%async_computation.4 | async-start | bytes 4194304 | tf_op jit(solution)/shard_map/all_to_all | solution.py:160
  122.1 50.2 %collective-permute-start.14 = (bf16[528,2048]{1,0:T(8,128)(2,1)}, bf16[528,2048]{1,0:T(8,128)(2,1)}, u32[]{:S(2)}, u32[]{:S(2)}) collective-permute-start(bf16[528,2048]{1,0:T(8,128)(2,1)} %pad_maximum_fusion.3), channel_id=1, source_target_pairs={{0,4},{4,0},{2,6},{6,2},{1,5},{5,1},{3,7},{7,3},{8,12},{12,8},{10,... | collective-permute-start | bytes 6488072 | tf_op jit(solution)/shard_map/ppermute | solution.py:666
  134.9 37.3 %all-to-all-start.5 = ((bf16[16,32,2176]{2,1,0:T(8,128)(2,1)}), bf16[16,32,2176]{2,1,0:T(8,128)(2,1)}, u32[]{:S(2)}, u32[]{:S(2)}) async-start(bf16[16,32,2176]{2,1,0:T(8,128)(2,1)} %bitcast.234), calls=%async_computation.5 | async-start | bytes 4456448 | tf_op jit(solution)/shard_map/all_to_all | solution.py:160
  141.7 34.3 %collective-permute-start.15 = (bf16[528,2048]{1,0:T(8,128)(2,1)}, bf16[528,2048]{1,0:T(8,128)(2,1)}, u32[]{:S(2)}, u32[]{:S(2)}) collective-permute-start(bf16[528,2048]{1,0:T(8,128)(2,1)} %pad_maximum_fusion.2.refs_3_.refs_5_), channel_id=1, source_target_pairs={{0,1},{1,0},{2,3},{3,2},{4,5},{5,4},{6,7},{7,6},{8,9},{9,8},{10,11... | collective-permute-start | bytes 6488072 | tf_op jit(solution)/shard_map/ppermute | solution.py:691
  142.6 33.4 %collective-permute-start.16 = (bf16[528,2048]{1,0:T(8,128)(2,1)}, bf16[528,2048]{1,0:T(8,128)(2,1)}, u32[]{:S(2)}, u32[]{:S(2)}) collective-permute-start(bf16[528,2048]{1,0:T(8,128)(2,1)} %collective-permute-done.8.refs_4_.refs_6_), channel_id=1, source_target_pairs={{0,1},{1,0},{2,3},{3,2},{4,5},{5,4},{6,7},{7,6},{8,9},{9,8},{10,11... | collective-permute-start | bytes 6488072 | tf_op jit(solution)/shard_map/ppermute | solution.py:691
  142.7 33.3 %collective-permute-start.17 = (bf16[528,2048]{1,0:T(8,128)(2,1)}, bf16[528,2048]{1,0:T(8,128)(2,1)}, u32[]{:S(2)}, u32[]{:S(2)}) collective-permute-start(bf16[528,2048]{1,0:T(8,128)(2,1)} %collective-permute-done.9.refs_5_.refs_7_), channel_id=1, source_target_pairs={{0,1},{1,0},{2,3},{3,2},{4,5},{5,4},{6,7},{7,6},{8,9},{9,8},{10,11... | collective-permute-start | bytes 6488072 | tf_op jit(solution)/shard_map/ppermute | solution.py:691
  205.0 35.8 %all-to-all-start.6 = ((bf16[16,32,2176]{2,1,0:T(8,128)(2,1)}), bf16[16,32,2176]{2,1,0:T(8,128)(2,1)S(1)}, u32[]{:S(2)}, u32[]{:S(2)}) async-start(bf16[16,32,2176]{2,1,0:T(8,128)(2,1)} %bitcast.254), calls=%async_computation.6 | async-start | bytes 4456448 | tf_op jit(solution)/shard_map/all_to_all | solution.py:160
  210.1 82.1 %all-gather.8.cloned.1.call-start = ((), (), s32[]{:S(2)}) async-start(), calls=%async_computation.10 | async-start | bytes 2359296 | tf_op jit(solution)/shard_map/all_gather | solution.py:35
  249.2 8.0 %collective-permute-start.20 = (bf16[64,2176]{1,0:T(8,128)(2,1)S(1)}, bf16[64,2176]{1,0:T(8,128)(2,1)S(1)}, u32[]{:S(2)}, u32[]{:S(2)}) collective-permute-start(bf16[64,2176]{1,0:T(8,128)(2,1)S(1)} %get-tuple-element.232), channel_id=1, source_target_pairs={{0,2},{2,0},{4,6},{6,4},{1,3},{3,1},{5,7},{7,5},{8,10},{10,8},{12,... | collective-permute-start | bytes 835592 | tf_op jit(solution)/shard_map/ppermute | solution.py:77
  249.3 9.2 %collective-permute-start.21 = (bf16[64,2176]{1,0:T(8,128)(2,1)S(1)}, bf16[64,2176]{1,0:T(8,128)(2,1)S(1)}, u32[]{:S(2)}, u32[]{:S(2)}) collective-permute-start(bf16[64,2176]{1,0:T(8,128)(2,1)S(1)} %get-tuple-element.234), channel_id=1, source_target_pairs={{2,4},{4,2},{6,0},{0,6},{3,5},{5,3},{7,1},{1,7},{10,12},{12,10},{1... | collective-permute-start | bytes 835592 | tf_op jit(solution)/shard_map/ppermute | solution.py:77
  251.4 12.7 %collective-permute-start.22 = (bf16[64,2176]{1,0:T(8,128)(2,1)S(1)}, bf16[64,2176]{1,0:T(8,128)(2,1)S(1)}, u32[]{:S(2)}, u32[]{:S(2)}) collective-permute-start(bf16[64,2176]{1,0:T(8,128)(2,1)S(1)} %get-tuple-element.233), channel_id=1, source_target_pairs={{0,4},{4,0},{2,6},{6,2},{1,5},{5,1},{3,7},{7,3},{8,12},{12,8},{10,... | collective-permute-start | bytes 835592 | tf_op jit(solution)/shard_map/ppermute | solution.py:77
  268.6 55.0 %collective-permute-start.23 = (bf16[2112,2048]{1,0:T(8,128)(2,1)}, bf16[2112,2048]{1,0:T(8,128)(2,1)}, u32[]{:S(2)}, u32[]{:S(2)}) collective-permute-start(bf16[2112,2048]{1,0:T(8,128)(2,1)} %get-tuple-element.148), channel_id=1, source_target_pairs={{0,1},{1,0},{2,3},{3,2},{4,5},{5,4},{6,7},{7,6},{8,9},{9,8},{10,11... | collective-permute-start | bytes 25952264 | tf_op jit(solution)/shard_map/ppermute | solution.py:701
  271.3 50.3 %all-to-all-start.7 = ((bf16[16,32,2048]{2,1,0:T(8,128)(2,1)}), bf16[16,32,2048]{2,1,0:T(8,128)(2,1)}, u32[]{:S(2)}, u32[]{:S(2)}) async-start(bf16[16,32,2048]{2,1,0:T(8,128)(2,1)} %bitcast.259), calls=%async_computation.7 | async-start | bytes 4194304 | tf_op jit(solution)/shard_map/all_to_all | solution.py:160
  275.7 217.5 %all-reduce.6.cloned.1.call-start = ((), (), s32[]{:S(2)}) async-start(), calls=%async_computation.11 | async-start | bytes 14942208 | tf_op jit(solution)/shard_map/psum | solution.py:791
  331.7 16.8 %all-to-all-start = ((bf16[8,96,512]{2,1,0:T(8,128)(2,1)}), bf16[8,96,512]{2,1,0:T(8,128)(2,1)S(1)}, u32[]{:S(2)}, u32[]{:S(2)}) async-start(bf16[8,96,512]{2,1,0:T(8,128)(2,1)} %get-tuple-element.66), calls=%async_computation | async-start | bytes 1572864 | tf_op jit(solution)/shard_map/cond/branch_1_fun/all_to_all | solution.py:827
  342.4 37.1 %collective-permute-start = (bf16[256,4096]{1,0:T(8,128)(2,1)}, bf16[256,4096]{1,0:T(8,128)(2,1)}, u32[]{:S(2)}, u32[]{:S(2)}) collective-permute-start(bf16[256,4096]{1,0:T(8,128)(2,1)} %pad_maximum_fusion.1), channel_id=1, source_target_pairs={{0,1},{1,0},{2,3},{3,2},{4,5},{5,4},{6,7},{7,6},{8,9},{9,8},{10,11... | collective-permute-start | bytes 6291464 | tf_op jit(solution)/shard_map/cond/branch_1_fun/ppermute | solution.py:69
  342.6 50.0 %collective-permute-start.4 = (bf16[528,2048]{1,0:T(8,128)(2,1)}, bf16[528,2048]{1,0:T(8,128)(2,1)}, u32[]{:S(2)}, u32[]{:S(2)}) collective-permute-start(bf16[528,2048]{1,0:T(8,128)(2,1)} %get-tuple-element.68), channel_id=1, source_target_pairs={{0,2},{2,0},{4,6},{6,4},{1,3},{3,1},{5,7},{7,5},{8,10},{10,8},{12,... | collective-permute-start | bytes 6488072 | tf_op jit(solution)/shard_map/cond/branch_1_fun/ppermute | solution.py:829
  344.2 59.7 %collective-permute-start.5 = (bf16[528,2048]{1,0:T(8,128)(2,1)}, bf16[528,2048]{1,0:T(8,128)(2,1)}, u32[]{:S(2)}, u32[]{:S(2)}) collective-permute-start(bf16[528,2048]{1,0:T(8,128)(2,1)} %get-tuple-element.73), channel_id=1, source_target_pairs={{2,4},{4,2},{6,0},{0,6},{3,5},{5,3},{7,1},{1,7},{10,12},{12,10},{1... | collective-permute-start | bytes 6488072 | tf_op jit(solution)/shard_map/cond/branch_1_fun/ppermute | solution.py:830
  349.3 91.3 %collective-permute-start.6 = (bf16[528,2048]{1,0:T(8,128)(2,1)}, bf16[528,2048]{1,0:T(8,128)(2,1)}, u32[]{:S(2)}, u32[]{:S(2)}) collective-permute-start(bf16[528,2048]{1,0:T(8,128)(2,1)} %get-tuple-element.75), channel_id=1, source_target_pairs={{0,4},{4,0},{2,6},{6,2},{1,5},{5,1},{3,7},{7,3},{8,12},{12,8},{10,... | collective-permute-start | bytes 6488072 | tf_op jit(solution)/shard_map/cond/branch_1_fun/ppermute | solution.py:846
  354.8 17.4 %all-to-all-start.1 = ((bf16[16,80,128]{2,1,0:T(8,128)(2,1)}), bf16[16,80,128]{2,1,0:T(8,128)(2,1)S(1)}, u32[]{:S(2)}, u32[]{:S(2)}) async-start(bf16[16,80,128]{2,1,0:T(8,128)(2,1)} %maximum_bitcast_fusion), calls=%async_computation.1 | async-start | bytes 655360 | tf_op jit(solution)/shard_map/cond/branch_1_fun/all_to_all | solution.py:86
  373.0 15.9 %all-to-all-start.2 = ((bf16[16,80,128]{2,1,0:T(8,128)(2,1)}), bf16[16,80,128]{2,1,0:T(8,128)(2,1)S(1)}, u32[]{:S(2)}, u32[]{:S(2)}) async-start(bf16[16,80,128]{2,1,0:T(8,128)(2,1)} %broadcast_in_dim.14), calls=%async_computation.2 | async-start | bytes 655360 | tf_op jit(solution)/shard_map/cond/branch_1_fun/all_to_all | solution.py:88
  393.9 60.9 %all-to-all-start.3 = ((bf16[4,1280,128]{2,1,0:T(8,128)(2,1)}), bf16[4,1280,128]{2,1,0:T(8,128)(2,1)}, u32[]{:S(2)}, u32[]{:S(2)}) async-start(bf16[4,1280,128]{2,1,0:T(8,128)(2,1)} %broadcast_in_dim.16), calls=%async_computation.3 | async-start | bytes 2621440 | tf_op jit(solution)/shard_map/cond/branch_1_fun/all_to_all | solution.py:40
  399.3 65.0 %collective-permute-start.1 = (bf16[64,4096]{1,0:T(8,128)(2,1)}, bf16[64,4096]{1,0:T(8,128)(2,1)}, u32[]{:S(2)}, u32[]{:S(2)}) collective-permute-start(bf16[64,4096]{1,0:T(8,128)(2,1)} %get-tuple-element.210), channel_id=1, source_target_pairs={{0,2},{2,0},{4,6},{6,4},{1,3},{3,1},{5,7},{7,5},{8,10},{10,8},{12,... | collective-permute-start | bytes 1572872 | tf_op jit(solution)/shard_map/cond/branch_1_fun/ppermute | solution.py:77
  400.8 66.1 %collective-permute-start.2 = (bf16[64,4096]{1,0:T(8,128)(2,1)}, bf16[64,4096]{1,0:T(8,128)(2,1)}, u32[]{:S(2)}, u32[]{:S(2)}) collective-permute-start(bf16[64,4096]{1,0:T(8,128)(2,1)} %get-tuple-element.212), channel_id=1, source_target_pairs={{2,4},{4,2},{6,0},{0,6},{3,5},{5,3},{7,1},{1,7},{10,12},{12,10},{1... | collective-permute-start | bytes 1572872 | tf_op jit(solution)/shard_map/cond/branch_1_fun/ppermute | solution.py:77
  402.5 74.7 %collective-permute-start.3 = (bf16[64,4096]{1,0:T(8,128)(2,1)S(1)}, bf16[64,4096]{1,0:T(8,128)(2,1)}, u32[]{:S(2)}, u32[]{:S(2)}) collective-permute-start(bf16[64,4096]{1,0:T(8,128)(2,1)S(1)} %get-tuple-element.211), channel_id=1, source_target_pairs={{0,4},{4,0},{2,6},{6,2},{1,5},{5,1},{3,7},{7,3},{8,12},{12,8},{10,... | collective-permute-start | bytes 1572872 | tf_op jit(solution)/shard_map/cond/branch_1_fun/ppermute | solution.py:77
  454.8 28.1 %collective-permute-start.7 = (bf16[4,1280,128]{2,1,0:T(8,128)(2,1)}, bf16[4,1280,128]{2,1,0:T(8,128)(2,1)S(1)}, u32[]{:S(2)}, u32[]{:S(2)}) collective-permute-start(bf16[4,1280,128]{2,1,0:T(8,128)(2,1)} %all-to-all-done.3), channel_id=1, source_target_pairs={{0,1},{1,0},{2,3},{3,2},{4,5},{5,4},{6,7},{7,6},{8,9},{9,8},{10,11... | collective-permute-start | bytes 3932168 | tf_op jit(solution)/shard_map/cond/branch_1_fun/ppermute | solution.py:42
  (100 other events, 534.1 us)
Sparse Core Ops, SparseCore 0:
  9.8 35.5 all-gather.3
  93.4 28.6 all-gather.5
  267.9 24.2 all-gather.7
  321.7 135.7 all-reduce.5

commit v4 on v3

--- a/solution.py
+++ b/solution.py
@@ -699,13 +699,6 @@
     back = after(to_owners(back), *block_grads)
 
     taken_grads = lax.ppermute(block_grads[RINGS], "core", SWAP)
-    grads_sent = [
-        (
-            block_grads[r].astype(jnp.float32)
-            + taken_grads[3 * HIDDEN * r : 3 * HIDDEN * (r + 1)].astype(jnp.float32)
-        ).astype(jnp.bfloat16)
-        for r in range(1, RINGS)
-    ]
 
     summed = sum_rows_directly(
         *(
@@ -824,6 +817,11 @@
     bundle = after(bundle, returned, *local_grads)
 
     def last_sums():
+        grads_sent, taken = [], taken_grads
+        for r in range(1, RINGS):
+            part = taken[3 * HIDDEN * r : 3 * HIDDEN * (r + 1)].astype(jnp.float32)
+            grads_sent.append((block_grads[r].astype(jnp.float32) + part).astype(jnp.bfloat16))
+            taken = after(taken_grads, grads_sent[-1])
         tiles = lax.all_to_all(bundle, GROUP, 0, 0, tiled=True)
         slices = total_of(tiles).astype(jnp.bfloat16)
         pair_grads = lax.ppermute(grads_sent[0], "y", PAIRS)

time: 520 us -> 514 us (0.988)
  waiting for transfers between devices: 184 us -> 171 us
    ppermute x1, waiting for transfers between devices: 36.7 us -> 0.01 us  [last_sums(): far_grads = lax.ppermute(after(grads_sent[2], slices), 'y', OPPOSITE)]
    ppermute x1, waiting for transfers between devices: 0.01 us -> 30.5 us  [last_sums(): cross_grads = lax.ppermute(grads_sent[1], 'y', CROSS)]
    convert_element_type x1 -> x3, other arithmetic: 7.12 us -> 12.6 us  [last_sums(): (block_grads[r].astype(jnp.float32) + part).astype(jnp.bfloat16)]
    unnamed x185 -> x183, local copies, waits for them, and re-layouts: 11.9 us -> 11.8 us
  transfers between devices with their start and end apart: 36 -> 36, of which waited for: 23 -> 21; matrix products, arithmetic and copies ran while one was open for 20% -> 21% of each run, Pallas kernels for 12% -> 12%
where the time goes in v4:
time: 514 us; the launch traced here: 505 us
  waiting for transfers between devices  171 us (33%)
  Pallas kernels  88.4 us (17%)
  starting transfers between devices  79.3 us (15%)
  other arithmetic  67.2 us (13%)
  matrix products  40.9 us (8%)
  local copies, waits for them, and re-layouts  30.5 us (6%)
  between operations  21.9 us (4%)
  loops' own time  6.36 us (1%)
    all_gather x3, waiting for transfers between devices, gather_rows(): return lax.all_gather(x, GROUP, axis=0, tiled=True)  39.6 us
    ppermute x9, waiting for transfers between devices, sum_rows_directly(): total = total + lax.ppermute(tile, 'y', pairs).astype(jnp.float32)  38.9 us
    ppermute x1, waiting for transfers between devices, last_sums(): cross_grads = lax.ppermute(grads_sent[1], 'y', CROSS)  30.5 us
    pallas_call x1, Pallas kernels, expert_rows(): pl.pallas_call(expert_kernel, out_shape=(jax.ShapeDtypeStruct(x.shape, bf...  25.4 us
    all_to_all x4, starting transfers between devices, to_owners(): lax.all_to_all(x.reshape(RANKS, x.shape[0] // RANKS, x.shape[1]), EXPERT,...  24.2 us
    dot_general x12, matrix products, matmul(): return jnp.dot(left, right, preferred_element_type=jnp.float32)  22.6 us
    all_to_all x4, waiting for transfers between devices, to_owners(): lax.all_to_all(x.reshape(RANKS, x.shape[0] // RANKS, x.shape[1]), EXPERT,...  22.4 us
    pallas_call x1, Pallas kernels, expert_weights(): pl.pallas_call(expert_weights_kernel, out_shape=(jax.ShapeDtypeStruct((sl...  21.6 us
  transfers between devices with their start and end apart: 36, of which 21 were waited for; matrix products, arithmetic and copies ran while one was open for 21% of the time, Pallas kernels for 12%

profile of v4, /device:TPU:1, one launch (start us, length us, event | category | flops | bytes accessed | tf_op | source)
XLA Modules:
  0.0 505.2 jit_solution(17762720529923669436)
XLA Ops:
  45.4 4.3 convolution_convert_fusion.1
  49.7 19.3 %collective-permute-done.8.refs_4_.refs_6_ = bf16[528,2048]{1,0:T(8,128)(2,1)} collective-permute-done((bf16[528,2048]{1,0:T(8,128)(2,1)}, bf16[528,2048]{1,0:T(8,128)(2,1)}, u32[]{:S(2)}, u32[]{:S(2)}) %collective-permute-start.8) | collective-permute-done | bytes 2162720 | tf_op jit(solution)/shard_map/ppermute | solution.py:588
  68.9 3.9 collective-permute-done.9.refs_5_.refs_7_
  84.0 6.0 %collective-permute-done.13 = bf16[64,2048]{1,0:T(8,128)(2,1)} collective-permute-done((bf16[64,2048]{1,0:T(8,128)(2,1)}, bf16[64,2048]{1,0:T(8,128)(2,1)}, u32[]{:S(2)}, u32[]{:S(2)}) %collective-permute-start.13) | collective-permute-done | bytes 262176 | tf_op jit(solution)/shard_map/ppermute | solution.py:77
  93.3 7.7 %all-to-all-start.4 = ((bf16[16,32,2048]{2,1,0:T(8,128)(2,1)}), bf16[16,32,2048]{2,1,0:T(8,128)(2,1)S(1)}, u32[]{:S(2)}, u32[]{:S(2)}) async-start(bf16[16,32,2048]{2,1,0:T(8,128)(2,1)} %bitcast.262), calls=%async_computation.4 | async-start | bytes 4194304 | tf_op jit(solution)/shard_map/all_to_all | solution.py:160
  101.0 21.1 %all-gather.6.cloned.1.call-done.rows_ref = bf16[512,2048]{1,0:T(8,128)(2,1)} async-done(((bf16[64,2048]{1,0:T(8,128)(2,1)}), bf16[512,2048]{1,0:T(8,128)(2,1)}) %all-gather.6.cloned.1.call-update) | async-done | bytes 2097168 | tf_op jit(solution)/shard_map/all_gather | solution.py:35
  128.3 5.3 %dispatch.1 = bf16[512,2176]{1,0:T(8,128)(2,1)} custom-call(bf16[512,512]{1,0:T(8,128)(2,1)} %get-tuple-element.260.map_ref, bf16[512,2048]{1,0:T(8,128)(2,1)} %all-gather.6.cloned.1.call-done.rows_ref, bf16[512,128]{1,0:T(8,128)(2,1)} %pad_maximum_fusion.9.tail_ref), custom_call_target="tpu_custom_call" | custom-call | flops 1140850688 | bytes 8388608 | tf_op jit(solution)/shard_map/dispatch/pallas_call | solution.py:204
  134.9 6.8 %all-to-all-start.5 = ((bf16[16,32,2176]{2,1,0:T(8,128)(2,1)}), bf16[16,32,2176]{2,1,0:T(8,128)(2,1)}, u32[]{:S(2)}, u32[]{:S(2)}) async-start(bf16[16,32,2176]{2,1,0:T(8,128)(2,1)} %bitcast.234), calls=%async_computation.5 | async-start | bytes 4456448 | tf_op jit(solution)/shard_map/all_to_all | solution.py:160
  143.2 15.6 %shared_experts.1 = (bf16[352,2048]{1,0:T(8,128)(2,1)}, bf16[352,2048]{1,0:T(8,128)(2,1)}, bf16[352,2048]{1,0:T(8,128)(2,1)}, bf16[512,352]{1,0:T(8,128)(2,1)}, ...) custom-call(s32[1]{0:T(128)} %bitcast.61.core, bf16[512,2048]{1,0:T(8,128)(2,1)} %all-gather.6.cloned.1.call-done.rows_ref, ...), custom_call_target="tpu_custom_call" | custom-call | flops 17999998976 | bytes 20971520 | tf_op jit(solution)/shard_map/shared_experts/pallas_call | solution.py:273
  158.8 13.4 %all-to-all-done.5 = bf16[16,32,2176]{2,1,0:T(8,128)(2,1)} async-done(((bf16[16,32,2176]{2,1,0:T(8,128)(2,1)}), bf16[16,32,2176]{2,1,0:T(8,128)(2,1)}, u32[]{:S(2)}, u32[]{:S(2)}) %all-to-all-start.5) | async-done | bytes 2228256 | tf_op jit(solution)/shard_map/all_to_all | solution.py:160
  179.5 25.4 %expert_rows.1 = (bf16[512,2176]{1,0:T(8,128)(2,1)}, bf16[512,1408]{1,0:T(8,128)(2,1)}, bf16[512,1408]{1,0:T(8,128)(2,1)}, bf16[512,1408]{1,0:T(8,128)(2,1)}) custom-call(s32[1]{0:T(128)} %bitcast.64.refs_0_, bf16[512,2176]{1,0:T(8,128)(2,1)} %bitcast.60.refs_1_.refs_0_, bf16[512,2048]{1,0:T(8,128)(2,1)} %bitcast.260, ...), custom_call_target="tpu_custom_call" | custom-call | flops 14763950080 | bytes 29360128 | tf_op jit(solution)/shard_map/expert_rows/pallas_call | solution.py:452
  205.0 5.2 %all-to-all-start.6 = ((bf16[16,32,2176]{2,1,0:T(8,128)(2,1)}), bf16[16,32,2176]{2,1,0:T(8,128)(2,1)S(1)}, u32[]{:S(2)}, u32[]{:S(2)}) async-start(bf16[16,32,2176]{2,1,0:T(8,128)(2,1)} %bitcast.254), calls=%async_computation.6 | async-start | bytes 4456448 | tf_op jit(solution)/shard_map/all_to_all | solution.py:160
  210.2 21.6 %expert_weights.1 = (bf16[512,2048]{1,0:T(8,128)(2,1)}, bf16[528,2048]{1,0:T(8,128)(2,1)}, bf16[528,2048]{1,0:T(8,128)(2,1)}, bf16[528,2048]{1,0:T(8,128)(2,1)},...) custom-call(bf16[512,2176]{1,0:T(8,128)(2,1)} %bitcast.60.refs_1_.refs_0_, bf16[512,2048]{1,0:T(8,128)(2,1)} %bitcast.261, ...), custom_call_target="tpu_custom_call" | custom-call | flops 99999997952 | bytes 35651584 | tf_op jit(solution)/shard_map/expert_weights/pallas_call | solution.py:529
  231.8 9.0 %all-to-all-done.6 = bf16[16,32,2176]{2,1,0:T(8,128)(2,1)S(1)} async-done(((bf16[16,32,2176]{2,1,0:T(8,128)(2,1)}), bf16[16,32,2176]{2,1,0:T(8,128)(2,1)S(1)}, u32[]{:S(2)}, u32[]{:S(2)}) %all-to-all-start.6) | async-done | bytes 2228256 | tf_op jit(solution)/shard_map/all_to_all | solution.py:160
  252.7 4.5 collective-permute-done.20
  258.6 5.6 %collective-permute-done.22 = bf16[64,2176]{1,0:T(8,128)(2,1)S(1)} collective-permute-done((bf16[64,2176]{1,0:T(8,128)(2,1)S(1)}, bf16[64,2176]{1,0:T(8,128)(2,1)S(1)}, u32[]{:S(2)}, u32[]{:S(2)}) %collective-permute-start.22) | collective-permute-done | bytes 278560 | tf_op jit(solution)/shard_map/ppermute | solution.py:77
  271.3 4.5 all-to-all-start.7
  275.8 16.6 %all-gather.8.cloned.1.call-done = bf16[512,2048]{1,0:T(8,128)(2,1)} async-done(((bf16[64,2048]{1,0:T(8,128)(2,1)}), bf16[512,2048]{1,0:T(8,128)(2,1)}) %all-gather.8.cloned.1.call-update) | async-done | bytes 2097168 | tf_op jit(solution)/shard_map/all_gather | solution.py:35
  305.9 8.2 %attention_rows.1 = (bf16[256,2048]{1,0:T(8,128)(2,1)}, bf16[256,2048]{1,0:T(8,128)(2,1)}, f32[1,2048]{1,0:T(1,128)}) custom-call(s32[1]{0:T(128)} %bitcast.61.core, bf16[512,384]{1,0:T(8,128)(2,1)} %copy.194.query_ref, bf16[512,576]{1,0:T(8,128)(2,1)} %pad_maximum_fusion.5.compressed_ref, bf16[512,2048]{1,0:T(8,128)(2,1)} %x_ref.1, ...), custom_call_target="tpu_custom_call" | custom-call | flops 99999997952 | bytes 10485760 | tf_op jit(solution)/shard_map/attention_rows/pallas_call | solution.py:367
  323.7 154.6 %conditional.1 = (f32[64,2048]{1,0:T(8,128)}, bf16[10240,128]{1,0:T(8,128)(2,1)S(1)}, bf16[64,2048]{1,0:T(8,128)(2,1)}, f32[2,176,2048]{2,1,0:T(8,128)}, f32[2,1...) conditional(s32[]{:T(128)} %bitcast.20, () %tuple.30, (s32[]{:T(128)}, f32[512,1]{0,1:T(1,128)}, ...), branch_computations={%region_12.13_spmd, %region_13.17_spmd} | conditional | flops 101846106112 | bytes 189091472 | solution.py:49
  328.1 4.9 add_convert_fusion.2
  349.5 3.9 add_convert_fusion
  359.3 6.5 %all-to-all-start.1 = ((bf16[16,80,128]{2,1,0:T(8,128)(2,1)}), bf16[16,80,128]{2,1,0:T(8,128)(2,1)S(1)}, u32[]{:S(2)}, u32[]{:S(2)}) async-start(bf16[16,80,128]{2,1,0:T(8,128)(2,1)} %maximum_bitcast_fusion), calls=%async_computation.1 | async-start | bytes 655360 | tf_op jit(solution)/shard_map/cond/branch_1_fun/all_to_all | solution.py:86
  377.5 6.7 %all-to-all-start.2 = ((bf16[16,80,128]{2,1,0:T(8,128)(2,1)}), bf16[16,80,128]{2,1,0:T(8,128)(2,1)S(1)}, u32[]{:S(2)}, u32[]{:S(2)}) async-start(bf16[16,80,128]{2,1,0:T(8,128)(2,1)} %broadcast_in_dim.14), calls=%async_computation.2 | async-start | bytes 655360 | tf_op jit(solution)/shard_map/cond/branch_1_fun/all_to_all | solution.py:88
  387.2 4.7 all-to-all-done.2
  393.2 4.3 all-to-all-start.3
  403.2 30.5 %collective-permute-done.5.cross = bf16[528,2048]{1,0:T(8,128)(2,1)} collective-permute-done((bf16[528,2048]{1,0:T(8,128)(2,1)}, bf16[528,2048]{1,0:T(8,128)(2,1)}, u32[]{:S(2)}, u32[]{:S(2)}) %collective-permute-start.5) | collective-permute-done | bytes 2162720 | tf_op jit(solution)/shard_map/cond/branch_1_fun/ppermute | solution.py:828
  433.7 9.4 %expert_outputs.1 = (f32[2,176,2048]{2,1,0:T(8,128)}, f32[2,176,2048]{2,1,0:T(8,128)}, f32[2,176,2048]{2,1,0:T(8,128)}) custom-call(s32[1]{0:T(128)} %bitcast.15.same, bf16[528,2048]{1,0:T(8,128)(2,1)} %get-tuple-element.72.own, bf16[2112,2048]{1,0:T(8,128)(2,1)} %get-tuple-element.76.taken_hbm, bf16[528,2048]{1,0:T(8,128)(2,1)} %collective-permute-done.4.pair, ...), custom_call_target="tpu_custom_call" | custom-call | bytes 20971520 | tf_op jit(solution)/shard_map/cond/branch_1_fun/expert_outputs/pallas_call | solution.py:303
  443.2 4.6 all-to-all-done.3
  450.7 6.3 %collective-permute-done.1 = bf16[64,4096]{1,0:T(8,128)(2,1)} collective-permute-done((bf16[64,4096]{1,0:T(8,128)(2,1)}, bf16[64,4096]{1,0:T(8,128)(2,1)}, u32[]{:S(2)}, u32[]{:S(2)}) %collective-permute-start.1) | collective-permute-done | bytes 524320 | tf_op jit(solution)/shard_map/cond/branch_1_fun/ppermute | solution.py:77
  457.1 13.4 %collective-permute-done.2 = bf16[64,4096]{1,0:T(8,128)(2,1)} collective-permute-done((bf16[64,4096]{1,0:T(8,128)(2,1)}, bf16[64,4096]{1,0:T(8,128)(2,1)}, u32[]{:S(2)}, u32[]{:S(2)}) %collective-permute-start.2) | collective-permute-done | bytes 524320 | tf_op jit(solution)/shard_map/cond/branch_1_fun/ppermute | solution.py:77
  479.1 4.4 copy.239
  (392 shorter events, 173.3 us)
Async XLA Ops:
  7.2 38.2 %all-gather.4.cloned.1.call-start = ((), (), s32[]{:S(2)}) async-start(), calls=%async_computation.8 | async-start | bytes 2359296 | tf_op jit(solution)/shard_map/all_gather | solution.py:35
  7.9 114.1 %all-gather.6.cloned.1.call-start = ((), (), s32[]{:S(2)}) async-start(), calls=%async_computation.9 | async-start | bytes 2359296 | tf_op jit(solution)/shard_map/all_gather | solution.py:35
  11.7 57.2 %collective-permute-start.8 = (bf16[528,2048]{1,0:T(8,128)(2,1)}, bf16[528,2048]{1,0:T(8,128)(2,1)}, u32[]{:S(2)}, u32[]{:S(2)}) collective-permute-start(bf16[528,2048]{1,0:T(8,128)(2,1)} %pad_maximum_fusion.2.refs_3_.refs_5_), channel_id=1, source_target_pairs={{0,2},{2,0},{4,6},{6,4},{1,3},{3,1},{5,7},{7,5},{8,10},{10,8},{12,... | collective-permute-start | bytes 6488072 | tf_op jit(solution)/shard_map/ppermute | solution.py:588
  15.3 57.5 %collective-permute-start.9 = (bf16[528,2048]{1,0:T(8,128)(2,1)}, bf16[528,2048]{1,0:T(8,128)(2,1)}, u32[]{:S(2)}, u32[]{:S(2)}) collective-permute-start(bf16[528,2048]{1,0:T(8,128)(2,1)} %pad_maximum_fusion.3), channel_id=1, source_target_pairs={{2,4},{4,2},{6,0},{0,6},{3,5},{5,3},{7,1},{1,7},{10,12},{12,10},{1... | collective-permute-start | bytes 6488072 | tf_op jit(solution)/shard_map/ppermute | solution.py:589
  32.5 40.4 %collective-permute-start.10 = (bf16[256,2048]{1,0:T(8,128)(2,1)}, bf16[256,2048]{1,0:T(8,128)(2,1)}, u32[]{:S(2)}, u32[]{:S(2)}) collective-permute-start(bf16[256,2048]{1,0:T(8,128)(2,1)} %bitcast.48), channel_id=1, source_target_pairs={{0,1},{1,0},{2,3},{3,2},{4,5},{5,4},{6,7},{7,6},{8,9},{9,8},{10,11... | collective-permute-start | bytes 3145736 | tf_op jit(solution)/shard_map/ppermute | solution.py:69
  78.4 11.6 %collective-permute-start.13 = (bf16[64,2048]{1,0:T(8,128)(2,1)}, bf16[64,2048]{1,0:T(8,128)(2,1)}, u32[]{:S(2)}, u32[]{:S(2)}) collective-permute-start(bf16[64,2048]{1,0:T(8,128)(2,1)} %get-tuple-element.235), channel_id=1, source_target_pairs={{0,4},{4,0},{2,6},{6,2},{1,5},{5,1},{3,7},{7,3},{8,12},{12,8},{10,... | collective-permute-start | bytes 786440 | tf_op jit(solution)/shard_map/ppermute | solution.py:77
  93.3 40.3 %all-to-all-start.4 = ((bf16[16,32,2048]{2,1,0:T(8,128)(2,1)}), bf16[16,32,2048]{2,1,0:T(8,128)(2,1)S(1)}, u32[]{:S(2)}, u32[]{:S(2)}) async-start(bf16[16,32,2048]{2,1,0:T(8,128)(2,1)} %bitcast.262), calls=%async_computation.4 | async-start | bytes 4194304 | tf_op jit(solution)/shard_map/all_to_all | solution.py:160
  122.1 50.2 %collective-permute-start.14 = (bf16[528,2048]{1,0:T(8,128)(2,1)}, bf16[528,2048]{1,0:T(8,128)(2,1)}, u32[]{:S(2)}, u32[]{:S(2)}) collective-permute-start(bf16[528,2048]{1,0:T(8,128)(2,1)} %pad_maximum_fusion.3), channel_id=1, source_target_pairs={{0,4},{4,0},{2,6},{6,2},{1,5},{5,1},{3,7},{7,3},{8,12},{12,8},{10,... | collective-permute-start | bytes 6488072 | tf_op jit(solution)/shard_map/ppermute | solution.py:666
  134.9 37.3 %all-to-all-start.5 = ((bf16[16,32,2176]{2,1,0:T(8,128)(2,1)}), bf16[16,32,2176]{2,1,0:T(8,128)(2,1)}, u32[]{:S(2)}, u32[]{:S(2)}) async-start(bf16[16,32,2176]{2,1,0:T(8,128)(2,1)} %bitcast.234), calls=%async_computation.5 | async-start | bytes 4456448 | tf_op jit(solution)/shard_map/all_to_all | solution.py:160
  141.7 34.3 %collective-permute-start.15 = (bf16[528,2048]{1,0:T(8,128)(2,1)}, bf16[528,2048]{1,0:T(8,128)(2,1)}, u32[]{:S(2)}, u32[]{:S(2)}) collective-permute-start(bf16[528,2048]{1,0:T(8,128)(2,1)} %pad_maximum_fusion.2.refs_3_.refs_5_), channel_id=1, source_target_pairs={{0,1},{1,0},{2,3},{3,2},{4,5},{5,4},{6,7},{7,6},{8,9},{9,8},{10,11... | collective-permute-start | bytes 6488072 | tf_op jit(solution)/shard_map/ppermute | solution.py:691
  142.6 33.4 %collective-permute-start.16 = (bf16[528,2048]{1,0:T(8,128)(2,1)}, bf16[528,2048]{1,0:T(8,128)(2,1)}, u32[]{:S(2)}, u32[]{:S(2)}) collective-permute-start(bf16[528,2048]{1,0:T(8,128)(2,1)} %collective-permute-done.8.refs_4_.refs_6_), channel_id=1, source_target_pairs={{0,1},{1,0},{2,3},{3,2},{4,5},{5,4},{6,7},{7,6},{8,9},{9,8},{10,11... | collective-permute-start | bytes 6488072 | tf_op jit(solution)/shard_map/ppermute | solution.py:691
  142.7 33.3 %collective-permute-start.17 = (bf16[528,2048]{1,0:T(8,128)(2,1)}, bf16[528,2048]{1,0:T(8,128)(2,1)}, u32[]{:S(2)}, u32[]{:S(2)}) collective-permute-start(bf16[528,2048]{1,0:T(8,128)(2,1)} %collective-permute-done.9.refs_5_.refs_7_), channel_id=1, source_target_pairs={{0,1},{1,0},{2,3},{3,2},{4,5},{5,4},{6,7},{7,6},{8,9},{9,8},{10,11... | collective-permute-start | bytes 6488072 | tf_op jit(solution)/shard_map/ppermute | solution.py:691
  205.0 35.8 %all-to-all-start.6 = ((bf16[16,32,2176]{2,1,0:T(8,128)(2,1)}), bf16[16,32,2176]{2,1,0:T(8,128)(2,1)S(1)}, u32[]{:S(2)}, u32[]{:S(2)}) async-start(bf16[16,32,2176]{2,1,0:T(8,128)(2,1)} %bitcast.254), calls=%async_computation.6 | async-start | bytes 4456448 | tf_op jit(solution)/shard_map/all_to_all | solution.py:160
  210.2 82.2 %all-gather.8.cloned.1.call-start = ((), (), s32[]{:S(2)}) async-start(), calls=%async_computation.10 | async-start | bytes 2359296 | tf_op jit(solution)/shard_map/all_gather | solution.py:35
  249.2 8.0 %collective-permute-start.20 = (bf16[64,2176]{1,0:T(8,128)(2,1)S(1)}, bf16[64,2176]{1,0:T(8,128)(2,1)S(1)}, u32[]{:S(2)}, u32[]{:S(2)}) collective-permute-start(bf16[64,2176]{1,0:T(8,128)(2,1)S(1)} %get-tuple-element.231), channel_id=1, source_target_pairs={{0,2},{2,0},{4,6},{6,4},{1,3},{3,1},{5,7},{7,5},{8,10},{10,8},{12,... | collective-permute-start | bytes 835592 | tf_op jit(solution)/shard_map/ppermute | solution.py:77
  249.3 9.2 %collective-permute-start.21 = (bf16[64,2176]{1,0:T(8,128)(2,1)S(1)}, bf16[64,2176]{1,0:T(8,128)(2,1)S(1)}, u32[]{:S(2)}, u32[]{:S(2)}) collective-permute-start(bf16[64,2176]{1,0:T(8,128)(2,1)S(1)} %get-tuple-element.233), channel_id=1, source_target_pairs={{2,4},{4,2},{6,0},{0,6},{3,5},{5,3},{7,1},{1,7},{10,12},{12,10},{1... | collective-permute-start | bytes 835592 | tf_op jit(solution)/shard_map/ppermute | solution.py:77
  251.4 12.8 %collective-permute-start.22 = (bf16[64,2176]{1,0:T(8,128)(2,1)S(1)}, bf16[64,2176]{1,0:T(8,128)(2,1)S(1)}, u32[]{:S(2)}, u32[]{:S(2)}) collective-permute-start(bf16[64,2176]{1,0:T(8,128)(2,1)S(1)} %get-tuple-element.232), channel_id=1, source_target_pairs={{0,4},{4,0},{2,6},{6,2},{1,5},{5,1},{3,7},{7,3},{8,12},{12,8},{10,... | collective-permute-start | bytes 835592 | tf_op jit(solution)/shard_map/ppermute | solution.py:77
  268.7 55.0 %collective-permute-start.23 = (bf16[2112,2048]{1,0:T(8,128)(2,1)}, bf16[2112,2048]{1,0:T(8,128)(2,1)}, u32[]{:S(2)}, u32[]{:S(2)}) collective-permute-start(bf16[2112,2048]{1,0:T(8,128)(2,1)} %get-tuple-element.150), channel_id=1, source_target_pairs={{0,1},{1,0},{2,3},{3,2},{4,5},{5,4},{6,7},{7,6},{8,9},{9,8},{10,11... | collective-permute-start | bytes 25952264 | tf_op jit(solution)/shard_map/ppermute | solution.py:701
  271.3 50.4 %all-to-all-start.7 = ((bf16[16,32,2048]{2,1,0:T(8,128)(2,1)}), bf16[16,32,2048]{2,1,0:T(8,128)(2,1)}, u32[]{:S(2)}, u32[]{:S(2)}) async-start(bf16[16,32,2048]{2,1,0:T(8,128)(2,1)} %bitcast.259), calls=%async_computation.7 | async-start | bytes 4194304 | tf_op jit(solution)/shard_map/all_to_all | solution.py:160
  275.7 210.7 %all-reduce.6.cloned.1.call-start = ((), (), s32[]{:S(2)}) async-start(), calls=%async_computation.11 | async-start | bytes 14942208 | tf_op jit(solution)/shard_map/psum | solution.py:784
  324.4 29.0 %all-to-all-start = ((bf16[8,96,512]{2,1,0:T(8,128)(2,1)}), bf16[8,96,512]{2,1,0:T(8,128)(2,1)S(1)}, u32[]{:S(2)}, u32[]{:S(2)}) async-start(bf16[8,96,512]{2,1,0:T(8,128)(2,1)} %get-tuple-element.66), calls=%async_computation | async-start | bytes 1572864 | tf_op jit(solution)/shard_map/cond/branch_1_fun/all_to_all | solution.py:825
  333.0 58.9 %collective-permute-start.4 = (bf16[528,2048]{1,0:T(8,128)(2,1)}, bf16[528,2048]{1,0:T(8,128)(2,1)}, u32[]{:S(2)}, u32[]{:S(2)}) collective-permute-start(bf16[528,2048]{1,0:T(8,128)(2,1)} %add_convert_fusion.2), channel_id=1, source_target_pairs={{0,2},{2,0},{4,6},{6,4},{1,3},{3,1},{5,7},{7,5},{8,10},{10,8},{12,... | collective-permute-start | bytes 6488072 | tf_op jit(solution)/shard_map/cond/branch_1_fun/ppermute | solution.py:827
  338.2 95.5 %collective-permute-start.5 = (bf16[528,2048]{1,0:T(8,128)(2,1)}, bf16[528,2048]{1,0:T(8,128)(2,1)}, u32[]{:S(2)}, u32[]{:S(2)}) collective-permute-start(bf16[528,2048]{1,0:T(8,128)(2,1)} %add_convert_fusion.1), channel_id=1, source_target_pairs={{2,4},{4,2},{6,0},{0,6},{3,5},{5,3},{7,1},{1,7},{10,12},{12,10},{1... | collective-permute-start | bytes 6488072 | tf_op jit(solution)/shard_map/cond/branch_1_fun/ppermute | solution.py:828
  345.9 38.3 %collective-permute-start = (bf16[256,4096]{1,0:T(8,128)(2,1)}, bf16[256,4096]{1,0:T(8,128)(2,1)}, u32[]{:S(2)}, u32[]{:S(2)}) collective-permute-start(bf16[256,4096]{1,0:T(8,128)(2,1)} %pad_maximum_fusion.1), channel_id=1, source_target_pairs={{0,1},{1,0},{2,3},{3,2},{4,5},{5,4},{6,7},{7,6},{8,9},{9,8},{10,11... | collective-permute-start | bytes 6291464 | tf_op jit(solution)/shard_map/cond/branch_1_fun/ppermute | solution.py:69
  354.2 79.6 %collective-permute-start.6 = (bf16[528,2048]{1,0:T(8,128)(2,1)}, bf16[528,2048]{1,0:T(8,128)(2,1)}, u32[]{:S(2)}, u32[]{:S(2)}) collective-permute-start(bf16[528,2048]{1,0:T(8,128)(2,1)} %add_convert_fusion), channel_id=1, source_target_pairs={{0,4},{4,0},{2,6},{6,2},{1,5},{5,1},{3,7},{7,3},{8,12},{12,8},{10,... | collective-permute-start | bytes 6488072 | tf_op jit(solution)/shard_map/cond/branch_1_fun/ppermute | solution.py:844
  359.3 17.4 %all-to-all-start.1 = ((bf16[16,80,128]{2,1,0:T(8,128)(2,1)}), bf16[16,80,128]{2,1,0:T(8,128)(2,1)S(1)}, u32[]{:S(2)}, u32[]{:S(2)}) async-start(bf16[16,80,128]{2,1,0:T(8,128)(2,1)} %maximum_bitcast_fusion), calls=%async_computation.1 | async-start | bytes 655360 | tf_op jit(solution)/shard_map/cond/branch_1_fun/all_to_all | solution.py:86
  377.5 14.5 %all-to-all-start.2 = ((bf16[16,80,128]{2,1,0:T(8,128)(2,1)}), bf16[16,80,128]{2,1,0:T(8,128)(2,1)S(1)}, u32[]{:S(2)}, u32[]{:S(2)}) async-start(bf16[16,80,128]{2,1,0:T(8,128)(2,1)} %broadcast_in_dim.14), calls=%async_computation.2 | async-start | bytes 655360 | tf_op jit(solution)/shard_map/cond/branch_1_fun/all_to_all | solution.py:88
  393.2 54.5 %all-to-all-start.3 = ((bf16[4,1280,128]{2,1,0:T(8,128)(2,1)}), bf16[4,1280,128]{2,1,0:T(8,128)(2,1)}, u32[]{:S(2)}, u32[]{:S(2)}) async-start(bf16[4,1280,128]{2,1,0:T(8,128)(2,1)} %broadcast_in_dim.16), calls=%async_computation.3 | async-start | bytes 2621440 | tf_op jit(solution)/shard_map/cond/branch_1_fun/all_to_all | solution.py:40
  398.6 58.4 %collective-permute-start.1 = (bf16[64,4096]{1,0:T(8,128)(2,1)}, bf16[64,4096]{1,0:T(8,128)(2,1)}, u32[]{:S(2)}, u32[]{:S(2)}) collective-permute-start(bf16[64,4096]{1,0:T(8,128)(2,1)} %get-tuple-element.212), channel_id=1, source_target_pairs={{0,2},{2,0},{4,6},{6,4},{1,3},{3,1},{5,7},{7,5},{8,10},{10,8},{12,... | collective-permute-start | bytes 1572872 | tf_op jit(solution)/shard_map/cond/branch_1_fun/ppermute | solution.py:77
  400.0 70.5 %collective-permute-start.2 = (bf16[64,4096]{1,0:T(8,128)(2,1)}, bf16[64,4096]{1,0:T(8,128)(2,1)}, u32[]{:S(2)}, u32[]{:S(2)}) collective-permute-start(bf16[64,4096]{1,0:T(8,128)(2,1)} %get-tuple-element.214), channel_id=1, source_target_pairs={{2,4},{4,2},{6,0},{0,6},{3,5},{5,3},{7,1},{1,7},{10,12},{12,10},{1... | collective-permute-start | bytes 1572872 | tf_op jit(solution)/shard_map/cond/branch_1_fun/ppermute | solution.py:77
  401.8 68.7 %collective-permute-start.3 = (bf16[64,4096]{1,0:T(8,128)(2,1)S(1)}, bf16[64,4096]{1,0:T(8,128)(2,1)}, u32[]{:S(2)}, u32[]{:S(2)}) collective-permute-start(bf16[64,4096]{1,0:T(8,128)(2,1)S(1)} %get-tuple-element.213), channel_id=1, source_target_pairs={{0,4},{4,0},{2,6},{6,2},{1,5},{5,1},{3,7},{7,3},{8,12},{12,8},{10,... | collective-permute-start | bytes 1572872 | tf_op jit(solution)/shard_map/cond/branch_1_fun/ppermute | solution.py:77
  447.7 28.4 %collective-permute-start.7 = (bf16[4,1280,128]{2,1,0:T(8,128)(2,1)}, bf16[4,1280,128]{2,1,0:T(8,128)(2,1)S(1)}, u32[]{:S(2)}, u32[]{:S(2)}) collective-permute-start(bf16[4,1280,128]{2,1,0:T(8,128)(2,1)} %all-to-all-done.3), channel_id=1, source_target_pairs={{0,1},{1,0},{2,3},{3,2},{4,5},{5,4},{6,7},{7,6},{8,9},{9,8},{10,11... | collective-permute-start | bytes 3932168 | tf_op jit(solution)/shard_map/cond/branch_1_fun/ppermute | solution.py:42
  (103 other events, 529.8 us)
Sparse Core Ops, SparseCore 0:
  9.8 35.5 all-gather.3
  93.4 28.6 all-gather.5
  267.9 24.4 all-gather.7
  321.9 134.2 all-reduce.5
